TPU v7x, 32 devices: a whole 2x2x4 slice. The times are simulated.
32 devices in a mesh: ep: 8 (over z, x), hp: 4 (over y, core).
Axes of the slice: x: 2, y: 2, z: 4, core: 2. Of those that a mesh axis runs over, the one named last changes fastest.
Arguments:
- tokens: bfloat16 [8192, 1280], P(('ep', 'hp')), may hold values from -6 to 6
- attn_gain: bfloat16 [1280], P('hp'), may hold values from 0.5 to 1.5
- query_weight: bfloat16 [1280, 1280], P('hp'), may hold values from -0.15625 to 0.15625
- key_weight: bfloat16 [1280, 1280], P('hp'), may hold values from -0.15625 to 0.15625
- value_weight: bfloat16 [1280, 1280], P('hp'), may hold values from -0.15625 to 0.15625
- out_weight: bfloat16 [1280, 1280], P('hp'), may hold values from -2.5 to 2.5
- ffn_gain: bfloat16 [1280], P('hp'), may hold values from 0.5 to 1.5
- router_weight: bfloat16 [1280, 16], P('hp'), may hold values from -0.078125 to 0.078125
- shared_gate: bfloat16 [1280, 896], P('hp'), may hold values from -0.15625 to 0.15625
- shared_up: bfloat16 [1280, 896], P('hp'), may hold values from -0.15625 to 0.15625
- shared_down: bfloat16 [896, 1280], P('hp'), may hold values from -0.1875 to 0.1875
- expert_gate: bfloat16 [16, 1280, 896], P('ep', None, 'hp'), may hold values from -0.15625 to 0.15625
- expert_up: bfloat16 [16, 1280, 896], P('ep', None, 'hp'), may hold values from -0.15625 to 0.15625
- expert_down: bfloat16 [16, 896, 1280], P('ep', 'hp'), may hold values from -0.75 to 0.75
- routes: int32 [8192, 7], P(('ep', 'hp')), may hold values from 0 to 15, all different within a row; in each aligned block of 256 rows (0 to 255, 256 to 511, ...) at most 140 rows name the same one
- keep_mask: int32 [8192, 7], P(('ep', 'hp')), may hold values 0 or 1
- cotangent: bfloat16 [8192, 1280], P(('ep', 'hp')), may hold values from -6 to 6
Outputs:
- layer_out: bfloat16 [8192, 1280], P(('ep', 'hp'))
- tokens_grad: float32 [8192, 1280], P(('ep', 'hp'))
- attn_gain_grad: float32 [1280], P('hp')
- query_grad: float32 [1280, 1280], P('hp')
- key_grad: float32 [1280, 1280], P('hp')
- value_grad: float32 [1280, 1280], P('hp')
- out_grad: float32 [1280, 1280], P('hp')
- ffn_gain_grad: float32 [1280], P('hp')
- router_grad: float32 [1280, 16], P('hp')
- shared_gate_grad: float32 [1280, 896], P('hp')
- shared_up_grad: float32 [1280, 896], P('hp')
- shared_down_grad: float32 [896, 1280], P('hp')
- expert_gate_grad: float32 [16, 1280, 896], P('ep', None, 'hp')
- expert_up_grad: float32 [16, 1280, 896], P('ep', None, 'hp')
- expert_down_grad: float32 [16, 896, 1280], P('ep', 'hp')
- expert_counts: int32 [16], P('hp')
Inputs may be any that keep to these rules, and one draw needn't show every extreme that they name: `routes`: each row names 7 different experts. Within each device's 256 rows no expert is named more than 140 times, and in some device's rows one expert is named exactly 140 times.
All inputs are finite; a program needn't handle non-finite values. No bound on the sum of `keep_mask` on one device may be relied on, other than what follows from the above.
Results may differ from a plain program's by a relative error of at most 0.024.
Values may be sent and summed in bfloat16 or wider, within the bound.
A program may use at most 384 MiB of HBM per device.

v0:
```python
import jax
import jax.numpy as jnp
from jax import lax
from jax.sharding import PartitionSpec as P

H = 10
HD = 128


epsilon = 1e-06


def norm_rows(values, gain_vec):
    inv_rms = lax.rsqrt(jnp.mean(values * values, axis=-1, keepdims=True) + epsilon)
    return (inv_rms, values * inv_rms * gain_vec)


def norm_back(values, inv_rms, gain_vec, upstream):
    weighted = upstream * gain_vec
    inner_mean = jnp.mean(weighted * values, axis=-1, keepdims=True)
    to_input = weighted * inv_rms - values * inv_rms * inv_rms * inv_rms * inner_mean
    to_gain = jnp.sum(upstream * values * inv_rms, axis=0)
    return (to_input, to_gain)


def half_turn(values):
    middle_at = values.shape[-1] // 2
    return jnp.concatenate([-values[..., middle_at:], values[..., :middle_at]], axis=-1)


def rotary_tables(positions, head_size):
    exponent = jnp.arange(head_size // 2, dtype=jnp.float32) * (2.0 / head_size)
    theta = positions.astype(jnp.float32)[:, None] * jnp.power(10000.0, -exponent)[None, :]
    theta = jnp.concatenate([theta, theta], axis=-1)
    return (jnp.cos(theta)[:, None, :], jnp.sin(theta)[:, None, :])


def rotate(values, cosine, sine):
    return values * cosine + half_turn(values) * sine


def rotate_back(values, cosine, sine):
    return values * cosine - half_turn(values * sine)


def silu_slope(values):
    sigmoid_v = jax.nn.sigmoid(values)
    return sigmoid_v * (1.0 + values * (1.0 - sigmoid_v))


def project(left, right):
    return jnp.dot(left, right, preferred_element_type=jnp.float32)


def per_device(
    tokens,
    attn_gain,
    query_weight,
    key_weight,
    value_weight,
    out_weight,
    ffn_gain,
    router_weight,
    shared_gate,
    shared_up,
    shared_down,
    expert_gate,
    expert_up,
    expert_down,
    routes,
    keep_mask,
    cotangent,
):
    (
        query_full,
        key_full,
        value_full,
        out_full,
        sgate_full,
        sup_full,
        sdown_full,
        router_full,
        gain_first,
        gain_second,
    ) = (
        lax.all_gather(query_weight, "hp", axis=0, tiled=True),
        lax.all_gather(key_weight, "hp", axis=0, tiled=True),
        lax.all_gather(value_weight, "hp", axis=0, tiled=True),
        lax.all_gather(out_weight, "hp", axis=0, tiled=True),
        lax.all_gather(shared_gate, "hp", axis=0, tiled=True),
        lax.all_gather(shared_up, "hp", axis=0, tiled=True),
        lax.all_gather(shared_down, "hp", axis=0, tiled=True),
        lax.all_gather(router_weight, "hp", axis=0, tiled=True),
        lax.all_gather(attn_gain, "hp", axis=0, tiled=True),
        lax.all_gather(ffn_gain, "hp", axis=0, tiled=True),
    )
    tok_rows = tokens.shape[0]
    model_width = tokens.shape[1]
    heads_width = H * HD
    hp_count = lax.axis_size("hp")
    ep_count = lax.axis_size("ep")
    seq_len = tok_rows * hp_count
    top_count = routes.shape[1]
    expert_total = router_full.shape[1]
    owned_count = expert_gate.shape[0]
    capacity = 5 * tok_rows * top_count // (4 * expert_total)
    score_scale = HD ** (-0.5)
    positions = lax.axis_index("hp") * tok_rows + jnp.arange(tok_rows, dtype=jnp.int32)
    cosine, sine = rotary_tables(positions, HD)
    residual = tokens.astype(jnp.float32)
    gain_one = gain_first.astype(jnp.float32)
    inv_one, normed = norm_rows(residual, gain_one)
    first_in = normed.astype(jnp.bfloat16)
    query = rotate(project(first_in, query_full).reshape(tok_rows, H, HD), cosine, sine).astype(
        jnp.bfloat16
    )
    key_own = (
        rotate(project(first_in, key_full).reshape(tok_rows, H, HD), cosine, sine)
        .astype(jnp.bfloat16)
        .reshape(tok_rows, heads_width)
    )
    value_own = project(first_in, value_full).astype(jnp.bfloat16)
    key_all, value_all = (
        lax.all_gather(key_own, "hp", axis=0, tiled=True),
        lax.all_gather(value_own, "hp", axis=0, tiled=True),
    )
    key_all = key_all.reshape(seq_len, H, HD)
    value_all = value_all.reshape(seq_len, H, HD)
    allowed = (jnp.arange(seq_len, dtype=jnp.int32)[None, :] <= positions[:, None])[None]
    scores = jnp.where(
        allowed,
        jnp.einsum("qhd,khd->hqk", query, key_all, preferred_element_type=jnp.float32)
        * score_scale,
        -1e30,
    )
    row_max = jnp.max(scores, axis=-1, keepdims=True)
    shifted = jnp.exp(scores - row_max)
    row_total = jnp.sum(shifted, axis=-1, keepdims=True)
    log_total = row_max + jnp.log(row_total)
    attention = (shifted / row_total).astype(jnp.bfloat16)
    mixed = (
        jnp.einsum("hqk,khd->qhd", attention, value_all, preferred_element_type=jnp.float32)
        .reshape(tok_rows, heads_width)
        .astype(jnp.bfloat16)
    )
    middle = residual + project(mixed, out_full)
    gain_two = gain_second.astype(jnp.float32)
    inv_two, normed = norm_rows(middle, gain_two)
    second_in = normed.astype(jnp.bfloat16)
    logits = project(second_in, router_full)
    route_hit = routes[:, :, None] == jnp.arange(expert_total, dtype=jnp.int32)[None, None, :]
    chosen = jnp.sum(jnp.where(route_hit, logits[:, None, :], 0.0), axis=-1)
    gates = jax.nn.softmax(chosen, axis=-1)
    kept = keep_mask.astype(jnp.float32)
    pair_weight = gates * kept
    shared_pre = project(second_in, sgate_full)
    shared_lin = project(second_in, sup_full)
    shared_act = (jax.nn.silu(shared_pre) * shared_lin).astype(jnp.bfloat16)
    shared_res = project(shared_act, sdown_full)
    flat_routes = routes.reshape(-1)
    onehot = route_hit.reshape(-1, expert_total).astype(jnp.int32)
    slots = jnp.sum((jnp.cumsum(onehot, axis=0) - onehot) * onehot, axis=1)
    target = flat_routes * capacity + slots
    source = jnp.arange(flat_routes.shape[0], dtype=jnp.int32) // top_count
    counts_here = jnp.sum(onehot * keep_mask.reshape(-1)[:, None], axis=0).astype(jnp.float32)
    outgoing = (
        jnp.zeros((expert_total * capacity, model_width), jnp.bfloat16)
        .at[target]
        .set(second_in[source])
    )
    outgoing = outgoing.reshape(ep_count, owned_count, capacity, model_width)
    incoming = lax.all_to_all(outgoing, "ep", split_axis=0, concat_axis=0, tiled=True)
    rows_in = lax.all_gather(incoming, "hp", axis=0, tiled=True)
    gate_use, up_use, down_use = (expert_gate, expert_up, expert_down)
    hidden_gate = jnp.einsum(
        "sxcd,xdf->sxcf", rows_in, gate_use, preferred_element_type=jnp.float32
    )
    hidden_up = jnp.einsum("sxcd,xdf->sxcf", rows_in, up_use, preferred_element_type=jnp.float32)
    hidden_act = (jax.nn.silu(hidden_gate) * hidden_up).astype(jnp.bfloat16)
    expert_res = jnp.einsum(
        "sxcf,xfd->sxcd", hidden_act, down_use, preferred_element_type=jnp.float32
    )
    expert_res = lax.psum_scatter(
        expert_res.astype(jnp.bfloat16), "hp", scatter_dimension=0, tiled=True
    ).astype(jnp.float32)
    returned = lax.all_to_all(
        expert_res.astype(jnp.bfloat16), "ep", split_axis=0, concat_axis=0, tiled=True
    ).reshape(expert_total * capacity, model_width)
    pair_out = returned[target].reshape(tok_rows, top_count, model_width).astype(jnp.float32)
    layer = middle + shared_res + jnp.sum(pair_out * pair_weight[:, :, None], axis=1)
    grad_out = cotangent.astype(jnp.float32)
    pair_back = (
        (pair_weight[:, :, None] * grad_out[:, None, :])
        .astype(jnp.bfloat16)
        .reshape(-1, model_width)
    )
    weight_back = jnp.sum(pair_out * grad_out[:, None, :], axis=-1)
    gate_back = weight_back * kept
    chosen_back = gates * (gate_back - jnp.sum(gates * gate_back, axis=-1, keepdims=True))
    logits_back = jnp.sum(jnp.where(route_hit, chosen_back[:, :, None], 0.0), axis=1).astype(
        jnp.bfloat16
    )
    router_part = jnp.einsum(
        "td,te->de", second_in, logits_back, preferred_element_type=jnp.float32
    )
    outgoing_back = (
        jnp.zeros((expert_total * capacity, model_width), jnp.bfloat16).at[target].set(pair_back)
    )
    outgoing_back = outgoing_back.reshape(ep_count, owned_count, capacity, model_width)
    incoming_back = lax.all_to_all(outgoing_back, "ep", split_axis=0, concat_axis=0, tiled=True)
    rows_back = lax.all_gather(incoming_back, "hp", axis=0, tiled=True)
    act_back = jnp.einsum("sxcd,xfd->sxcf", rows_back, down_use, preferred_element_type=jnp.float32)
    gate_in_back = (act_back * hidden_up * silu_slope(hidden_gate)).astype(jnp.bfloat16)
    up_in_back = (act_back * jax.nn.silu(hidden_gate)).astype(jnp.bfloat16)
    down_part = jnp.einsum(
        "sxcf,sxcd->xfd", hidden_act, rows_back, preferred_element_type=jnp.float32
    )
    gate_part = jnp.einsum(
        "sxcd,sxcf->xdf", rows_in, gate_in_back, preferred_element_type=jnp.float32
    )
    up_part = jnp.einsum("sxcd,sxcf->xdf", rows_in, up_in_back, preferred_element_type=jnp.float32)
    rows_in_back = jnp.einsum(
        "sxcf,xdf->sxcd", gate_in_back, gate_use, preferred_element_type=jnp.float32
    )
    rows_in_back = rows_in_back + jnp.einsum(
        "sxcf,xdf->sxcd", up_in_back, up_use, preferred_element_type=jnp.float32
    )
    rows_in_back = lax.psum_scatter(
        rows_in_back.astype(jnp.bfloat16), "hp", scatter_dimension=0, tiled=True
    ).astype(jnp.float32)
    gate_final, up_final, down_final = (gate_part, up_part, down_part)
    back_rows = lax.all_to_all(
        rows_in_back.astype(jnp.bfloat16), "ep", split_axis=0, concat_axis=0, tiled=True
    ).reshape(expert_total * capacity, model_width)
    expert_in_back = jnp.sum(
        back_rows[target].reshape(tok_rows, top_count, model_width).astype(jnp.float32), axis=1
    )
    shared_back = jnp.einsum("td,fd->tf", cotangent, sdown_full, preferred_element_type=jnp.float32)
    sdown_part = jnp.einsum("tf,td->fd", shared_act, cotangent, preferred_element_type=jnp.float32)
    sgate_back = (shared_back * shared_lin * silu_slope(shared_pre)).astype(jnp.bfloat16)
    sup_back = (shared_back * jax.nn.silu(shared_pre)).astype(jnp.bfloat16)
    sgate_part = jnp.einsum("td,tf->df", second_in, sgate_back, preferred_element_type=jnp.float32)
    sup_part = jnp.einsum("td,tf->df", second_in, sup_back, preferred_element_type=jnp.float32)
    second_back = jnp.einsum(
        "tf,df->td", sgate_back, sgate_full, preferred_element_type=jnp.float32
    )
    second_back = second_back + jnp.einsum(
        "tf,df->td", sup_back, sup_full, preferred_element_type=jnp.float32
    )
    second_back = second_back + jnp.einsum(
        "te,de->td", logits_back, router_full, preferred_element_type=jnp.float32
    )
    second_back = second_back + expert_in_back
    middle_norm_back, gain_two_part = norm_back(middle, inv_two, gain_two, second_back)
    middle_back = grad_out + middle_norm_back
    attn_back = middle_back.astype(jnp.bfloat16)
    out_part = jnp.einsum("ta,td->ad", mixed, attn_back, preferred_element_type=jnp.float32)
    mixed_back = (
        jnp.einsum("td,ad->ta", attn_back, out_full, preferred_element_type=jnp.float32)
        .astype(jnp.bfloat16)
        .reshape(tok_rows, H, HD)
    )
    scores_again = jnp.where(
        allowed,
        jnp.einsum("qhd,khd->hqk", query, key_all, preferred_element_type=jnp.float32)
        * score_scale,
        -1e30,
    )
    soft_again = jnp.exp(scores_again - log_total)
    probs_back = jnp.einsum(
        "qhd,khd->hqk", mixed_back, value_all, preferred_element_type=jnp.float32
    )
    inner_sum = jnp.sum(soft_again * probs_back, axis=-1, keepdims=True)
    score_back = (soft_again * (probs_back - inner_sum) * score_scale).astype(jnp.bfloat16)
    query_back = jnp.einsum("hqk,khd->qhd", score_back, key_all, preferred_element_type=jnp.float32)
    key_part = jnp.einsum(
        "hqk,qhd->khd", score_back, query, preferred_element_type=jnp.float32
    ).reshape(seq_len, heads_width)
    value_part = jnp.einsum(
        "hqk,qhd->khd",
        soft_again.astype(jnp.bfloat16),
        mixed_back,
        preferred_element_type=jnp.float32,
    ).reshape(seq_len, heads_width)
    key_back, value_back = (
        lax.psum_scatter(
            key_part.astype(jnp.bfloat16), "hp", scatter_dimension=0, tiled=True
        ).astype(jnp.float32),
        lax.psum_scatter(
            value_part.astype(jnp.bfloat16), "hp", scatter_dimension=0, tiled=True
        ).astype(jnp.float32),
    )
    query_raw_back = (
        rotate_back(query_back, cosine, sine).reshape(tok_rows, heads_width).astype(jnp.bfloat16)
    )
    key_raw_back = (
        rotate_back(key_back.reshape(tok_rows, H, HD), cosine, sine)
        .reshape(tok_rows, heads_width)
        .astype(jnp.bfloat16)
    )
    value_raw_back = value_back.astype(jnp.bfloat16)
    query_part = jnp.einsum(
        "td,ta->da", first_in, query_raw_back, preferred_element_type=jnp.float32
    )
    key_wpart = jnp.einsum("td,ta->da", first_in, key_raw_back, preferred_element_type=jnp.float32)
    value_wpart = jnp.einsum(
        "td,ta->da", first_in, value_raw_back, preferred_element_type=jnp.float32
    )
    first_back = jnp.einsum(
        "ta,da->td", query_raw_back, query_full, preferred_element_type=jnp.float32
    )
    first_back = first_back + jnp.einsum(
        "ta,da->td", key_raw_back, key_full, preferred_element_type=jnp.float32
    )
    first_back = first_back + jnp.einsum(
        "ta,da->td", value_raw_back, value_full, preferred_element_type=jnp.float32
    )
    input_norm_back, gain_one_part = norm_back(residual, inv_one, gain_one, first_back)
    tokens_back = middle_back + input_norm_back
    shares = (
        lax.psum_scatter(
            query_part.astype(jnp.bfloat16), "hp", scatter_dimension=0, tiled=True
        ).astype(jnp.float32),
        lax.psum_scatter(
            key_wpart.astype(jnp.bfloat16), "hp", scatter_dimension=0, tiled=True
        ).astype(jnp.float32),
        lax.psum_scatter(
            value_wpart.astype(jnp.bfloat16), "hp", scatter_dimension=0, tiled=True
        ).astype(jnp.float32),
        lax.psum_scatter(
            out_part.astype(jnp.bfloat16), "hp", scatter_dimension=0, tiled=True
        ).astype(jnp.float32),
        lax.psum_scatter(
            sgate_part.astype(jnp.bfloat16), "hp", scatter_dimension=0, tiled=True
        ).astype(jnp.float32),
        lax.psum_scatter(
            sup_part.astype(jnp.bfloat16), "hp", scatter_dimension=0, tiled=True
        ).astype(jnp.float32),
        lax.psum_scatter(
            sdown_part.astype(jnp.bfloat16), "hp", scatter_dimension=0, tiled=True
        ).astype(jnp.float32),
        lax.psum_scatter(
            router_part.astype(jnp.bfloat16), "hp", scatter_dimension=0, tiled=True
        ).astype(jnp.float32),
        lax.psum_scatter(
            gain_one_part.astype(jnp.bfloat16), "hp", scatter_dimension=0, tiled=True
        ).astype(jnp.float32),
        lax.psum_scatter(
            gain_two_part.astype(jnp.bfloat16), "hp", scatter_dimension=0, tiled=True
        ).astype(jnp.float32),
        lax.psum_scatter(
            counts_here.astype(jnp.bfloat16), "hp", scatter_dimension=0, tiled=True
        ).astype(jnp.float32),
    )
    summed = (
        lax.psum(shares[0].astype(jnp.bfloat16), "ep").astype(jnp.float32),
        lax.psum(shares[1].astype(jnp.bfloat16), "ep").astype(jnp.float32),
        lax.psum(shares[2].astype(jnp.bfloat16), "ep").astype(jnp.float32),
        lax.psum(shares[3].astype(jnp.bfloat16), "ep").astype(jnp.float32),
        lax.psum(shares[4].astype(jnp.bfloat16), "ep").astype(jnp.float32),
        lax.psum(shares[5].astype(jnp.bfloat16), "ep").astype(jnp.float32),
        lax.psum(shares[6].astype(jnp.bfloat16), "ep").astype(jnp.float32),
        lax.psum(shares[7].astype(jnp.bfloat16), "ep").astype(jnp.float32),
        lax.psum(shares[8].astype(jnp.bfloat16), "ep").astype(jnp.float32),
        lax.psum(shares[9].astype(jnp.bfloat16), "ep").astype(jnp.float32),
        lax.psum(shares[10].astype(jnp.bfloat16), "ep").astype(jnp.float32),
    )
    return (
        layer.astype(jnp.bfloat16),
        tokens_back,
        summed[8],
        summed[0],
        summed[1],
        summed[2],
        summed[3],
        summed[9],
        summed[7],
        summed[4],
        summed[5],
        summed[6],
        gate_final,
        up_final,
        down_final,
        summed[10].astype(jnp.int32),
    )


def solution(mesh):
    return jax.shard_map(
        per_device,
        mesh=mesh,
        in_specs=(
            P(("ep", "hp"), None),
            P("hp"),
            P("hp", None),
            P("hp", None),
            P("hp", None),
            P("hp", None),
            P("hp"),
            P("hp", None),
            P("hp", None),
            P("hp", None),
            P("hp", None),
            P("ep", None, "hp"),
            P("ep", None, "hp"),
            P("ep", "hp", None),
            P(("ep", "hp"), None),
            P(("ep", "hp"), None),
            P(("ep", "hp"), None),
        ),
        out_specs=(
            P(("ep", "hp"), None),
            P(("ep", "hp"), None),
            P("hp"),
            P("hp", None),
            P("hp", None),
            P("hp", None),
            P("hp", None),
            P("hp"),
            P("hp", None),
            P("hp", None),
            P("hp", None),
            P("hp", None),
            P("ep", None, "hp"),
            P("ep", None, "hp"),
            P("ep", "hp", None),
            P("hp"),
        ),
        check_vma=False,
    )
```

profile of v0, /device:TPU:0, one launch (start us, length us, event | category | flops | bytes accessed | tf_op | source)
XLA Modules:
  0.0 2347.7 jit_solution(12515351446244318177)
XLA Ops:
  23.1 18.5 all-gather.13.cloned.1.call-done
  47.9 24.6 %all-gather.19.cloned.1.call-done = bf16[1280,1280]{1,0:T(8,128)(2,1)} async-done(((bf16[320,1280]{1,0:T(8,128)(2,1)}), bf16[1280,1280]{1,0:T(8,128)(2,1)}) %all-gather.19.cloned.1.call-update) | async-done | bytes 3276816 | tf_op jit(solution)/shard_map/all_gather | solution.py:87
  79.4 23.9 %all-gather.17.cloned.1.call-done = bf16[1280,1280]{1,0:T(8,128)(2,1)} async-done(((bf16[320,1280]{1,0:T(8,128)(2,1)}), bf16[1280,1280]{1,0:T(8,128)(2,1)}) %all-gather.17.cloned.1.call-update) | async-done | bytes 3276816 | tf_op jit(solution)/shard_map/all_gather | solution.py:86
  135.4 23.1 all-gather.21.cloned.1.call-done
  193.6 32.4 %scatter_custom_fusion = bf16[2240,1280]{1,0:T(8,128)(2,1)} fusion(s32[1792]{0:T(1024)S(1)} %fusion.102, bf16[256,1280]{1,0:T(8,128)(2,1)S(1)} %multiply_convert_fusion.3, s32[2048]{0:T(1024)S(1)} %pad_clamp_fusion.1, bf16[]{:T(256)} %constant.54.clone.1), kind=kCustom, calls=%fused_computation.59 | custom fusion | bytes 5734402 | tf_op jit(solution)/shard_map/scatter | solution.py:169
  242.6 131.9 %all_to_all.20 = bf16[8,2,140,1280]{3,1,2,0:T(2,128)(2,1)S(1)} all-to-all(bf16[8,2,140,1280]{3,1,2,0:T(2,128)(2,1)S(1)} %copy.118), channel_id=1, replica_groups=mesh['ep'=8,'hp'=4] {'ep'}, dimensions={0} | all-to-all | bytes 11468800 | tf_op jit(solution)/shard_map/all_to_all | solution.py:172
  402.6 22.4 scatter_custom_fusion.1
  441.7 130.5 %all_to_all.21 = bf16[8,2,140,1280]{3,1,2,0:T(2,128)(2,1)S(1)} all-to-all(bf16[8,2,140,1280]{3,1,2,0:T(2,128)(2,1)S(1)} %copy.126), channel_id=1, replica_groups=mesh['ep'=8,'hp'=4] {'ep'}, dimensions={0} | all-to-all | bytes 11468800 | tf_op jit(solution)/shard_map/all_to_all | solution.py:210
  576.8 18.4 fusion.82
  608.7 110.3 %all-gather.33.cloned.1.call-done = bf16[32,2,140,1280]{3,2,0,1:T(8,128)(2,1)} async-done(((bf16[8,2,140,1280]{3,2,0,1:T(8,128)(2,1)}), bf16[32,2,140,1280]{3,2,0,1:T(8,128)(2,1)}) %all-gather.33.cloned.1.call-update) | async-done | bytes 22937616 | tf_op jit(solution)/shard_map/all_gather | solution.py:211
  719.0 22.8 fusion.6
  741.8 14.5 fusion.2
  756.3 43.0 %copy.120 = bf16[32,2,140,1280]{3,1,2,0:T(2,128)(2,1)} copy(bf16[32,2,140,1280]{3,2,0,1:T(8,128)(2,1)} %fusion.2) | data formatting | bytes 45875200 | tf_op jit(solution)/shard_map/convert_element_type | solution.py:184
  799.4 21.7 fusion.84
  821.1 27.2 %fusion.1 = bf16[32,2,140,1280]{3,2,0,1:T(8,128)(2,1)} fusion(f32[2,32,140,1280]{3,2,1,0:T(8,128)} %fusion.84, bf16[32,2,140,224]{3,2,0,1:T(8,128)(2,1)} %get-tuple-element.40, bf16[2,1280,224]{1,2,0:T(8,128)(2,1)S(1)} %copy-done.37), kind=kOutput, calls=%fused_computation.8 | convolution fusion | flops 5160960000 | bytes 73973760 | tf_op jit(solution)/shard_map/sxcf,xdf->sxcd/dot_general | solution.py:225
  848.3 43.1 %copy.128 = bf16[32,2,140,1280]{3,1,2,0:T(2,128)(2,1)} copy(bf16[32,2,140,1280]{3,2,0,1:T(8,128)(2,1)} %fusion.1) | data formatting | bytes 45875200 | tf_op jit(solution)/shard_map/convert_element_type | solution.py:229
  892.0 295.5 %all-reduce.15.cloned.1.call-done = bf16[32,2,140,1280]{3,1,2,0:T(2,128)(2,1)} async-done(((bf16[32,2,140,1280]{3,1,2,0:T(2,128)(2,1)}), bf16[32,2,140,1280]{3,1,2,0:T(2,128)(2,1)}) %all-reduce.15.cloned.1.call-update) | async-done | bytes 22937616
  1200.2 378.0 %all-reduce.17.cloned.1.call-done = bf16[32,2,140,1280]{3,1,2,0:T(2,128)(2,1)} async-done(((bf16[32,2,140,1280]{3,1,2,0:T(2,128)(2,1)}), bf16[32,2,140,1280]{3,1,2,0:T(2,128)(2,1)}) %all-reduce.17.cloned.1.call-update) | async-done | bytes 22937616
  1606.8 21.7 all-gather.25.cloned.1.call-done
  1632.0 21.9 all-gather.29.cloned.1.call-done
  1786.3 29.6 %fusion.59 = bf16[10,128,1024]{2,1,0:T(8,128)(2,1)} fusion(bf16[256,10,128]{0,2,1:T(8,128)(2,1)} %get-tuple-element.57, f32[10,256,1024]{2,1,0:T(8,128)} %fusion.136, f32[10,256,1024]{2,1,0:T(8,128)} %copy-done.2, f32[10,256]{1,0:T(8,128)S(1)} %log_add_fusion, pred[256,1024]{1,0:T(8,128)(4,1)S(1)} %copy-done.27), kind=kOutput, calls=%fused_computation.87 | convolution fusion | flops 701238784 | bytes 24520704 | tf_op jit(solution)/shard_map/hqk,qhd->khd/dot_general | solution.py:276
  1849.1 24.5 %broadcast_multiply_fusion = (f32[256,10,128]{0,2,1:T(8,128)}, f32[256,10,128]{0,2,1:T(8,128)}, f32[256,10,128]{0,2,1:T(8,128)}) fusion(f32[256,128]{0,1:T(8,128)S(1)} %copy-done.46, bf16[1024,10,128]{0,2,1:T(8,128)(2,1)} %bitcast.187, f32[10,256,1024]{2,1,0:T(8,128)} %fusion.136, f32[10,256,1024]{2,1,0:T(8,128)} %copy-done.2, ...), kind=kOutput, calls=%fused_computation.136 | convolution fusion | flops 700911104 | bytes 28583936 | tf_op jit(solution)/shard_map/hqk,khd->qhd/dot_general | solution.py:275
  1889.1 14.5 convolution_bitcast_fusion.1
  1903.6 17.0 reduce-scatter.25.cloned.1.call-done
  1920.7 35.1 %reduce-scatter.29.cloned.1.call-done = bf16[224,1280]{1,0:T(8,128)(2,1)} async-done(((bf16[896,1280]{1,0:T(8,128)(2,1)}), bf16[224,1280]{1,0:T(8,128)(2,1)}) %reduce-scatter.29.cloned.1.call-update) | async-done | bytes 573456 | tf_op jit(solution)/shard_map/reduce_scatter | solution.py:339
  1955.8 41.5 %reduce-scatter.23.cloned.1.call-done = bf16[320,1280]{1,0:T(8,128)(2,1)} async-done(((bf16[1280,1280]{1,0:T(8,128)(2,1)}), bf16[320,1280]{1,0:T(8,128)(2,1)}) %reduce-scatter.23.cloned.1.call-update) | async-done | bytes 819216 | tf_op jit(solution)/shard_map/reduce_scatter | solution.py:330
  1997.3 41.2 %reduce-scatter.21.cloned.1.call-done = bf16[320,1280]{1,0:T(8,128)(2,1)} async-done(((bf16[1280,1280]{1,0:T(8,128)(2,1)}), bf16[320,1280]{1,0:T(8,128)(2,1)}) %reduce-scatter.21.cloned.1.call-update) | async-done | bytes 819216 | tf_op jit(solution)/shard_map/reduce_scatter | solution.py:327
  2038.5 41.5 %reduce-scatter.19.cloned.1.call-done = bf16[320,1280]{1,0:T(8,128)(2,1)} async-done(((bf16[1280,1280]{1,0:T(8,128)(2,1)}), bf16[320,1280]{1,0:T(8,128)(2,1)}) %reduce-scatter.19.cloned.1.call-update) | async-done | bytes 819216 | tf_op jit(solution)/shard_map/reduce_scatter | solution.py:324
  2080.0 41.3 %reduce-scatter.17.cloned.1.call-done = bf16[320,1280]{1,0:T(8,128)(2,1)} async-done(((bf16[1280,1280]{1,0:T(8,128)(2,1)}), bf16[320,1280]{1,0:T(8,128)(2,1)}) %reduce-scatter.17.cloned.1.call-update) | async-done | bytes 819216 | tf_op jit(solution)/shard_map/reduce_scatter | solution.py:321
  2135.1 16.3 convolution_bitcast_fusion
  2170.8 39.9 %all-reduce.7 = (bf16[320]{0:T(512)(128)(2,1)S(1)}, bf16[320]{0:T(512)(128)(2,1)S(1)}, bf16[320,16]{0,1:T(8,128)(2,1)S(1)}, bf16[4]{0:T(256)(128)(2,1)S(1)}) all-reduce(bf16[320]{0:T(512)(128)(2,1)S(1)} %dynamic-slice.7, bf16[320]{0:T(512)(128)(2,1)S(1)} %dynamic-slice.9, ...), channel_id=1, replica_groups=mesh['ep'=8,'hp'=4] {'ep'}, use_global_device_ids=true, to_apply=%region_26.27 | all-reduce | flops 5764 | bytes 23056 | tf_op jit(solution)/shard_map/psum | solution.py:364
  2215.8 113.9 %all-reduce.19.cloned.1.call-done = (bf16[320,1280]{1,0:T(8,128)(2,1)}, bf16[320,1280]{1,0:T(8,128)(2,1)}, bf16[320,1280]{1,0:T(8,128)(2,1)}, bf16[320,1280]{1,0...) async-done(((bf16[320,1280]{1,0:T(8,128)(2,1)}, bf16[320,1280]{1,0:T(8,128)(2,1)}, bf16[320,1280]{1,0:T(8,128)(2,1)}, ...) | async-done | bytes 4997136 | tf_op jit(solution)/shard_map/psum | solution.py:356
  (353 shorter events, 447.5 us)
Async XLA Ops:
  7.2 711.8 %copy-start = (bf16[2,224,1280]{2,1,0:T(8,128)(2,1)S(1)}, bf16[2,224,1280]{2,1,0:T(8,128)(2,1)}, u32[]{:S(2)}) copy-start(bf16[2,224,1280]{2,1,0:T(8,128)(2,1)} %param.30) | copy-start | bytes 3440644
  7.2 34.4 %all-gather.13.cloned.1.call-start = ((), (), s32[]{:S(2)}) async-start(), calls=%async_computation.14 | async-start | bytes 4096000 | tf_op jit(solution)/shard_map/all_gather | solution.py:88
  7.9 64.5 %all-gather.19.cloned.1.call-start = ((), (), s32[]{:S(2)}) async-start(), calls=%async_computation.17 | async-start | bytes 4096000 | tf_op jit(solution)/shard_map/all_gather | solution.py:87
  8.7 94.7 %all-gather.17.cloned.1.call-start = ((), (), s32[]{:S(2)}) async-start(), calls=%async_computation.16 | async-start | bytes 4096000 | tf_op jit(solution)/shard_map/all_gather | solution.py:86
  9.4 121.5 %all-gather.15.cloned.1.call-start = ((), (), s32[]{:S(2)}) async-start(), calls=%async_computation.15 | async-start | bytes 3276800 | tf_op jit(solution)/shard_map/all_gather | solution.py:125
  21.8 81.6 %copy-start.51 = (f32[1280]{0:T(1024)}, f32[1280]{0:T(1024)S(1)}, u32[]{:S(2)}) copy-start(f32[1280]{0:T(1024)S(1)} %convert_element_type.256) | copy-start | bytes 15364
  23.1 80.3 %copy-start.67 = (f32[256]{0:T(256)}, f32[256]{0:T(256)S(1)}, u32[]{:S(2)}) copy-start(f32[256]{0:T(256)S(1)} %add_rsqrt_fusion.1) | copy-start | bytes 3076
  45.7 112.8 %all-gather.21.cloned.1.call-start = ((), (), s32[]{:S(2)}) async-start(), calls=%async_computation.18 | async-start | bytes 3276800 | tf_op jit(solution)/shard_map/all_gather | solution.py:124
  114.4 74.8 %all-gather.23.cloned.1.call-start = ((), (), s32[]{:S(2)}) async-start(), calls=%async_computation.19 | async-start | bytes 4096000 | tf_op jit(solution)/shard_map/all_gather | solution.py:89
  115.0 461.1 %all-gather.31.cloned.1.call-start = ((), (), s32[]{:S(2)}) async-start(), calls=%async_computation.23 | async-start | bytes 29491200 | tf_op jit(solution)/shard_map/all_gather | solution.py:173
  115.6 76.8 %copy-start.55 = (f32[1280]{0:T(1024)}, f32[1280]{0:T(1024)S(1)}, u32[]{:S(2)}) copy-start(f32[1280]{0:T(1024)S(1)} %convert_element_type.266) | copy-start | bytes 15364
  122.9 279.7 %copy-start.63 = (s32[1792]{0:T(1024)}, s32[1792]{0:T(1024)S(1)}, u32[]{:S(2)}) copy-start(s32[1792]{0:T(1024)S(1)} %fusion.102) | copy-start | bytes 21508
  193.6 207.7 %copy-start.7 = (bf16[256,1280]{1,0:T(8,128)(2,1)}, bf16[256,1280]{1,0:T(8,128)(2,1)S(1)}, u32[]{:S(2)}) copy-start(bf16[256,1280]{1,0:T(8,128)(2,1)S(1)} %multiply_convert_fusion.3) | copy-start | bytes 1966084
  377.8 341.2 %all-gather.33.cloned.1.call-start = ((), (), s32[]{:S(2)}) async-start(), calls=%async_computation.24 | async-start | bytes 29491200 | tf_op jit(solution)/shard_map/all_gather | solution.py:211
  575.6 612.0 %all-reduce.15.cloned.1.call-start = ((), (), s32[]{:S(2)}) async-start(), calls=%async_computation.35 | async-start | bytes 45875200
  799.3 778.8 %all-reduce.17.cloned.1.call-start = ((), (), s32[]{:S(2)}) async-start(), calls=%async_computation.36 | async-start | bytes 45875200
  1193.9 390.8 %all-to-all-start.1 = ((bf16[8,2,140,1280]{3,1,2,0:T(2,128)(2,1)}), bf16[8,2,140,1280]{3,1,2,0:T(2,128)(2,1)}, u32[]{:S(2)}, u32[]{:S(2)}) async-start(bf16[8,2,140,1280]{3,1,2,0:T(2,128)(2,1)} %constant_dynamic-slice_fusion.1), calls=%async_computation.1 | async-start | bytes 11468800 | tf_op jit(solution)/shard_map/all_to_all | solution.py:186
  1199.4 404.0 %all-gather.27.cloned.1.call-start = ((), (), s32[]{:S(2)}) async-start(), calls=%async_computation.21 | async-start | bytes 2867200 | tf_op jit(solution)/shard_map/all_gather | solution.py:91
  1584.7 132.0 %all-to-all-start.3 = ((bf16[8,2,140,1280]{3,1,2,0:T(2,128)(2,1)}), bf16[8,2,140,1280]{3,1,2,0:T(2,128)(2,1)}, u32[]{:S(2)}, u32[]{:S(2)}) async-start(bf16[8,2,140,1280]{3,1,2,0:T(2,128)(2,1)} %constant_dynamic-slice_fusion), calls=%async_computation.3 | async-start | bytes 11468800 | tf_op jit(solution)/shard_map/all_to_all | solution.py:232
  1590.4 38.2 %all-gather.25.cloned.1.call-start = ((), (), s32[]{:S(2)}) async-start(), calls=%async_computation.20 | async-start | bytes 2867200 | tf_op jit(solution)/shard_map/all_gather | solution.py:90
  1591.0 62.9 %all-gather.29.cloned.1.call-start = ((), (), s32[]{:S(2)}) async-start(), calls=%async_computation.22 | async-start | bytes 2867200 | tf_op jit(solution)/shard_map/all_gather | solution.py:92
  1591.7 238.8 %reduce-scatter.15.cloned.1.call-start = ((), (), s32[]{:S(2)}) async-start(), calls=%async_computation.26 | async-start | bytes 3276800 | tf_op jit(solution)/shard_map/reduce_scatter | solution.py:289
  1778.4 70.7 %reduce-scatter.13.cloned.1.call-start = ((), (), s32[]{:S(2)}) async-start(), calls=%async_computation.25 | async-start | bytes 3276800 | tf_op jit(solution)/shard_map/reduce_scatter | solution.py:286
  1815.9 87.7 %reduce-scatter.27.cloned.1.call-start = ((), (), s32[]{:S(2)}) async-start(), calls=%async_computation.32 | async-start | bytes 2867200 | tf_op jit(solution)/shard_map/reduce_scatter | solution.py:336
  1819.3 101.4 %reduce-scatter.25.cloned.1.call-start = ((), (), s32[]{:S(2)}) async-start(), calls=%async_computation.31 | async-start | bytes 2867200 | tf_op jit(solution)/shard_map/reduce_scatter | solution.py:333
  1822.7 133.1 %reduce-scatter.29.cloned.1.call-start = ((), (), s32[]{:S(2)}) async-start(), calls=%async_computation.33 | async-start | bytes 2867200 | tf_op jit(solution)/shard_map/reduce_scatter | solution.py:339
  1826.0 171.3 %reduce-scatter.23.cloned.1.call-start = ((), (), s32[]{:S(2)}) async-start(), calls=%async_computation.30 | async-start | bytes 4096000 | tf_op jit(solution)/shard_map/reduce_scatter | solution.py:330
  1830.4 208.1 %reduce-scatter.21.cloned.1.call-start = ((), (), s32[]{:S(2)}) async-start(), calls=%async_computation.29 | async-start | bytes 4096000 | tf_op jit(solution)/shard_map/reduce_scatter | solution.py:327
  1835.6 244.5 %reduce-scatter.19.cloned.1.call-start = ((), (), s32[]{:S(2)}) async-start(), calls=%async_computation.28 | async-start | bytes 4096000 | tf_op jit(solution)/shard_map/reduce_scatter | solution.py:324
  1880.7 240.6 %reduce-scatter.17.cloned.1.call-start = ((), (), s32[]{:S(2)}) async-start(), calls=%async_computation.27 | async-start | bytes 4096000 | tf_op jit(solution)/shard_map/reduce_scatter | solution.py:321
  1886.6 268.3 %reduce-scatter.31.cloned.1.call-start = ((), (), s32[]{:S(2)}) async-start(), calls=%async_computation.34 | async-start | bytes 409600
  1889.0 440.7 %all-reduce.19.cloned.1.call-start = ((), (), s32[]{:S(2)}) async-start(), calls=%async_computation.37 | async-start | bytes 9994240 | tf_op jit(solution)/shard_map/psum | solution.py:356
  (71 other events, 748.1 us)
Sparse Core Ops, SparseCore 0:
  9.6 31.9 all-gather.12
  43.2 29.2 all-gather.18
  74.0 29.2 all-gather.16
  105.3 25.5 all-gather.14
  132.9 25.5 all-gather.20
  159.9 29.2 all-gather.22
  377.9 142.9 all-gather.30
  575.7 143.2 all-gather.32
  799.5 388.0 all-reduce.14
  1190.0 388.0 all-reduce.16
  1579.7 23.6 all-gather.26
  1604.8 23.6 all-gather.24
  1630.1 23.6 all-gather.28
  1778.5 32.8 reduce-scatter.14
  1816.0 32.9 reduce-scatter.12
  1852.1 32.7 reduce-scatter.26
  1888.1 32.5 reduce-scatter.24
  1923.1 32.6 reduce-scatter.28
  1958.5 38.7 reduce-scatter.22
  1999.7 38.7 reduce-scatter.20
  2041.2 38.7 reduce-scatter.18
  2082.6 38.7 reduce-scatter.16
  2124.6 20.4 reduce-scatter.30
  2149.5 180.1 all-reduce.18
where the time goes:
time: 2360 us; the launch traced here: 2350 us
  waiting for transfers between devices  1310 us (56%)
  blocking collectives  323 us (14%)
  matrix products  308 us (13%)
  local copies, waits for them, and re-layouts  296 us (13%)
  other arithmetic  78.5 us (3%)
    unnamed x27, waiting for transfers between devices  678 us
    all_to_all x1, blocking collectives, per_device(): lax.all_to_all(outgoing, 'ep', split_axis=0, concat_axis=0, tiled=True)  132 us
    all_to_all x1, blocking collectives, per_device(): lax.all_to_all(outgoing_back, 'ep', split_axis=0, concat_axis=0, tiled=True)  130 us
    psum x1, waiting for transfers between devices, per_device(): lax.psum(shares[0].astype(jnp.bfloat16), 'ep').astype(jnp.float32)  114 us
    all_gather x1, waiting for transfers between devices, per_device(): rows_back = lax.all_gather(incoming_back, 'hp', axis=0, tiled=True)  110 us
  transfers between devices with their start and end apart: 26, of which 21 were waited for; matrix products, arithmetic and copies ran while one was open for 20% of the time, Pallas kernels for 0%

commit v1 on v0

v1 whole, which is shorter than its diff:
```python
import functools

import jax
import jax.numpy as jnp
from jax import lax
from jax.experimental import pallas as pl
from jax.experimental.pallas import tpu as pltpu
from jax.sharding import PartitionSpec as P

H = 10
HD = 128
LANES = 128
BF = jnp.bfloat16
F32 = jnp.float32
epsilon = 1e-06
MIB = 1 << 20


def dot(left, right, over=(1, 0)):
    return lax.dot_general(
        left, right, (((over[0],), (over[1],)), ((), ())), preferred_element_type=F32
    )


def swap_core(v):
    return lax.ppermute(v, "hp", [(i, i ^ 1) for i in range(4)])


def swap_y(v):
    return lax.ppermute(v, "hp", [(i, i ^ 2) for i in range(4)])


def swap_pair(v):
    n = lax.axis_size("ep")
    return lax.ppermute(v, "ep", [(i, i ^ 1) for i in range(n)])


def ring(v):
    n = lax.axis_size("ep")
    return lax.ppermute(v, "ep", [(i, (i + 2) % n) for i in range(n)])


def gather_hp(v):
    far = swap_y(v)
    return [v, swap_core(v), far, swap_core(far)]


def scatter_hp(parts):
    near = swap_core(parts[1].astype(BF)).astype(F32) + parts[0]
    over = swap_core(parts[3].astype(BF)).astype(F32) + parts[2]
    return near + swap_y(over.astype(BF)).astype(F32)


def relative(v, h, axis):
    b = jnp.split(v, 4, axis=axis)
    odd = (h & 1) == 1
    c = [jnp.where(odd, b[i ^ 1], b[i]) for i in range(4)]
    high = (h & 2) == 2
    return jnp.concatenate([jnp.where(high, c[i ^ 2], c[i]) for i in range(4)], axis=axis)


def gather_ep(v):
    stages = lax.axis_size("ep") // 2
    own, out = v, []
    for k in range(stages):
        out.append((own, swap_pair(own)))
        if k < stages - 1:
            own = ring(own)
    return out


def scatter_ep(parts):
    stages = len(parts)
    total = None
    for k in list(range(1, stages)) + [0]:
        here = parts[k][0].astype(F32) + swap_pair(parts[k][1]).astype(F32)
        if total is not None:
            here = here + total.astype(F32)
        total = here if k == 0 else ring(here.astype(BF))
    return total


def sum_ep(v, e):
    n = lax.axis_size("ep")
    stages = n // 2
    x, z = e & 1, e >> 1
    halves = v.reshape(2, v.shape[0] // 2, v.shape[1])
    mine = lax.dynamic_index_in_dim(halves, x, 0, False)
    other = lax.dynamic_index_in_dim(halves, 1 - x, 0, False)
    mine = mine + swap_pair(other.astype(BF)).astype(F32)
    chunks = mine.reshape(stages, mine.shape[0] // stages, mine.shape[1])

    def chunk(back):
        return lax.dynamic_index_in_dim(chunks, (z + stages - back) % stages, 0, False)

    total = chunk(1 % stages)
    for back in list(range(2, stages)) + [0]:
        total = ring(total.astype(BF)).astype(F32) + chunk(back)
    total = total.astype(BF)
    half = jnp.zeros(chunks.shape, BF)
    for back in range(stages):
        half = lax.dynamic_update_index_in_dim(half, total, (z + stages - back) % stages, 0)
        if back < stages - 1:
            total = ring(total)
    half = half.reshape(mine.shape)
    far = swap_pair(half)
    low = jnp.where(x == 0, half, far)
    high = jnp.where(x == 0, far, half)
    return jnp.concatenate([low, high], axis=0).astype(F32)


def sum_all_small(v):
    v = v + swap_core(v)
    v = v + swap_y(v)
    n = lax.axis_size("ep")
    bit = 1
    while bit < n:
        v = v + lax.ppermute(v, "ep", [(i, i ^ bit) for i in range(n)])
        bit *= 2
    return v


def score_mask(h_ref, rows, cols):
    h = h_ref[0]
    at = lax.broadcasted_iota(jnp.int32, (rows, cols), 0) + h * rows
    key = lax.broadcasted_iota(jnp.int32, (rows, cols), 1)
    block = key // rows
    other = jnp.where(
        block == 0, h, jnp.where(block == 1, h ^ 2, jnp.where(block == 2, h ^ 1, h ^ 3))
    )
    return other * rows + key % rows <= at


def attend_kernel(h_ref, q_ref, ka_ref, kb_ref, va_ref, vb_ref, o_ref, lse_ref):
    rows = q_ref.shape[0]
    half = ka_ref.shape[0]
    q = q_ref[...]
    s = jnp.concatenate([dot(q, ka_ref[...], (1, 1)), dot(q, kb_ref[...], (1, 1))], axis=1)
    s = jnp.where(score_mask(h_ref, rows, 2 * half), s * HD ** (-0.5), -1e30)
    top = jnp.max(s, axis=1, keepdims=True)
    p = jnp.exp(s - top)
    total = jnp.sum(p, axis=1, keepdims=True)
    p = (p * (1.0 / total)).astype(BF)
    o = dot(p[:, :half], va_ref[...]) + dot(p[:, half:], vb_ref[...])
    o_ref[...] = o.astype(BF)
    lse_ref[...] = jnp.broadcast_to(top + jnp.log(total), lse_ref.shape)


def attend_back_kernel(
    h_ref,
    q_ref,
    ka_ref,
    kb_ref,
    va_ref,
    vb_ref,
    d_ref,
    lse_ref,
    dq_ref,
    dka_ref,
    dva_ref,
    dkb_ref,
    dvb_ref,
):
    rows = q_ref.shape[0]
    half = ka_ref.shape[0]
    q, d = q_ref[...], d_ref[...]
    s = jnp.concatenate([dot(q, ka_ref[...], (1, 1)), dot(q, kb_ref[...], (1, 1))], axis=1)
    s = jnp.where(score_mask(h_ref, rows, 2 * half), s * HD ** (-0.5), -1e30)
    p = jnp.exp(s - lse_ref[:, 0:1])
    back = jnp.concatenate([dot(d, va_ref[...], (1, 1)), dot(d, vb_ref[...], (1, 1))], axis=1)
    inner = jnp.sum(p * back, axis=1, keepdims=True)
    sb = (p * (back - inner) * HD ** (-0.5)).astype(BF)
    p = p.astype(BF)
    dq_ref[...] = dot(sb[:, :half], ka_ref[...]) + dot(sb[:, half:], kb_ref[...])
    dk = dot(sb, q, (0, 0))
    dv = dot(p, d, (0, 0))
    dka_ref[...] = dk[:half]
    dkb_ref[...] = dk[half:].astype(BF)
    dva_ref[...] = dv[:half]
    dvb_ref[...] = dv[half:].astype(BF)


def head_spec(rows, skip=0):
    return pl.BlockSpec((rows, HD), lambda i, h: (0, i + skip))


def attend(h, q, kv_a, kv_b):
    rows, width = q.shape
    half = kv_a.shape[0]
    flops = 4 * rows * 2 * half * width
    return pl.pallas_call(
        attend_kernel,
        grid_spec=pltpu.PrefetchScalarGridSpec(
            num_scalar_prefetch=1,
            grid=(H,),
            in_specs=[
                head_spec(rows),
                head_spec(half),
                head_spec(half),
                head_spec(half, H),
                head_spec(half, H),
            ],
            out_specs=[head_spec(rows), head_spec(rows)],
        ),
        out_shape=[
            jax.ShapeDtypeStruct((rows, width), BF),
            jax.ShapeDtypeStruct((rows, width), F32),
        ],
        compiler_params=pltpu.CompilerParams(vmem_limit_bytes=40 * MIB),
        cost_estimate=pl.CostEstimate(
            flops=flops, bytes_accessed=8 * MIB, transcendentals=rows * 2 * half * H
        ),
    )(h, q, kv_a, kv_b, kv_a, kv_b)


def attend_back(h, q, kv_a, kv_b, d, lse):
    rows, width = q.shape
    half = kv_a.shape[0]
    flops = 10 * rows * 2 * half * width
    return pl.pallas_call(
        attend_back_kernel,
        grid_spec=pltpu.PrefetchScalarGridSpec(
            num_scalar_prefetch=1,
            grid=(H,),
            in_specs=[
                head_spec(rows),
                head_spec(half),
                head_spec(half),
                head_spec(half, H),
                head_spec(half, H),
                head_spec(rows),
                head_spec(rows),
            ],
            out_specs=[head_spec(rows)] + [head_spec(half)] * 4,
        ),
        out_shape=[
            jax.ShapeDtypeStruct((rows, width), F32),
            jax.ShapeDtypeStruct((half, width), F32),
            jax.ShapeDtypeStruct((half, width), F32),
            jax.ShapeDtypeStruct((half, width), BF),
            jax.ShapeDtypeStruct((half, width), BF),
        ],
        compiler_params=pltpu.CompilerParams(vmem_limit_bytes=40 * MIB),
        cost_estimate=pl.CostEstimate(
            flops=flops, bytes_accessed=16 * MIB, transcendentals=rows * 2 * half * H
        ),
    )(h, q, kv_a, kv_b, kv_a, kv_b, d, lse)


def pick_matrix(meta, col, capacity):
    lane = lax.broadcasted_iota(jnp.int32, meta.shape, 1)
    code = jnp.sum(jnp.where(lane == col, meta.astype(F32), 0.0), axis=1, keepdims=True)
    place = lax.broadcasted_iota(jnp.int32, (meta.shape[0], capacity), 1).astype(F32)
    return jnp.where(code == place, 1.0, 0.0).astype(BF)


def expert_kernel(capacity, total, olds, e_ref, x0_ref, x1_ref, g0_ref, g1_ref, *refs):
    gates, ups, downs = refs[0:4], refs[4:8], refs[8:12]
    sg_ref, su_ref, sd_ref, sgg_old, sdg_old = refs[12:17]
    (
        dx0_ref,
        dx1_ref,
        sgg_ref,
        sdg_ref,
        sa_ref,
        xr_ref,
        gr_ref,
        gi_ref,
        ui_ref,
        wa_ref,
    ) = refs[17 + olds :]
    xs, gs, dxs = (x0_ref, x1_ref), (g0_ref, g1_ref), (dx0_ref, dx1_ref)
    width = sg_ref.shape[0]
    tokens = x0_ref.shape[0]
    c = capacity
    x2 = jnp.concatenate([r[:, :width] for r in xs], axis=0)
    g2 = jnp.concatenate([r[:, :width] for r in gs], axis=0)
    hg, hu = dot(x2, sg_ref[...]), dot(x2, su_ref[...])
    ab = dot(g2, sd_ref[...], (1, 1))
    s = jax.nn.sigmoid(hg)
    silu = hg * s
    act = (silu * hu).astype(BF)
    gi = (ab * hu * (s * (1.0 + hg * (1.0 - s)))).astype(BF)
    ui = (ab * silu).astype(BF)
    sa_ref[0] = act
    gu = jnp.concatenate([gi, ui], axis=1)
    sgg_ref[...] = sgg_old[...] + dot(x2, gu, (0, 0))
    sdg_ref[...] = sdg_old[...] + dot(act, g2, (0, 0))
    dx = dot(gi, sg_ref[...], (1, 1)) + dot(ui, su_ref[...], (1, 1))
    totals = [dx[:tokens], dx[tokens:]]
    metas = [0.0, 0.0]
    lane = lax.broadcasted_iota(jnp.int32, (2 * c, LANES), 1)
    for x in range(2):
        col = 2 * e_ref[0] + x
        picks, weights = [], []
        for j in range(2):
            pick = pick_matrix(gs[j][:, width:], col, c)
            picks.append(pick)
            rows = dot(pick, xs[j][...], (0, 0))
            xr_ref[x, 0, j * c : (j + 1) * c, :] = rows[:, :width].astype(BF)
            weights.append(rows[:, width:])
            gr_ref[x, 0, j * c : (j + 1) * c, :] = dot(pick, gs[j][:, :width], (0, 0)).astype(BF)
        w = jnp.concatenate(weights, axis=0)
        w = jnp.sum(jnp.where(lane == col, w, 0.0), axis=1, keepdims=True)
        xr, gr = xr_ref[x, 0], gr_ref[x, 0]
        dxr = jnp.zeros((2 * c, width), F32)
        wb = jnp.zeros((2 * c, 1), F32)
        for r in range(4):
            wg, wu, wd = gates[r][x], ups[r][x], downs[r][x]
            hg, hu = dot(xr, wg), dot(xr, wu)
            ab = dot(gr, wd, (1, 1))
            s = jax.nn.sigmoid(hg)
            silu = hg * s
            act = silu * hu
            wb = wb + jnp.sum(act * ab, axis=1, keepdims=True)
            ab = ab * w
            gi = (ab * hu * (s * (1.0 + hg * (1.0 - s)))).astype(BF)
            ui = (ab * silu).astype(BF)
            gi_ref[r, x, 0] = gi
            ui_ref[r, x, 0] = ui
            wa_ref[r, x, 0] = (act * w).astype(BF)
            dxr = dxr + dot(gi, wg, (1, 1)) + dot(ui, wu, (1, 1))
        dxr = dxr.astype(BF)
        high = wb.astype(BF).astype(F32)
        meta = jnp.where(lane == col, high, 0.0) + jnp.where(lane == total + col, wb - high, 0.0)
        meta = meta.astype(BF)
        for j in range(2):
            span = slice(j * c, (j + 1) * c)
            totals[j] = totals[j] + dot(picks[j], dxr[span])
            metas[j] = metas[j] + dot(picks[j], meta[span])
    for j in range(2):
        dxs[j][:, :width] = totals[j].astype(BF)
        dxs[j][:, width:] = metas[j].astype(BF)


def expert_out_kernel(capacity, e_ref, g0_ref, g1_ref, wa_ref, sa_ref, *refs):
    downs, sd_ref, outs = refs[0:4], refs[4], refs[5:7]
    width = sd_ref.shape[1]
    tokens = g0_ref.shape[0]
    c = capacity
    gs = (g0_ref, g1_ref)
    shared = dot(sa_ref[0], sd_ref[...])
    totals = [shared[:tokens], shared[tokens:]]
    for x in range(2):
        rows = jnp.zeros((2 * c, width), F32)
        for r in range(4):
            rows = rows + dot(wa_ref[r, x, 0], downs[r][x])
        rows = rows.astype(BF)
        for j in range(2):
            pick = pick_matrix(gs[j][...], 2 * e_ref[0] + x, c)
            totals[j] = totals[j] + dot(pick, rows[j * c : (j + 1) * c])
    for j in range(2):
        outs[j][...] = totals[j].astype(BF)


def whole(shape):
    return pl.BlockSpec(shape, lambda i, e: (0,) * len(shape), pipeline_mode=pl.Buffered(1))


def expert_stage(
    k, stages, capacity, total, e, x_pair, g_pair, gates, ups, downs, sg, su, sd, carry, bufs
):
    tokens, wide = x_pair[0].shape
    width = sg.shape[0]
    hidden = gates[0].shape[2]
    c2 = 2 * capacity
    shared = sg.shape[1]
    olds = 0 if bufs is None else 6
    shapes = [
        ((stages, 2 * tokens, shared), (1, 2 * tokens, shared), (k, 0, 0)),
        ((2, stages, c2, width), (2, 1, c2, width), (0, k, 0, 0)),
        ((2, stages, c2, width), (2, 1, c2, width), (0, k, 0, 0)),
        ((4, 2, stages, c2, hidden), (4, 2, 1, c2, hidden), (0, 0, k, 0, 0)),
        ((4, 2, stages, c2, hidden), (4, 2, 1, c2, hidden), (0, 0, k, 0, 0)),
        ((4, 2, stages, c2, hidden), (4, 2, 1, c2, hidden), (0, 0, k, 0, 0)),
    ]

    def at(block, where):
        return pl.BlockSpec(block, lambda i, e: where)

    ins = [e, *x_pair, *g_pair, *gates, *ups, *downs, sg, su, sd, *carry]
    in_specs = [whole(v.shape) for v in ins[1:]]
    alias = {}
    if bufs is not None:
        for n, b in enumerate(bufs):
            alias[len(ins)] = 4 + n
            ins.append(b)
            in_specs.append(pl.BlockSpec(memory_space=pl.ANY))
    out_shape = [jax.ShapeDtypeStruct((tokens, wide), BF)] * 2 + [
        jax.ShapeDtypeStruct(v.shape, v.dtype) for v in carry
    ]
    out_specs = [whole((tokens, wide))] * 2 + [whole(v.shape) for v in carry]
    for full, block, where in shapes:
        out_shape.append(jax.ShapeDtypeStruct(full, BF))
        out_specs.append(at(block, where))
    outs = pl.pallas_call(
        functools.partial(expert_kernel, capacity, total, olds),
        grid_spec=pltpu.PrefetchScalarGridSpec(
            num_scalar_prefetch=1, grid=(1,), in_specs=in_specs, out_specs=out_specs
        ),
        out_shape=out_shape,
        input_output_aliases=alias,
        compiler_params=pltpu.CompilerParams(vmem_limit_bytes=60 * MIB),
        cost_estimate=pl.CostEstimate(
            flops=20 * c2 * width * 4 * hidden, bytes_accessed=24 * MIB, transcendentals=c2 * 8 * hidden
        ),
    )(*ins)
    return outs[0:2], outs[2:4], outs[4:]


def expert_out(k, capacity, e, g_pair, wa, sa, downs, sd):
    tokens = g_pair[0].shape[0]
    width = sd.shape[1]
    c2 = wa.shape[3]
    last = g_pair[0].shape[1] // LANES - 1
    meta = pl.BlockSpec((tokens, LANES), lambda i, e: (0, last))
    return pl.pallas_call(
        functools.partial(expert_out_kernel, capacity),
        grid_spec=pltpu.PrefetchScalarGridSpec(
            num_scalar_prefetch=1,
            grid=(1,),
            in_specs=[
                meta,
                meta,
                pl.BlockSpec((4, 2, 1, c2, wa.shape[4]), lambda i, e: (0, 0, k, 0, 0)),
                pl.BlockSpec((1,) + sa.shape[1:], lambda i, e: (k, 0, 0)),
            ]
            + [whole(d.shape) for d in downs]
            + [whole(sd.shape)],
            out_specs=[whole((tokens, width))] * 2,
        ),
        out_shape=[jax.ShapeDtypeStruct((tokens, width), BF)] * 2,
        compiler_params=pltpu.CompilerParams(vmem_limit_bytes=40 * MIB),
        cost_estimate=pl.CostEstimate(
            flops=4 * c2 * width * 4 * wa.shape[4], bytes_accessed=10 * MIB, transcendentals=0
        ),
    )(e, *g_pair, wa, sa, *downs, sd)


def rms(values):
    return lax.rsqrt(jnp.mean(values * values, axis=-1, keepdims=True) + epsilon)


def norm_back(values, inv, gain, upstream):
    weighted = upstream * gain
    inner = jnp.mean(weighted * values, axis=-1, keepdims=True)
    to_input = weighted * inv - values * (inv * inv * inv * inner)
    return to_input, jnp.sum(upstream * values * inv, axis=0)


def half_turn(v):
    lane = lax.broadcasted_iota(jnp.int32, v.shape, 1)
    return jnp.where(
        lane % HD < HD // 2, -jnp.roll(v, -HD // 2, axis=1), jnp.roll(v, HD // 2, axis=1)
    )


def rotary_tables(positions):
    exponent = jnp.arange(HD // 2, dtype=F32) * (2.0 / HD)
    theta = positions.astype(F32)[:, None] * jnp.power(10000.0, -exponent)[None, :]
    theta = jnp.concatenate([theta, theta], axis=-1)
    return jnp.tile(jnp.cos(theta), (1, H)), jnp.tile(jnp.sin(theta), (1, H))


def per_device(
    tokens,
    attn_gain,
    query_weight,
    key_weight,
    value_weight,
    out_weight,
    ffn_gain,
    router_weight,
    shared_gate,
    shared_up,
    shared_down,
    expert_gate,
    expert_up,
    expert_down,
    routes,
    keep_mask,
    cotangent,
):
    e, h = lax.axis_index("ep"), lax.axis_index("hp")
    ep = lax.axis_size("ep")
    stages = ep // 2
    rows, width = tokens.shape
    top = routes.shape[1]
    total = router_weight.shape[1]
    capacity = -(-(5 * rows * top // (4 * total)) // 16) * 16
    e_arr, h_arr = jnp.full((1,), e, jnp.int32), jnp.full((1,), h, jnp.int32)

    far_tokens = swap_y(tokens)
    k_w, v_w = gather_hp(key_weight), gather_hp(value_weight)
    q_w = gather_hp(query_weight)
    o_w = gather_hp(out_weight)
    gates, ups, downs = gather_hp(expert_gate), gather_hp(expert_up), gather_hp(expert_down)
    units = shared_down.shape[0] // ep
    tiny = [attn_gain[:, None], ffn_gain[:, None], router_weight]
    small = jnp.concatenate(tiny + [jnp.zeros((width // 4, LANES - 2 - total), BF)], axis=1)

    def mine(v):
        v = v.reshape(width // 4, 4, -1)
        v = lax.dynamic_slice_in_dim(v, e * units, units, axis=2).reshape(width // 4, 4 * units)
        return jnp.pad(v, ((0, 0), (0, LANES - 4 * units)))

    small = jnp.concatenate([small, mine(shared_gate), mine(shared_up)], axis=1)
    small = jnp.concatenate(gather_hp(small), axis=0)
    gain_one = small[:, 0].astype(F32)[None, :]
    small = relative(small, h, 0)
    gain_two = small[:, 1].astype(F32)[None, :]
    router = small[:, 2 : 2 + total]
    sg, su = small[:, LANES : 2 * LANES], small[:, 2 * LANES :]
    sd = lax.dynamic_slice_in_dim(shared_down, e * units, units, axis=0)
    sd = relative(jnp.concatenate(gather_hp(sd), axis=0), h, 0)
    sd = jnp.pad(sd, ((0, LANES - 4 * units), (0, 0)))

    expert = jnp.arange(total, dtype=jnp.int32)
    hit_each = routes[:, :, None] == expert[None, None, :]
    hit = jnp.any(hit_each, axis=1)
    kept = jnp.sum(jnp.where(hit_each, keep_mask[:, :, None], 0), axis=1)
    below = (jnp.arange(rows)[:, None] > jnp.arange(rows)[None, :]).astype(BF)
    place = jnp.where(hit, dot(below, hit.astype(BF)), -1.0)
    kept = kept.astype(F32)
    g_ext = jnp.concatenate(
        [
            cotangent,
            place.astype(BF),
            jnp.zeros((rows, LANES - total), BF),
        ],
        axis=1,
    )
    g_blocks = gather_ep(g_ext)

    pos = jnp.arange(rows, dtype=jnp.int32)
    pos = jnp.concatenate([h * rows + pos, (h ^ 2) * rows + pos])
    cosine, sine = rotary_tables(pos)
    residual = tokens.astype(F32)
    both = relative(jnp.concatenate([tokens, far_tokens], axis=0), h, 1).astype(F32)
    inv_one = rms(both)
    first_in = (both * inv_one * gain_one).astype(BF)

    def rotate(v, n):
        return v * cosine[:n] + half_turn(v) * sine[:n]

    def rotate_back(v, n):
        return v * cosine[:n] - half_turn(v * sine[:n])

    k_w, v_w = jnp.concatenate(k_w, axis=0), jnp.concatenate(v_w, axis=0)
    q_w, o_w = jnp.concatenate(q_w, axis=0), jnp.concatenate(o_w, axis=0)
    keys = rotate(dot(first_in, k_w), 2 * rows).astype(BF)
    values = dot(first_in, v_w).astype(BF)
    kv_a = jnp.concatenate([keys, values], axis=1)
    kv_b = swap_core(kv_a)
    query = rotate(dot(first_in[:rows], q_w), rows).astype(BF)
    mixed, lse = attend(h_arr, query, kv_a, kv_b)
    mixed_rel = relative(mixed, h, 1)
    middle = residual + dot(mixed_rel, o_w)
    inv_two = rms(middle)
    second_in = (middle * inv_two * gain_two).astype(BF)

    logits = jnp.where(hit, dot(second_in, router), -1e30)
    gates_of = jnp.where(hit, jnp.exp(logits - jnp.max(logits, axis=1, keepdims=True)), 0.0)
    gates_of = gates_of / jnp.sum(gates_of, axis=1, keepdims=True)
    pair_weight = gates_of * kept
    x_ext = jnp.concatenate(
        [second_in, pair_weight.astype(BF), jnp.zeros((rows, LANES - total), BF)], axis=1
    )

    x_blocks = gather_ep(x_ext)
    carry = (jnp.zeros((width, 2 * LANES), F32), jnp.zeros((LANES, width), F32))
    bufs, dx_parts = None, []
    for k in range(stages):
        dx, carry, bufs = expert_stage(
            k,
            stages,
            capacity,
            total,
            e_arr,
            x_blocks[k],
            g_blocks[k],
            gates,
            ups,
            downs,
            sg,
            su,
            sd,
            carry,
            bufs,
        )
        dx_parts.append(dx)
    dx_sum = scatter_ep(dx_parts)
    sa, xr, gr, gi, ui, wa = bufs
    out_parts = [
        expert_out(k, capacity, e_arr, g_blocks[k], wa, sa, downs, sd) for k in range(stages)
    ]
    layer = (middle + scatter_ep(out_parts)).astype(BF)

    flat = (2, stages * 2 * capacity)
    xr, gr = xr.reshape(flat + (width,)), gr.reshape(flat + (width,))
    gi, ui, wa = (v.reshape((4,) + flat + (v.shape[-1],)) for v in (gi, ui, wa))

    def expert_grad(spec, left, right):
        return jnp.einsum(spec, left, right, preferred_element_type=F32)

    gate_grad = scatter_hp([expert_grad("xnd,xnf->xdf", xr, gi[r]) for r in range(4)])
    up_grad = scatter_hp([expert_grad("xnd,xnf->xdf", xr, ui[r]) for r in range(4)])
    down_grad = scatter_hp([expert_grad("xnf,xnd->xfd", wa[r], gr) for r in range(4)])

    sgg, sdg = carry
    sgg = relative(sgg, h, 0)
    sgg = scatter_hp(jnp.split(sgg, 4, axis=0)).astype(BF)
    sdg = scatter_hp(jnp.split(relative(sdg[: 4 * units], h, 0), 4, axis=0)).astype(BF)
    sgg = lax.all_gather(sgg, "ep", axis=0, tiled=False)
    sdg = lax.all_gather(sdg, "ep", axis=0, tiled=True)

    def spread(v):
        v = v[:, :, : 4 * units].reshape(ep, width // 4, 4, units)
        return v.transpose(1, 2, 0, 3).reshape(width // 4, 4 * ep * units).astype(F32)

    sgate_grad, sup_grad = spread(sgg[:, :, :LANES]), spread(sgg[:, :, LANES:])
    sdown_grad = sdg.astype(F32)

    grad_out = cotangent.astype(F32)
    weight_back = dx_sum[:, width : width + total] + dx_sum[:, width + total : width + 2 * total]
    gate_back = weight_back * kept
    chosen_back = gates_of * (gate_back - jnp.sum(gates_of * gate_back, axis=1, keepdims=True))
    logits_back = chosen_back.astype(BF)
    router_part = dot(logits_back, second_in, (0, 0))
    second_back = dx_sum[:, :width] + dot(logits_back, router, (1, 1))
    to_middle, gain_two_part = norm_back(middle, inv_two, gain_two, second_back)
    middle_back = grad_out + to_middle
    attn_back = middle_back.astype(BF)
    counts_part = jnp.sum(kept, axis=0)
    tail = jnp.zeros((1, width - total), F32)
    sums = jnp.concatenate(
        [
            router_part,
            gain_two_part[None, :],
            jnp.concatenate([counts_part[None, :], tail], axis=1),
        ],
        axis=0,
    )
    sums = sum_all_small(sums)

    mixed_back = relative(dot(attn_back, o_w, (1, 1)).astype(BF), h, 1)
    out_part = dot(mixed_rel, attn_back, (0, 0))
    out_grad = sum_ep(scatter_hp(jnp.split(out_part, 4, axis=0)), e)
    dq, dka, dva, dkb, dvb = attend_back(h_arr, query, kv_a, kv_b, mixed_back, lse)
    dk = dka + swap_core(dkb).astype(F32)
    dv = dva + swap_core(dvb).astype(F32)
    query_raw = rotate_back(dq, rows).astype(BF)
    key_raw = rotate_back(dk, 2 * rows).astype(BF)
    value_raw = dv.astype(BF)
    kv_back = dot(key_raw, k_w, (1, 1)) + dot(value_raw, v_w, (1, 1))
    from_far = swap_y(kv_back[rows:].astype(BF))
    q_part = dot(first_in[:rows], query_raw, (0, 0))
    k_part = dot(first_in, key_raw, (0, 0))
    v_part = dot(first_in, value_raw, (0, 0))
    query_grad, key_grad, value_grad = (
        sum_ep(scatter_hp(jnp.split(v, 4, axis=0)), e) for v in (q_part, k_part, v_part)
    )
    first_back = dot(query_raw, q_w, (1, 1)) + kv_back[:rows]
    quarters = jnp.split(from_far.astype(F32), 4, axis=1)
    first_back = first_back + jnp.concatenate([quarters[i ^ 2] for i in range(4)], axis=1)
    to_tokens, gain_one_part = norm_back(both[:rows], inv_one[:rows], gain_one, first_back)
    tokens_grad = middle_back + relative(to_tokens, h, 1)
    gain_one_grad = sum_all_small(relative(gain_one_part[None, :], h, 1))[0]

    def own(v, n):
        return lax.dynamic_slice_in_dim(v, h * n, n, axis=0)

    return (
        layer,
        tokens_grad,
        own(gain_one_grad, width // 4),
        query_grad,
        key_grad,
        value_grad,
        out_grad,
        own(sums[total], width // 4),
        own(sums[:total].T, width // 4),
        sgate_grad,
        sup_grad,
        sdown_grad,
        gate_grad,
        up_grad,
        down_grad,
        own(sums[total + 1], total // 4).astype(jnp.int32),
    )


def solution(mesh):
    row, ep_hp = P("hp", None), P(("ep", "hp"), None)
    return jax.shard_map(
        per_device,
        mesh=mesh,
        in_specs=(
            ep_hp,
            P("hp"),
            row,
            row,
            row,
            row,
            P("hp"),
            row,
            row,
            row,
            row,
            P("ep", None, "hp"),
            P("ep", None, "hp"),
            P("ep", "hp", None),
            ep_hp,
            ep_hp,
            ep_hp,
        ),
        out_specs=(
            ep_hp,
            ep_hp,
            P("hp"),
            row,
            row,
            row,
            row,
            P("hp"),
            row,
            row,
            row,
            row,
            P("ep", None, "hp"),
            P("ep", None, "hp"),
            P("ep", "hp", None),
            P("hp"),
        ),
        check_vma=False,
    )
```

time: 2360 us -> 998 us (0.42)
  waiting for transfers between devices: 1310 us -> 403 us
  blocking collectives: 323 us -> 44.3 us
  matrix products: 308 us -> 77.1 us
  local copies, waits for them, and re-layouts: 296 us -> 139 us
  Pallas kernels: 0 us -> 149 us
  starting transfers between devices: 12.5 us -> 84.2 us
    unnamed x27 -> x1, waiting for transfers between devices: 678 us -> 0.02 us
    ppermute x0 -> x129, waiting for transfers between devices: none -> 403 us  [the longest x36 141 us: ring(): return lax.ppermute(v, 'ep', [(i, (i + 2) % n) for i in range(n)])]
    all_gather x11 -> x1, waiting for transfers between devices: 277 us -> 0.01 us  [per_device(): sgg = lax.all_gather(sgg, 'ep', axis=0, tiled=False)]
    all_to_all x2 -> x0, blocking collectives: 262 us -> none  [the longest x1 132 us: per_device(): lax.all_to_all(outgoing, 'ep', split_axis=0, concat_axis=0, tiled=True)]
    reduce_scatter x9 -> x0, waiting for transfers between devices: 231 us -> none  [the longest x1 41.5 us: per_device(): lax.psum_scatter(key_wpart.astype(jnp.bfloat16), 'hp', scatter_dimension=...]
    dot_general x39 -> x28, matrix products: 308 us -> 77.1 us  [the longest x16 39.8 us: dot(): lax.dot_general(left, right, (((over[0],), (over[1],)), ((), ())), prefer...]
    pallas_call x0 -> x10, Pallas kernels: none -> 149 us  [the longest x4 100 us: expert_stage(): pl.pallas_call(functools.partial(expert_kernel, capacity, total, olds), g...]
    psum x1 -> x0, waiting for transfers between devices: 114 us -> none  [per_device(): lax.psum(shares[0].astype(jnp.bfloat16), 'ep').astype(jnp.float32)]
  transfers between devices with their start and end apart: 26 -> 130, of which waited for: 21 -> 57; matrix products, arithmetic and copies ran while one was open for 20% -> 26% of each run, Pallas kernels for 0% -> 14%
where the time goes in v1:
time: 998 us; the launch traced here: 992 us
  waiting for transfers between devices  403 us (40%)
  Pallas kernels  149 us (15%)
  local copies, waits for them, and re-layouts  139 us (14%)
  starting transfers between devices  84.2 us (8%)
  other arithmetic  79.7 us (8%)
  matrix products  77.1 us (8%)
  blocking collectives  44.3 us (4%)
  between operations  16.2 us (2%)
    ppermute x36, waiting for transfers between devices, ring(): return lax.ppermute(v, 'ep', [(i, (i + 2) % n) for i in range(n)])  141 us
    ppermute x22, waiting for transfers between devices, swap_y(): return lax.ppermute(v, 'hp', [(i, i ^ 2) for i in range(4)])  125 us
    ppermute x24, waiting for transfers between devices, swap_pair(): return lax.ppermute(v, 'ep', [(i, i ^ 1) for i in range(n)])  108 us
    pallas_call x4, Pallas kernels, expert_stage(): pl.pallas_call(functools.partial(expert_kernel, capacity, total, olds), g...  100 us
    unnamed x234, local copies, waits for them, and re-layouts  53.1 us
    all_gather x1, blocking collectives, per_device(): sdg = lax.all_gather(sdg, 'ep', axis=0, tiled=True)  44.3 us
    dot_general x16, matrix products, dot(): lax.dot_general(left, right, (((over[0],), (over[1],)), ((), ())), prefer...  39.8 us
    dot_general x12, matrix products, expert_grad(): return jnp.einsum(spec, left, right, preferred_element_type=F32)  37.2 us
  transfers between devices with their start and end apart: 130, of which 57 were waited for; matrix products, arithmetic and copies ran while one was open for 26% of the time, Pallas kernels for 14%

profile of v1, /device:TPU:0, one launch (start us, length us, event | category | flops | bytes accessed | tf_op | source)
XLA Modules:
  0.0 992.0 jit_solution(13314513764696724505)
XLA Ops:
  62.8 9.1 collective-permute-done.8
  81.4 8.0 collective-permute-done.11
  115.2 9.5 shard_map.288
  141.6 24.4 %collective-permute-done.30 = bf16[2,1280,224]{1,2,0:T(8,128)(2,1)} collective-permute-done((bf16[2,1280,224]{1,2,0:T(8,128)(2,1)}, bf16[2,1280,224]{1,2,0:T(8,128)(2,1)}, u32[]{:S(2)}, u32[]{:S(2)}) %collective-permute-start.30) | collective-permute-done | bytes 1146912 | tf_op jit(solution)/shard_map/ppermute | solution.py:30
  177.0 13.2 %collective-permute-done.33.refs_10_.refs_2_ = bf16[2,224,1280]{2,1,0:T(8,128)(2,1)} collective-permute-done((bf16[2,224,1280]{2,1,0:T(8,128)(2,1)}, bf16[2,224,1280]{2,1,0:T(8,128)(2,1)}, u32[]{:S(2)}, u32[]{:S(2)}) %collective-permute-start.33) | collective-permute-done | bytes 1146912 | tf_op jit(solution)/shard_map/ppermute | solution.py:30
  216.5 24.7 %shard_map.289 = (bf16[256,1408]{1,0:T(8,128)(2,1)}, bf16[256,1408]{1,0:T(8,128)(2,1)}, f32[1280,256]{1,0:T(8,128)}, f32[128,1280]{1,0:T(8,128)}, bf16[4,512,128...) custom-call(s32[1]{0:T(128)} %bitcast.10.e_ref, ...), custom_call_target="tpu_custom_call" | custom-call | flops 6606028800 | bytes 25165824 | tf_op jit(solution)/shard_map/pallas_call | solution.py:396
  241.3 25.2 %shard_map.290 = (bf16[256,1408]{1,0:T(8,128)(2,1)}, bf16[256,1408]{1,0:T(8,128)(2,1)}, f32[1280,256]{1,0:T(8,128)}, f32[128,1280]{1,0:T(8,128)}, bf16[4,512,128...) custom-call(s32[1]{0:T(128)} %bitcast.10.e_ref, ...), custom_call_target="tpu_custom_call", output_to_operand_aliasing={{4}: (22, {}), {5}: (23, {}), {6}: (24, {}), {7}: (25, {}),... | custom-call | flops 6606028800 | bytes 25165824 | tf_op jit(solution)/shard_map/pallas_call | solution.py:396
  273.0 12.8 %collective-permute-done.53 = bf16[256,1408]{1,0:T(8,128)(2,1)S(1)} collective-permute-done((bf16[256,1408]{1,0:T(8,128)(2,1)}, bf16[256,1408]{1,0:T(8,128)(2,1)S(1)}, u32[]{:S(2)}, u32[]{:S(2)}) %collective-permute-start.53) | collective-permute-done | bytes 720928 | tf_op jit(solution)/shard_map/ppermute | solution.py:35
  289.3 12.1 %collective-permute-done.39.g1_ref = bf16[256,1408]{1,0:T(8,128)(2,1)} collective-permute-done((bf16[256,1408]{1,0:T(8,128)(2,1)}, bf16[256,1408]{1,0:T(8,128)(2,1)}, u32[]{:S(2)}, u32[]{:S(2)}) %collective-permute-start.39) | collective-permute-done | bytes 720928 | tf_op jit(solution)/shard_map/ppermute | solution.py:35
  301.4 13.9 %collective-permute-done.38.x1_ref = bf16[256,1408]{1,0:T(8,128)(2,1)} collective-permute-done((bf16[256,1408]{1,0:T(8,128)(2,1)}, bf16[256,1408]{1,0:T(8,128)(2,1)}, u32[]{:S(2)}, u32[]{:S(2)}) %collective-permute-start.38) | collective-permute-done | bytes 720928 | tf_op jit(solution)/shard_map/ppermute | solution.py:35
  315.3 24.9 %shard_map.291 = (bf16[256,1408]{1,0:T(8,128)(2,1)}, bf16[256,1408]{1,0:T(8,128)(2,1)}, f32[1280,256]{1,0:T(8,128)}, f32[128,1280]{1,0:T(8,128)}, bf16[4,512,128...) custom-call(s32[1]{0:T(128)} %bitcast.10.e_ref, ...), custom_call_target="tpu_custom_call", output_to_operand_aliasing={{4}: (22, {}), {5}: (23, {}), {6}: (24, {}), {7}: (25, {}),... | custom-call | flops 6606028800 | bytes 25165824 | tf_op jit(solution)/shard_map/pallas_call | solution.py:396
  347.9 11.7 %collective-permute-done.52 = bf16[256,1408]{1,0:T(8,128)(2,1)} collective-permute-done((bf16[256,1408]{1,0:T(8,128)(2,1)}, bf16[256,1408]{1,0:T(8,128)(2,1)}, u32[]{:S(2)}, u32[]{:S(2)}) %collective-permute-start.52) | collective-permute-done | bytes 720928 | tf_op jit(solution)/shard_map/ppermute | solution.py:35
  363.7 11.4 %collective-permute-done.25.g1_ref = bf16[256,1408]{1,0:T(8,128)(2,1)} collective-permute-done((bf16[256,1408]{1,0:T(8,128)(2,1)}, bf16[256,1408]{1,0:T(8,128)(2,1)}, u32[]{:S(2)}, u32[]{:S(2)}) %collective-permute-start.25) | collective-permute-done | bytes 720928 | tf_op jit(solution)/shard_map/ppermute | solution.py:35
  375.1 15.4 %collective-permute-done.21.x1_ref = bf16[256,1408]{1,0:T(8,128)(2,1)} collective-permute-done((bf16[256,1408]{1,0:T(8,128)(2,1)}, bf16[256,1408]{1,0:T(8,128)(2,1)}, u32[]{:S(2)}, u32[]{:S(2)}) %collective-permute-start.21) | collective-permute-done | bytes 720928 | tf_op jit(solution)/shard_map/ppermute | solution.py:35
  390.5 25.3 %shard_map.292 = (bf16[256,1408]{1,0:T(8,128)(2,1)}, bf16[256,1408]{1,0:T(8,128)(2,1)}, f32[1280,256]{1,0:T(8,128)}, f32[128,1280]{1,0:T(8,128)}, bf16[4,512,128...) custom-call(s32[1]{0:T(128)} %bitcast.10.e_ref, ...), custom_call_target="tpu_custom_call", output_to_operand_aliasing={{4}: (22, {}), {5}: (23, {}), {6}: (24, {}), {7}: (25, {}),... | custom-call | flops 6606028800 | bytes 25165824 | tf_op jit(solution)/shard_map/pallas_call | solution.py:396
  445.7 6.6 shard_map.296
  460.6 6.5 shard_map.294
  476.4 44.3 %all-gather.1 = bf16[8,28,1280]{2,1,0:T(8,128)(2,1)} all-gather(bf16[1,28,1280]{2,1,0:T(8,128)(2,1)S(1)} %fusion.81), channel_id=1, replica_groups=mesh['ep'=8,'hp'=4] {'ep'}, dimensions={0}, use_global_device_ids=true | all-gather | bytes 645120 | tf_op jit(solution)/shard_map/all_gather | solution.py:615
  534.1 22.1 %collective-permute-done.56 = bf16[256,1408]{1,0:T(8,128)(2,1)} collective-permute-done((bf16[256,1408]{1,0:T(8,128)(2,1)}, bf16[256,1408]{1,0:T(8,128)(2,1)}, u32[]{:S(2)}, u32[]{:S(2)}) %collective-permute-start.56) | collective-permute-done | bytes 720928 | tf_op jit(solution)/shard_map/ppermute | solution.py:40
  577.0 15.1 %collective-permute-done.111 = f32[18,1280]{1,0:T(8,128)S(1)} collective-permute-done((f32[18,1280]{1,0:T(8,128)S(1)}, f32[18,1280]{1,0:T(8,128)S(1)}, u32[]{:S(2)}, u32[]{:S(2)}) %collective-permute-start.111) | collective-permute-done | bytes 92192 | tf_op jit(solution)/shard_map/ppermute | solution.py:118
  610.2 15.7 %collective-permute-done.48 = bf16[256,1280]{1,0:T(8,128)(2,1)S(1)} collective-permute-done((bf16[256,1280]{1,0:T(8,128)(2,1)S(1)}, bf16[256,1280]{1,0:T(8,128)(2,1)S(1)}, u32[]{:S(2)}, u32[]{:S(2)}) %collective-permute-start.48) | collective-permute-done | bytes 655392 | tf_op jit(solution)/shard_map/ppermute | solution.py:40
  633.3 21.1 %collective-permute-done.125 = bf16[2,1280,224]{1,2,0:T(8,128)(2,1)} collective-permute-done((bf16[2,1280,224]{1,2,0:T(8,128)(2,1)}, bf16[2,1280,224]{1,2,0:T(8,128)(2,1)}, u32[]{:S(2)}, u32[]{:S(2)}) %collective-permute-start.125) | collective-permute-done | bytes 1146912 | tf_op jit(solution)/shard_map/ppermute | solution.py:30
  658.9 17.6 %collective-permute-done.128 = bf16[2,224,1280]{2,1,0:T(8,128)(2,1)S(1)} collective-permute-done((bf16[2,224,1280]{2,1,0:T(8,128)(2,1)S(1)}, bf16[2,224,1280]{2,1,0:T(8,128)(2,1)S(1)}, u32[]{:S(2)}, u32[]{:S(2)}) %collective-permute-start.128) | collective-permute-done | bytes 1146912 | tf_op jit(solution)/shard_map/ppermute | solution.py:30
  705.5 14.6 %shard_map.297 = (f32[256,1280]{1,0:T(8,128)S(1)}, f32[512,1280]{1,0:T(8,128)S(1)}, f32[512,1280]{1,0:T(8,128)S(1)}, bf16[512,1280]{1,0:T(8,128)(2,1)}, bf16[512,1280]{1,0:T(8,128)(2,1)S(1)}) custom-call(s32[1]{0:T(128)} %bitcast.h_ref, bf16[256,1280]{1,0:T(8,128)(2,1)S(1)} %fusion.26.q_ref, bf16[512,2560]{1,0:T(8,128)(2,1)S(1)} %pad_maximum_fusion.ka_ref.va_ref, ...), custom_call_target="tpu_custom_call" | custom-call | flops 3355443200 | bytes 16777216 | tf_op jit(solution)/shard_map/pallas_call | solution.py:220
  776.7 9.1 collective-permute-done.100
  790.5 8.4 collective-permute-done.59
  825.3 9.0 collective-permute-done.101
  855.9 6.8 collective-permute-done.71
  862.8 7.1 collective-permute-done.104
  876.3 6.4 collective-permute-done.105
  882.8 6.4 collective-permute-done.73
  889.2 6.9 collective-permute-done.106
  (713 shorter events, 510.5 us)
Async XLA Ops:
  7.2 672.6 %all-gather.4.cloned.1.call-start = ((), (), s32[]{:S(2)}) async-start(), calls=%async_computation | async-start | bytes 1474560 | tf_op jit(solution)/shard_map/all_gather | solution.py:614
  7.2 66.8 %collective-permute-start.4 = (bf16[320,1280]{1,0:T(8,128)(2,1)}, bf16[320,1280]{1,0:T(8,128)(2,1)}, u32[]{:S(2)}, u32[]{:S(2)}) collective-permute-start(bf16[320,1280]{1,0:T(8,128)(2,1)} %param.19), channel_id=1, source_target_pairs={{0,1},{1,0},{2,3},{3,2},{4,5},{5,4},{6,7},{7,6},{8,9},{9,8},{10,11... | collective-permute-start | bytes 2457608 | tf_op jit(solution)/shard_map/ppermute | solution.py:26
  7.8 68.0 %collective-permute-start.5 = (bf16[320,1280]{1,0:T(8,128)(2,1)}, bf16[320,1280]{1,0:T(8,128)(2,1)}, u32[]{:S(2)}, u32[]{:S(2)}) collective-permute-start(bf16[320,1280]{1,0:T(8,128)(2,1)} %param.19), channel_id=1, source_target_pairs={{0,2},{1,3},{2,0},{3,1},{4,6},{5,7},{6,4},{7,5},{8,10},{9,11},{10,... | collective-permute-start | bytes 2457608 | tf_op jit(solution)/shard_map/ppermute | solution.py:30
  77.5 48.4 %collective-permute-start.35 = (bf16[28,1280]{1,0:T(8,128)(2,1)}, bf16[28,1280]{1,0:T(8,128)(2,1)S(1)}, u32[]{:S(2)}, u32[]{:S(2)}) collective-permute-start(bf16[28,1280]{1,0:T(8,128)(2,1)} %constant_dynamic-slice_fusion.3), channel_id=1, source_target_pairs={{0,2},{1,3},{2,0},{3,1},{4,6},{5,7},{6,4},{7,5},{8,10},{9,11},{10,... | collective-permute-start | bytes 215048 | tf_op jit(solution)/shard_map/ppermute | solution.py:30
  134.6 55.6 %collective-permute-start.33 = (bf16[2,224,1280]{2,1,0:T(8,128)(2,1)}, bf16[2,224,1280]{2,1,0:T(8,128)(2,1)}, u32[]{:S(2)}, u32[]{:S(2)}) collective-permute-start(bf16[2,224,1280]{2,1,0:T(8,128)(2,1)} %refs_0_.11), channel_id=1, source_target_pairs={{0,2},{1,3},{2,0},{3,1},{4,6},{5,7},{6,4},{7,5},{8,10},{9,11},{10,... | collective-permute-start | bytes 3440648 | tf_op jit(solution)/shard_map/ppermute | solution.py:30
  141.4 49.9 %collective-permute-start.28 = (bf16[2,1280,224]{1,2,0:T(8,128)(2,1)}, bf16[2,1280,224]{1,2,0:T(8,128)(2,1)}, u32[]{:S(2)}, u32[]{:S(2)}) collective-permute-start(bf16[2,1280,224]{1,2,0:T(8,128)(2,1)} %collective-permute-done.27), channel_id=1, source_target_pairs={{0,1},{1,0},{2,3},{3,2},{4,5},{5,4},{6,7},{7,6},{8,9},{9,8},{10,11... | collective-permute-start | bytes 3440648 | tf_op jit(solution)/shard_map/ppermute | solution.py:26
  193.6 47.6 %collective-permute-start.41 = (bf16[256,1408]{1,0:T(8,128)(2,1)}, bf16[256,1408]{1,0:T(8,128)(2,1)}, u32[]{:S(2)}, u32[]{:S(2)}) collective-permute-start(bf16[256,1408]{1,0:T(8,128)(2,1)} %collective-permute-done.22.g0_ref), channel_id=1, source_target_pairs={{0,4},{4,0},{8,12},{12,8},{16,20},{20,16},{24,28},{28,24},{1,5},{5... | collective-permute-start | bytes 2162696 | tf_op jit(solution)/shard_map/ppermute | solution.py:35
  194.2 47.1 %collective-permute-start.40 = (bf16[256,1408]{1,0:T(8,128)(2,1)}, bf16[256,1408]{1,0:T(8,128)(2,1)}, u32[]{:S(2)}, u32[]{:S(2)}) collective-permute-start(bf16[256,1408]{1,0:T(8,128)(2,1)} %collective-permute-done.18.x0_ref), channel_id=1, source_target_pairs={{0,4},{4,0},{8,12},{12,8},{16,20},{20,16},{24,28},{28,24},{1,5},{5... | collective-permute-start | bytes 2162696 | tf_op jit(solution)/shard_map/ppermute | solution.py:35
  210.9 56.9 %collective-permute-start.23 = (bf16[256,1408]{1,0:T(8,128)(2,1)}, bf16[256,1408]{1,0:T(8,128)(2,1)}, u32[]{:S(2)}, u32[]{:S(2)}) collective-permute-start(bf16[256,1408]{1,0:T(8,128)(2,1)} %collective-permute-done.22.g0_ref), channel_id=1, source_target_pairs={{0,8},{4,12},{8,16},{12,20},{16,24},{20,28},{24,0},{28,4},{1,9},{5... | collective-permute-start | bytes 2162696 | tf_op jit(solution)/shard_map/ppermute | solution.py:40
  212.5 56.1 %collective-permute-start.19 = (bf16[256,1408]{1,0:T(8,128)(2,1)}, bf16[256,1408]{1,0:T(8,128)(2,1)}, u32[]{:S(2)}, u32[]{:S(2)}) collective-permute-start(bf16[256,1408]{1,0:T(8,128)(2,1)} %collective-permute-done.18.x0_ref), channel_id=1, source_target_pairs={{0,8},{4,12},{8,16},{12,20},{16,24},{20,28},{24,0},{28,4},{1,9},{5... | collective-permute-start | bytes 2162696 | tf_op jit(solution)/shard_map/ppermute | solution.py:40
  268.6 46.7 %collective-permute-start.38 = (bf16[256,1408]{1,0:T(8,128)(2,1)}, bf16[256,1408]{1,0:T(8,128)(2,1)}, u32[]{:S(2)}, u32[]{:S(2)}) collective-permute-start(bf16[256,1408]{1,0:T(8,128)(2,1)} %collective-permute-done.19.x0_ref), channel_id=1, source_target_pairs={{0,4},{4,0},{8,12},{12,8},{16,20},{20,16},{24,28},{28,24},{1,5},{5... | collective-permute-start | bytes 2162696 | tf_op jit(solution)/shard_map/ppermute | solution.py:35
  269.9 71.9 %collective-permute-start.24 = (bf16[256,1408]{1,0:T(8,128)(2,1)}, bf16[256,1408]{1,0:T(8,128)(2,1)}, u32[]{:S(2)}, u32[]{:S(2)}) collective-permute-start(bf16[256,1408]{1,0:T(8,128)(2,1)} %collective-permute-done.23.g0_ref), channel_id=1, source_target_pairs={{0,8},{4,12},{8,16},{12,20},{16,24},{20,28},{24,0},{28,4},{1,9},{5... | collective-permute-start | bytes 2162696 | tf_op jit(solution)/shard_map/ppermute | solution.py:40
  271.4 70.9 %collective-permute-start.20 = (bf16[256,1408]{1,0:T(8,128)(2,1)}, bf16[256,1408]{1,0:T(8,128)(2,1)}, u32[]{:S(2)}, u32[]{:S(2)}) collective-permute-start(bf16[256,1408]{1,0:T(8,128)(2,1)} %collective-permute-done.19.x0_ref), channel_id=1, source_target_pairs={{0,8},{4,12},{8,16},{12,20},{16,24},{20,28},{24,0},{28,4},{1,9},{5... | collective-permute-start | bytes 2162696 | tf_op jit(solution)/shard_map/ppermute | solution.py:40
  287.9 60.0 %collective-permute-start.54 = (bf16[256,1408]{1,0:T(8,128)(2,1)}, bf16[256,1408]{1,0:T(8,128)(2,1)}, u32[]{:S(2)}, u32[]{:S(2)}) collective-permute-start(bf16[256,1408]{1,0:T(8,128)(2,1)} %add_convert_fusion.3), channel_id=1, source_target_pairs={{0,8},{4,12},{8,16},{12,20},{16,24},{20,28},{24,0},{28,4},{1,9},{5... | collective-permute-start | bytes 2162696 | tf_op jit(solution)/shard_map/ppermute | solution.py:40
  342.3 48.3 %collective-permute-start.21 = (bf16[256,1408]{1,0:T(8,128)(2,1)}, bf16[256,1408]{1,0:T(8,128)(2,1)}, u32[]{:S(2)}, u32[]{:S(2)}) collective-permute-start(bf16[256,1408]{1,0:T(8,128)(2,1)} %collective-permute-done.20.x0_ref), channel_id=1, source_target_pairs={{0,4},{4,0},{8,12},{12,8},{16,20},{20,16},{24,28},{28,24},{1,5},{5... | collective-permute-start | bytes 2162696 | tf_op jit(solution)/shard_map/ppermute | solution.py:35
  347.4 186.3 %collective-permute-start.50 = (bf16[256,1408]{1,0:T(8,128)(2,1)}, bf16[256,1408]{1,0:T(8,128)(2,1)}, u32[]{:S(2)}, u32[]{:S(2)}) collective-permute-start(bf16[256,1408]{1,0:T(8,128)(2,1)} %get-tuple-element.107), channel_id=1, source_target_pairs={{0,4},{4,0},{8,12},{12,8},{16,20},{20,16},{24,28},{28,24},{1,5},{5... | collective-permute-start | bytes 2162696 | tf_op jit(solution)/shard_map/ppermute | solution.py:35
  362.1 162.4 %collective-permute-start.55 = (bf16[256,1408]{1,0:T(8,128)(2,1)}, bf16[256,1408]{1,0:T(8,128)(2,1)}, u32[]{:S(2)}, u32[]{:S(2)}) collective-permute-start(bf16[256,1408]{1,0:T(8,128)(2,1)} %add_convert_fusion.2), channel_id=1, source_target_pairs={{0,8},{4,12},{8,16},{12,20},{16,24},{20,28},{24,0},{28,4},{1,9},{5... | collective-permute-start | bytes 2162696 | tf_op jit(solution)/shard_map/ppermute | solution.py:40
  415.8 108.7 %collective-permute-start.51 = (bf16[256,1408]{1,0:T(8,128)(2,1)}, bf16[256,1408]{1,0:T(8,128)(2,1)}, u32[]{:S(2)}, u32[]{:S(2)}) collective-permute-start(bf16[256,1408]{1,0:T(8,128)(2,1)} %get-tuple-element.109), channel_id=1, source_target_pairs={{0,4},{4,0},{8,12},{12,8},{16,20},{20,16},{24,28},{28,24},{1,5},{5... | collective-permute-start | bytes 2162696 | tf_op jit(solution)/shard_map/ppermute | solution.py:35
  420.9 54.9 %collective-permute-start.117 = (bf16[28,1280]{1,0:T(8,128)(2,1)S(1)}, bf16[28,1280]{1,0:T(8,128)(2,1)S(1)}, u32[]{:S(2)}, u32[]{:S(2)}) collective-permute-start(bf16[28,1280]{1,0:T(8,128)(2,1)S(1)} %get-tuple-element.252), channel_id=1, source_target_pairs={{0,1},{1,0},{2,3},{3,2},{4,5},{5,4},{6,7},{7,6},{8,9},{9,8},{10,11... | collective-permute-start | bytes 215048 | tf_op jit(solution)/shard_map/ppermute | solution.py:26
  475.8 56.2 %collective-permute-start.46 = (bf16[256,1280]{1,0:T(8,128)(2,1)}, bf16[256,1280]{1,0:T(8,128)(2,1)}, u32[]{:S(2)}, u32[]{:S(2)}) collective-permute-start(bf16[256,1280]{1,0:T(8,128)(2,1)} %get-tuple-element.105), channel_id=1, source_target_pairs={{0,4},{4,0},{8,12},{12,8},{16,20},{20,16},{24,28},{28,24},{1,5},{5... | collective-permute-start | bytes 1966088 | tf_op jit(solution)/shard_map/ppermute | solution.py:35
  476.3 46.5 %collective-permute-start.115 = (bf16[320,256]{1,0:T(8,128)(2,1)}, bf16[320,256]{1,0:T(8,128)(2,1)}, u32[]{:S(2)}, u32[]{:S(2)}) collective-permute-start(bf16[320,256]{1,0:T(8,128)(2,1)} %get-tuple-element.219), channel_id=1, source_target_pairs={{0,1},{1,0},{2,3},{3,2},{4,5},{5,4},{6,7},{7,6},{8,9},{9,8},{10,11... | collective-permute-start | bytes 491528 | tf_op jit(solution)/shard_map/ppermute | solution.py:26
  522.9 69.2 %collective-permute-start.45 = (bf16[256,1280]{1,0:T(8,128)(2,1)}, bf16[256,1280]{1,0:T(8,128)(2,1)}, u32[]{:S(2)}, u32[]{:S(2)}) collective-permute-start(bf16[256,1280]{1,0:T(8,128)(2,1)} %copy-done.18), channel_id=1, source_target_pairs={{0,4},{4,0},{8,12},{12,8},{16,20},{20,16},{24,28},{28,24},{1,5},{5... | collective-permute-start | bytes 1966088 | tf_op jit(solution)/shard_map/ppermute | solution.py:35
  528.6 81.5 %collective-permute-start.44 = (bf16[256,1280]{1,0:T(8,128)(2,1)}, bf16[256,1280]{1,0:T(8,128)(2,1)}, u32[]{:S(2)}, u32[]{:S(2)}) collective-permute-start(bf16[256,1280]{1,0:T(8,128)(2,1)} %get-tuple-element.101), channel_id=1, source_target_pairs={{0,4},{4,0},{8,12},{12,8},{16,20},{20,16},{24,28},{28,24},{1,5},{5... | collective-permute-start | bytes 1966088 | tf_op jit(solution)/shard_map/ppermute | solution.py:35
  573.1 121.8 %collective-permute-start.43 = (bf16[256,1280]{1,0:T(8,128)(2,1)}, bf16[256,1280]{1,0:T(8,128)(2,1)}, u32[]{:S(2)}, u32[]{:S(2)}) collective-permute-start(bf16[256,1280]{1,0:T(8,128)(2,1)} %get-tuple-element.99), channel_id=1, source_target_pairs={{0,4},{4,0},{8,12},{12,8},{16,20},{20,16},{24,28},{28,24},{1,5},{5... | collective-permute-start | bytes 1966088 | tf_op jit(solution)/shard_map/ppermute | solution.py:35
  628.5 48.1 %collective-permute-start.128 = (bf16[2,224,1280]{2,1,0:T(8,128)(2,1)S(1)}, bf16[2,224,1280]{2,1,0:T(8,128)(2,1)S(1)}, u32[]{:S(2)}, u32[]{:S(2)}) collective-permute-start(bf16[2,224,1280]{2,1,0:T(8,128)(2,1)S(1)} %fusion.5), channel_id=1, source_target_pairs={{0,2},{1,3},{2,0},{3,1},{4,6},{5,7},{6,4},{7,5},{8,10},{9,11},{10,... | collective-permute-start | bytes 3440648 | tf_op jit(solution)/shard_map/ppermute | solution.py:30
  633.3 61.6 %collective-permute-start.49 = (bf16[256,1280]{1,0:T(8,128)(2,1)}, bf16[256,1280]{1,0:T(8,128)(2,1)}, u32[]{:S(2)}, u32[]{:S(2)}) collective-permute-start(bf16[256,1280]{1,0:T(8,128)(2,1)} %add_convert_fusion.5), channel_id=1, source_target_pairs={{0,8},{4,12},{8,16},{12,20},{16,24},{20,28},{24,0},{28,4},{1,9},{5... | collective-permute-start | bytes 1966088 | tf_op jit(solution)/shard_map/ppermute | solution.py:40
  773.6 62.8 %collective-permute-start.77 = (bf16[320,1280]{1,0:T(8,128)(2,1)}, bf16[320,1280]{1,0:T(8,128)(2,1)}, u32[]{:S(2)}, u32[]{:S(2)}) collective-permute-start(bf16[320,1280]{1,0:T(8,128)(2,1)} %get-tuple-element.205), channel_id=1, source_target_pairs={{0,1},{1,0},{2,3},{3,2},{4,5},{5,4},{6,7},{7,6},{8,9},{9,8},{10,11... | collective-permute-start | bytes 2457608 | tf_op jit(solution)/shard_map/ppermute | solution.py:26
  773.6 137.2 %collective-permute-start.76 = (bf16[320,1280]{1,0:T(8,128)(2,1)}, bf16[320,1280]{1,0:T(8,128)(2,1)}, u32[]{:S(2)}, u32[]{:S(2)}) collective-permute-start(bf16[320,1280]{1,0:T(8,128)(2,1)} %get-tuple-element.204), channel_id=1, source_target_pairs={{0,1},{1,0},{2,3},{3,2},{4,5},{5,4},{6,7},{7,6},{8,9},{9,8},{10,11... | collective-permute-start | bytes 2457608 | tf_op jit(solution)/shard_map/ppermute | solution.py:26
  776.7 62.0 %collective-permute-start.88 = (bf16[320,1280]{1,0:T(8,128)(2,1)}, bf16[320,1280]{1,0:T(8,128)(2,1)}, u32[]{:S(2)}, u32[]{:S(2)}) collective-permute-start(bf16[320,1280]{1,0:T(8,128)(2,1)} %get-tuple-element.203), channel_id=1, source_target_pairs={{0,1},{1,0},{2,3},{3,2},{4,5},{5,4},{6,7},{7,6},{8,9},{9,8},{10,11... | collective-permute-start | bytes 2457608 | tf_op jit(solution)/shard_map/ppermute | solution.py:26
  821.5 93.0 %collective-permute-start.87 = (bf16[320,1280]{1,0:T(8,128)(2,1)}, bf16[320,1280]{1,0:T(8,128)(2,1)S(1)}, u32[]{:S(2)}, u32[]{:S(2)}) collective-permute-start(bf16[320,1280]{1,0:T(8,128)(2,1)} %get-tuple-element.202), channel_id=1, source_target_pairs={{0,1},{1,0},{2,3},{3,2},{4,5},{5,4},{6,7},{7,6},{8,9},{9,8},{10,11... | collective-permute-start | bytes 2457608 | tf_op jit(solution)/shard_map/ppermute | solution.py:26
  838.6 72.6 %collective-permute-start.78 = (bf16[320,1280]{1,0:T(8,128)(2,1)S(1)}, bf16[320,1280]{1,0:T(8,128)(2,1)S(1)}, u32[]{:S(2)}, u32[]{:S(2)}) collective-permute-start(bf16[320,1280]{1,0:T(8,128)(2,1)S(1)} %fusion.19), channel_id=1, source_target_pairs={{0,2},{1,3},{2,0},{3,1},{4,6},{5,7},{6,4},{7,5},{8,10},{9,11},{10,... | collective-permute-start | bytes 2457608 | tf_op jit(solution)/shard_map/ppermute | solution.py:30
  841.2 73.3 %collective-permute-start.89 = (bf16[320,1280]{1,0:T(8,128)(2,1)S(1)}, bf16[320,1280]{1,0:T(8,128)(2,1)S(1)}, u32[]{:S(2)}, u32[]{:S(2)}) collective-permute-start(bf16[320,1280]{1,0:T(8,128)(2,1)S(1)} %fusion.17), channel_id=1, source_target_pairs={{0,2},{1,3},{2,0},{3,1},{4,6},{5,7},{6,4},{7,5},{8,10},{9,11},{10,... | collective-permute-start | bytes 2457608 | tf_op jit(solution)/shard_map/ppermute | solution.py:30
  (205 other events, 2891.9 us)
Sparse Core Ops, SparseCore 0:
  532.1 50.9 all-gather.3

commit v2 on v1

--- a/solution.py
+++ b/solution.py
@@ -40,14 +40,23 @@
     return lax.ppermute(v, "ep", [(i, (i + 2) % n) for i in range(n)])
 
 
+def shift(v, steps):
+    n = lax.axis_size("ep")
+    return lax.ppermute(v, "ep", [(i, (i + 2 * steps) % n) for i in range(n)])
+
+
+def after(v, *others):
+    return lax.optimization_barrier((v, others))[0]
+
+
 def gather_hp(v):
     far = swap_y(v)
     return [v, swap_core(v), far, swap_core(far)]
 
 
 def scatter_hp(parts):
-    near = swap_core(parts[1].astype(BF)).astype(F32) + parts[0]
-    over = swap_core(parts[3].astype(BF)).astype(F32) + parts[2]
+    near = swap_core(parts[1].astype(BF)).astype(F32) + parts[0].astype(F32)
+    over = swap_core(parts[3].astype(BF)).astype(F32) + parts[2].astype(F32)
     return near + swap_y(over.astype(BF)).astype(F32)
 
 
@@ -80,6 +89,20 @@
     return total
 
 
+def spread_ep(v, e):
+    n = lax.axis_size("ep")
+    stages = n // 2
+    x, z = e & 1, e >> 1
+    column = lax.dynamic_update_index_in_dim(jnp.zeros((stages,) + v.shape, v.dtype), v, z, 0)
+    for step in range(1, stages):
+        column = lax.dynamic_update_index_in_dim(
+            column, shift(v, step), (z + stages - step) % stages, 0
+        )
+    far = swap_pair(column)
+    both = [jnp.where(x == 0, column, far), jnp.where(x == 0, far, column)]
+    return jnp.stack(both, axis=1).reshape((n,) + v.shape)
+
+
 def sum_ep(v, e):
     n = lax.axis_size("ep")
     stages = n // 2
@@ -89,19 +112,17 @@
     other = lax.dynamic_index_in_dim(halves, 1 - x, 0, False)
     mine = mine + swap_pair(other.astype(BF)).astype(F32)
     chunks = mine.reshape(stages, mine.shape[0] // stages, mine.shape[1])
-
-    def chunk(back):
-        return lax.dynamic_index_in_dim(chunks, (z + stages - back) % stages, 0, False)
-
-    total = chunk(1 % stages)
-    for back in list(range(2, stages)) + [0]:
-        total = ring(total.astype(BF)).astype(F32) + chunk(back)
+    low = chunks.astype(BF)
+    total = lax.dynamic_index_in_dim(chunks, z, 0, False)
+    for step in range(1, stages):
+        part = lax.dynamic_index_in_dim(low, (z + step) % stages, 0, False)
+        total = total + shift(part, step).astype(F32)
     total = total.astype(BF)
-    half = jnp.zeros(chunks.shape, BF)
-    for back in range(stages):
-        half = lax.dynamic_update_index_in_dim(half, total, (z + stages - back) % stages, 0)
-        if back < stages - 1:
-            total = ring(total)
+    half = lax.dynamic_update_index_in_dim(jnp.zeros(chunks.shape, BF), total, z, 0)
+    for step in range(1, stages):
+        half = lax.dynamic_update_index_in_dim(
+            half, shift(total, step), (z + stages - step) % stages, 0
+        )
     half = half.reshape(mine.shape)
     far = swap_pair(half)
     low = jnp.where(x == 0, half, far)
@@ -437,6 +458,276 @@
     )(e, *g_pair, wa, sa, *downs, sd)
 
 
+def dispatch_kernel(capacity, total, x_ref, g_ref, *refs):
+    gates, ups, downs = refs[0:4], refs[4:8], refs[8:12]
+    sg_ref, su_ref, sd_ref = refs[12:15]
+    dx_ref, out_ref, sgg_ref, sdg_ref, xr_ref, gr_ref, gu_ref, wa_ref = refs[15:23]
+    xbuf, sbuf, tbuf, wgu, wd, bounce = refs[23:29]
+    rx_s, rx_r, sx_s, sx_r, sr_s, sr_r, rt_s, rt_r, w_sem, d_sem = refs[29:]
+    k = pl.program_id(0)
+    stages = xbuf.shape[0]
+    tokens, width = x_ref.shape[0], sg_ref.shape[0]
+    hidden = gates[0].shape[2]
+    wide = wd.shape[1] // 4
+    c = capacity
+    e, h = lax.axis_index("ep"), lax.axis_index("hp")
+    n = 2 * stages
+    right, left = lax.rem(e + 2, n), lax.rem(e + n - 2, n)
+    pair = e + 1 - 2 * lax.rem(e, 2)
+
+    def send(src, dst, s, r, i, where):
+        return pltpu.make_async_remote_copy(
+            src_ref=src,
+            dst_ref=dst,
+            send_sem=s.at[i],
+            recv_sem=r.at[i],
+            device_id=(where, h),
+            device_id_type=pl.DeviceIdType.MESH,
+        )
+
+    def ring_x(i):
+        return send(xbuf.at[i, 0], xbuf.at[i + 1, 0], rx_s, rx_r, i, right)
+
+    def swap_x(i):
+        return send(xbuf.at[i, 0], xbuf.at[i, 1], sx_s, sx_r, i, pair)
+
+    def swap_r(i):
+        return send(xbuf.at[i, 1], sbuf.at[i], sr_s, sr_r, i, pair)
+
+    def ring_t(i):
+        return send(xbuf.at[i, 0], tbuf.at[i], rt_s, rt_r, i, right)
+
+    @pl.when(k == 0)
+    def _():
+        barrier = pltpu.get_barrier_semaphore()
+        for where in (right, left, pair):
+            pl.semaphore_signal(
+                barrier, inc=1, device_id=(where, h), device_id_type=pl.DeviceIdType.MESH
+            )
+        xbuf[0, 0] = x_ref[...]
+        pl.semaphore_wait(barrier, 3)
+        ring_x(0).start()
+        swap_x(0).start()
+        rest = wide - hidden
+        down_copies = []
+        for r in range(4):
+            for x in range(2):
+                copy = pltpu.make_async_copy(
+                    downs[r].at[x],
+                    wd.at[x, pl.ds(r * wide, hidden), :],
+                    d_sem.at[2 * r + x],
+                )
+                copy.start()
+                down_copies.append(copy)
+        todo = [
+            (v[r], x, 2 * r + i)
+            for x in range(2)
+            for r in range(4)
+            for i, v in enumerate((gates, ups))
+        ]
+        slots = bounce.shape[0]
+
+        def load(i):
+            ref, x, _ = todo[i]
+            return pltpu.make_async_copy(ref.at[x], bounce.at[i % slots], w_sem.at[i % slots])
+
+        for i in range(slots):
+            load(i).start()
+        for i, (_, x, at) in enumerate(todo):
+            load(i).wait()
+            wgu[x, :, at * wide : (at + 1) * wide] = jnp.concatenate(
+                [bounce[i % slots], jnp.zeros((width, rest), BF)], axis=1
+            )
+            if i + slots < len(todo):
+                load(i + slots).start()
+        for copy in down_copies:
+            copy.wait()
+        for r in range(4):
+            for x in range(2):
+                wd[x, r * wide + hidden : (r + 1) * wide, :] = jnp.zeros((rest, width), BF)
+        sgg_ref[...] = jnp.zeros_like(sgg_ref)
+        sdg_ref[...] = jnp.zeros_like(sdg_ref)
+
+    @pl.when(k < stages - 1)
+    def _():
+        ring_x(k).wait_recv()
+
+    @pl.when(k < stages - 2)
+    def _():
+        ring_x(k + 1).start()
+
+    @pl.when(k < stages - 1)
+    def _():
+        swap_x(k + 1).start()
+
+    swap_x(k).wait_recv()
+
+    x2 = jnp.concatenate([xbuf[k, j, :, :width] for j in range(2)], axis=0)
+    g2 = jnp.concatenate([g_ref[0, j, :, :width] for j in range(2)], axis=0)
+    hg, hu = dot(x2, sg_ref[...]), dot(x2, su_ref[...])
+    ab = dot(g2, sd_ref[...], (1, 1))
+    s = jax.nn.sigmoid(hg)
+    silu = hg * s
+    act = (silu * hu).astype(BF)
+    gi = (ab * hu * (s * (1.0 + hg * (1.0 - s)))).astype(BF)
+    ui = (ab * silu).astype(BF)
+    sgg_ref[...] += dot(x2, jnp.concatenate([gi, ui], axis=1), (0, 0))
+    sdg_ref[...] += dot(act, g2, (0, 0))
+    dx = dot(gi, sg_ref[...], (1, 1)) + dot(ui, su_ref[...], (1, 1))
+    totals = [dx[:tokens], dx[tokens:]]
+    out = dot(act, sd_ref[...])
+    outs = [out[:tokens], out[tokens:]]
+    metas = [0.0, 0.0]
+    lane = lax.broadcasted_iota(jnp.int32, (2 * c, LANES), 1)
+    for x in range(2):
+        col = 2 * e + x
+        picks, weights = [], []
+        for j in range(2):
+            pick = pick_matrix(g_ref[0, j, :, width:], col, c)
+            picks.append(pick)
+            rows = dot(pick, xbuf[k, j], (0, 0))
+            xr_ref[x, 0, j * c : (j + 1) * c, :] = rows[:, :width].astype(BF)
+            weights.append(rows[:, width:])
+            gr_ref[x, 0, j * c : (j + 1) * c, :] = dot(
+                pick, g_ref[0, j, :, :width], (0, 0)
+            ).astype(BF)
+        w = jnp.concatenate(weights, axis=0)
+        w = jnp.sum(jnp.where(lane == col, w, 0.0), axis=1, keepdims=True)
+        xr, gr = xr_ref[x, 0], gr_ref[x, 0]
+        wb = jnp.zeros((2 * c, 1), F32)
+        for r in range(4):
+            hgu = dot(xr, wgu[x, :, 2 * r * wide : 2 * (r + 1) * wide])
+            ab = dot(gr, wd[x, r * wide : (r + 1) * wide, :], (1, 1))
+            hg, hu = hgu[:, :wide], hgu[:, wide:]
+            s = jax.nn.sigmoid(hg)
+            silu = hg * s
+            act = silu * hu
+            wb = wb + jnp.sum(act * ab, axis=1, keepdims=True)
+            ab = ab * w
+            at = 2 * r * wide
+            gu_ref[x, 0, :, at : at + wide] = (ab * hu * (s * (1.0 + hg * (1.0 - s)))).astype(BF)
+            gu_ref[x, 0, :, at + wide : at + 2 * wide] = (ab * silu).astype(BF)
+            wa_ref[x, 0, :, r * wide : (r + 1) * wide] = (act * w).astype(BF)
+        dxr = dot(gu_ref[x, 0], wgu[x], (1, 1)).astype(BF)
+        rows = dot(wa_ref[x, 0], wd[x]).astype(BF)
+        high = wb.astype(BF).astype(F32)
+        meta = jnp.where(lane == col, high, 0.0) + jnp.where(lane == total + col, wb - high, 0.0)
+        meta = meta.astype(BF)
+        for j in range(2):
+            span = slice(j * c, (j + 1) * c)
+            totals[j] = totals[j] + dot(picks[j], dxr[span])
+            outs[j] = outs[j] + dot(picks[j], rows[span])
+            metas[j] = metas[j] + dot(picks[j], meta[span])
+
+    @pl.when(k < stages - 1)
+    def _():
+        ring_x(k).wait_send()
+
+    swap_x(k).wait_send()
+    for j in range(2):
+        xbuf[k, j, :, :width] = totals[j].astype(BF)
+        xbuf[k, j, :, width:] = metas[j].astype(BF)
+        out_ref[0, j] = outs[j].astype(BF)
+
+    @pl.when(k >= 1)
+    def _():
+        swap_r(k).start()
+
+    def advance(i, first):
+        swap_r(i).wait_recv()
+        here = xbuf[i, 0].astype(F32) + sbuf[i].astype(F32)
+        if not first:
+            ring_t(i - 1).wait_recv()
+            here = here + tbuf[i - 1].astype(F32)
+        xbuf[i, 0] = here.astype(BF)
+        ring_t(i).start()
+
+    for i in range(1, stages - 1):
+
+        @pl.when(k == i + 1)
+        def _(i=i):
+            advance(i, i == 1)
+
+    @pl.when(k == stages - 1)
+    def _():
+        swap_r(0).start()
+        advance(stages - 1, stages == 2)
+        swap_r(0).wait_recv()
+        ring_t(stages - 1).wait_recv()
+        dx_ref[...] = (
+            xbuf[0, 0].astype(F32) + sbuf[0].astype(F32) + tbuf[stages - 1].astype(F32)
+        )
+        for i in range(stages):
+            swap_r(i).wait_send()
+        for i in range(1, stages):
+            ring_t(i).wait_send()
+
+
+def dispatch(capacity, total, x_ext, g_all, gates, ups, downs, sg, su, sd):
+    stages, _, tokens, ext = g_all.shape
+    width, shared = sg.shape
+    hidden = gates[0].shape[2]
+    wide = -(-hidden // LANES) * LANES
+    c2 = 2 * capacity
+    once = pl.Buffered(1)
+
+    def fixed(shape):
+        return pl.BlockSpec(shape, lambda k: (0,) * len(shape), pipeline_mode=once)
+
+    def per_stage(shape):
+        return pl.BlockSpec(shape, lambda k: (0, k, 0, 0), pipeline_mode=once)
+
+    anywhere = pl.BlockSpec(memory_space=pl.ANY)
+    return pl.pallas_call(
+        functools.partial(dispatch_kernel, capacity, total),
+        grid=(stages,),
+        in_specs=[
+            fixed((tokens, ext)),
+            pl.BlockSpec((1, 2, tokens, ext), lambda k: (k, 0, 0, 0)),
+        ]
+        + [anywhere] * 12
+        + [fixed(sg.shape), fixed(su.shape), fixed(sd.shape)],
+        out_specs=[
+            fixed((tokens, ext)),
+            pl.BlockSpec((1, 2, tokens, width), lambda k: (k, 0, 0, 0), pipeline_mode=once),
+            fixed((width, 2 * shared)),
+            fixed((shared, width)),
+            per_stage((2, 1, c2, width)),
+            per_stage((2, 1, c2, width)),
+            per_stage((2, 1, c2, 8 * wide)),
+            per_stage((2, 1, c2, 4 * wide)),
+        ],
+        out_shape=[
+            jax.ShapeDtypeStruct((tokens, ext), F32),
+            jax.ShapeDtypeStruct((stages, 2, tokens, width), BF),
+            jax.ShapeDtypeStruct((width, 2 * shared), F32),
+            jax.ShapeDtypeStruct((shared, width), F32),
+            jax.ShapeDtypeStruct((2, stages, c2, width), BF),
+            jax.ShapeDtypeStruct((2, stages, c2, width), BF),
+            jax.ShapeDtypeStruct((2, stages, c2, 8 * wide), BF),
+            jax.ShapeDtypeStruct((2, stages, c2, 4 * wide), BF),
+        ],
+        scratch_shapes=[
+            pltpu.VMEM((stages, 2, tokens, ext), BF),
+            pltpu.VMEM((stages, tokens, ext), BF),
+            pltpu.VMEM((stages, tokens, ext), BF),
+            pltpu.VMEM((2, width, 8 * wide), BF),
+            pltpu.VMEM((2, 4 * wide, width), BF),
+            pltpu.VMEM((2, width, hidden), BF),
+        ]
+        + [pltpu.SemaphoreType.DMA((stages,))] * 8
+        + [pltpu.SemaphoreType.DMA((2,)), pltpu.SemaphoreType.DMA((8,))],
+        compiler_params=pltpu.CompilerParams(
+            vmem_limit_bytes=63 * MIB, collective_id=0, has_side_effects=True
+        ),
+        cost_estimate=pl.CostEstimate(
+            flops=24 * c2 * stages * width * 4 * hidden,
+            bytes_accessed=80 * MIB,
+            transcendentals=stages * c2 * 8 * hidden,
+        ),
+    )(x_ext, g_all, *gates, *ups, *downs, sg, su, sd)
+
+
 def rms(values):
     return lax.rsqrt(jnp.mean(values * values, axis=-1, keepdims=True) + epsilon)
 
@@ -493,8 +784,10 @@
     far_tokens = swap_y(tokens)
     k_w, v_w = gather_hp(key_weight), gather_hp(value_weight)
     q_w = gather_hp(query_weight)
-    o_w = gather_hp(out_weight)
-    gates, ups, downs = gather_hp(expert_gate), gather_hp(expert_up), gather_hp(expert_down)
+    o_w = gather_hp(after(out_weight, q_w[2], k_w[2], v_w[2]))
+    gates, ups, downs = (
+        gather_hp(after(v, o_w[2])) for v in (expert_gate, expert_up, expert_down)
+    )
     units = shared_down.shape[0] // ep
     tiny = [attn_gain[:, None], ffn_gain[:, None], router_weight]
     small = jnp.concatenate(tiny + [jnp.zeros((width // 4, LANES - 2 - total), BF)], axis=1)
@@ -538,7 +831,7 @@
     residual = tokens.astype(F32)
     both = relative(jnp.concatenate([tokens, far_tokens], axis=0), h, 1).astype(F32)
     inv_one = rms(both)
-    first_in = (both * inv_one * gain_one).astype(BF)
+    first_in = after((both * inv_one * gain_one).astype(BF), g_blocks)
 
     def rotate(v, n):
         return v * cosine[:n] + half_turn(v) * sine[:n]
@@ -567,52 +860,69 @@
         [second_in, pair_weight.astype(BF), jnp.zeros((rows, LANES - total), BF)], axis=1
     )
 
-    x_blocks = gather_ep(x_ext)
-    carry = (jnp.zeros((width, 2 * LANES), F32), jnp.zeros((LANES, width), F32))
-    bufs, dx_parts = None, []
-    for k in range(stages):
-        dx, carry, bufs = expert_stage(
-            k,
-            stages,
-            capacity,
-            total,
-            e_arr,
-            x_blocks[k],
-            g_blocks[k],
-            gates,
-            ups,
-            downs,
-            sg,
-            su,
-            sd,
-            carry,
-            bufs,
+    flat = (2, ep * capacity)
+
+    def expert_grad(left, right):
+        return jnp.einsum("xna,xnb->xab", left, right, preferred_element_type=F32)
+
+    if stages <= 4:
+        g_all = jnp.stack([jnp.stack(pair) for pair in g_blocks])
+        dx_sum, out_all, sgg, sdg, xr, gr, gu, wa = dispatch(
+            capacity, total, x_ext, g_all, gates, ups, downs, sg, su, sd
         )
-        dx_parts.append(dx)
-    dx_sum = scatter_ep(dx_parts)
-    sa, xr, gr, gi, ui, wa = bufs
-    out_parts = [
-        expert_out(k, capacity, e_arr, g_blocks[k], wa, sa, downs, sd) for k in range(stages)
-    ]
-    layer = (middle + scatter_ep(out_parts)).astype(BF)
-
-    flat = (2, stages * 2 * capacity)
-    xr, gr = xr.reshape(flat + (width,)), gr.reshape(flat + (width,))
-    gi, ui, wa = (v.reshape((4,) + flat + (v.shape[-1],)) for v in (gi, ui, wa))
-
-    def expert_grad(spec, left, right):
-        return jnp.einsum(spec, left, right, preferred_element_type=F32)
-
-    gate_grad = scatter_hp([expert_grad("xnd,xnf->xdf", xr, gi[r]) for r in range(4)])
-    up_grad = scatter_hp([expert_grad("xnd,xnf->xdf", xr, ui[r]) for r in range(4)])
-    down_grad = scatter_hp([expert_grad("xnf,xnd->xfd", wa[r], gr) for r in range(4)])
-
-    sgg, sdg = carry
+        out_parts = [(out_all[k, 0], out_all[k, 1]) for k in range(stages)]
+        hidden, wide = expert_gate.shape[2], wa.shape[3] // 4
+        xr, gr, gu, wa = (v.reshape(flat + (v.shape[-1],)) for v in (xr, gr, gu, wa))
+        gu = expert_grad(xr, gu).astype(BF)
+        wa = expert_grad(wa, gr).astype(BF)
+        gate_parts, up_parts = (
+            [gu[:, :, at * wide : at * wide + hidden] for at in range(i, 8, 2)] for i in (0, 1)
+        )
+        down_parts = [wa[:, r * wide : r * wide + hidden] for r in range(4)]
+    else:
+        x_blocks = gather_ep(after(x_ext, g_blocks))
+        carry = (jnp.zeros((width, 2 * LANES), F32), jnp.zeros((LANES, width), F32))
+        bufs, dx_parts = None, []
+        for k in range(stages):
+            dx, carry, bufs = expert_stage(
+                k,
+                stages,
+                capacity,
+                total,
+                e_arr,
+                x_blocks[k],
+                g_blocks[k],
+                gates,
+                ups,
+                downs,
+                sg,
+                su,
+                sd,
+                carry,
+                bufs,
+            )
+            dx_parts.append(dx)
+        dx_sum = scatter_ep(dx_parts)
+        sgg, sdg = carry
+        sa, xr, gr, gi, ui, wa = bufs
+        out_parts = [
+            expert_out(k, capacity, e_arr, g_blocks[k], wa, sa, downs, sd) for k in range(stages)
+        ]
+        xr, gr = xr.reshape(flat + (width,)), gr.reshape(flat + (width,))
+        gi, ui, wa = (v.reshape((4,) + flat + (v.shape[-1],)) for v in (gi, ui, wa))
+        gate_parts = [expert_grad(xr, gi[r]) for r in range(4)]
+        up_parts = [expert_grad(xr, ui[r]) for r in range(4)]
+        down_parts = [expert_grad(wa[r], gr) for r in range(4)]
+    layer = (middle + scatter_ep(after(out_parts, dx_sum))).astype(BF)
+    gate_grad, up_grad, down_grad = (
+        scatter_hp(parts) for parts in (gate_parts, up_parts, down_parts)
+    )
+
     sgg = relative(sgg, h, 0)
     sgg = scatter_hp(jnp.split(sgg, 4, axis=0)).astype(BF)
     sdg = scatter_hp(jnp.split(relative(sdg[: 4 * units], h, 0), 4, axis=0)).astype(BF)
-    sgg = lax.all_gather(sgg, "ep", axis=0, tiled=False)
-    sdg = lax.all_gather(sdg, "ep", axis=0, tiled=True)
+    sgg, sdg = (spread_ep(after(v, dx_sum), e) for v in (sgg, sdg))
+    sdg = sdg.reshape(ep * units, width)
 
     def spread(v):
         v = v[:, :, : 4 * units].reshape(ep, width // 4, 4, units)

time: 998 us -> 871 us (0.87)
  waiting for transfers between devices: 403 us -> 289 us
  blocking collectives: 44.3 us -> 0 us
  Pallas kernels: 149 us -> 176 us
  starting transfers between devices: 84.2 us -> 100 us
  between operations: 16.2 us -> 2.93 us
    ppermute x36 -> x6, waiting for transfers between devices: 141 us -> 20.1 us  [ring(): return lax.ppermute(v, 'ep', [(i, (i + 2) % n) for i in range(n)])]
    ppermute x0 -> x30, waiting for transfers between devices: none -> 61.4 us  [shift(): return lax.ppermute(v, 'ep', [(i, (i + 2 * steps) % n) for i in range(n)])]
    ppermute x0 -> x30, starting transfers between devices: none -> 45.1 us  [shift(): return lax.ppermute(v, 'ep', [(i, (i + 2 * steps) % n) for i in range(n)])]
    all_gather x1 -> x0, blocking collectives: 44.3 us -> none  [per_device(): sdg = lax.all_gather(sdg, 'ep', axis=0, tiled=True)]
    ppermute x22, waiting for transfers between devices: 125 us -> 96.6 us  [swap_y(): return lax.ppermute(v, 'hp', [(i, i ^ 2) for i in range(4)])]
    pallas_call x8 -> x1, Pallas kernels: 125 us -> 152 us  [dispatch(): pl.pallas_call(functools.partial(dispatch_kernel, capacity, total), grid=...]
    ppermute x24 -> x18, waiting for transfers between devices: 108 us -> 89.8 us  [swap_pair(): return lax.ppermute(v, 'ep', [(i, i ^ 1) for i in range(n)])]
    unnamed x234 -> x188, local copies, waits for them, and re-layouts: 53.1 us -> 37.5 us
  transfers between devices with their start and end apart: 130 -> 123, of which waited for: 57 -> 50; matrix products, arithmetic and copies ran while one was open for 26% -> 30% of each run, Pallas kernels for 14% -> 3%
where the time goes in v2:
time: 871 us; the launch traced here: 860 us
  waiting for transfers between devices  289 us (33%)
  Pallas kernels  176 us (20%)
  local copies, waits for them, and re-layouts  130 us (15%)
  starting transfers between devices  100 us (11%)
  other arithmetic  85.6 us (10%)
  matrix products  76.8 us (9%)
    pallas_call x1, Pallas kernels, dispatch(): pl.pallas_call(functools.partial(dispatch_kernel, capacity, total), grid=...  152 us
    ppermute x22, waiting for transfers between devices, swap_y(): return lax.ppermute(v, 'hp', [(i, i ^ 2) for i in range(4)])  96.6 us
    ppermute x18, waiting for transfers between devices, swap_pair(): return lax.ppermute(v, 'ep', [(i, i ^ 1) for i in range(n)])  89.8 us
    ppermute x30, waiting for transfers between devices, shift(): return lax.ppermute(v, 'ep', [(i, (i + 2 * steps) % n) for i in range(n)])  61.4 us
    dot_general x16, matrix products, dot(): lax.dot_general(left, right, (((over[0],), (over[1],)), ((), ())), prefer...  47.9 us
    ppermute x30, starting transfers between devices, shift(): return lax.ppermute(v, 'ep', [(i, (i + 2 * steps) % n) for i in range(n)])  45.1 us
    unnamed x188, local copies, waits for them, and re-layouts  37.5 us
    dot_general x2, matrix products, expert_grad(): return jnp.einsum('xna,xnb->xab', left, right, preferred_element_type=F32)  28.9 us
  transfers between devices with their start and end apart: 123, of which 50 were waited for; matrix products, arithmetic and copies ran while one was open for 30% of the time, Pallas kernels for 3%

profile of v2, /device:TPU:0, one launch (start us, length us, event | category | flops | bytes accessed | tf_op | source)
XLA Modules:
  0.0 860.2 jit_solution(4687807655268903652)
XLA Ops:
  58.8 15.2 %collective-permute-done.18 = bf16[320,1280]{1,0:T(8,128)(2,1)} collective-permute-done((bf16[320,1280]{1,0:T(8,128)(2,1)}, bf16[320,1280]{1,0:T(8,128)(2,1)}, u32[]{:S(2)}, u32[]{:S(2)}) %collective-permute-start.18) | collective-permute-done | bytes 819232 | tf_op jit(solution)/shard_map/ppermute | solution.py:30
  75.6 15.5 %collective-permute-done.12 = bf16[320,1280]{1,0:T(8,128)(2,1)S(1)} collective-permute-done((bf16[320,1280]{1,0:T(8,128)(2,1)S(1)}, bf16[320,1280]{1,0:T(8,128)(2,1)S(1)}, u32[]{:S(2)}, u32[]{:S(2)}) %collective-permute-start.12) | collective-permute-done | bytes 819232 | tf_op jit(solution)/shard_map/ppermute | solution.py:30
  101.3 7.8 collective-permute-done.6
  118.7 14.0 %collective-permute-done.9 = bf16[256,1408]{1,0:T(8,128)(2,1)S(1)} collective-permute-done((bf16[256,1408]{1,0:T(8,128)(2,1)S(1)}, bf16[256,1408]{1,0:T(8,128)(2,1)S(1)}, u32[]{:S(2)}, u32[]{:S(2)}) %collective-permute-start.9) | collective-permute-done | bytes 720928 | tf_op jit(solution)/shard_map/ppermute | solution.py:40
  150.2 18.2 %collective-permute-done.28 = bf16[2,1280,224]{1,2,0:T(8,128)(2,1)} collective-permute-done((bf16[2,1280,224]{1,2,0:T(8,128)(2,1)}, bf16[2,1280,224]{1,2,0:T(8,128)(2,1)}, u32[]{:S(2)}, u32[]{:S(2)}) %collective-permute-start.28) | collective-permute-done | bytes 1146912 | tf_op jit(solution)/shard_map/ppermute | solution.py:30
  173.7 18.3 %collective-permute-done.31.refs_10_ = bf16[2,224,1280]{2,1,0:T(8,128)(2,1)} collective-permute-done((bf16[2,224,1280]{2,1,0:T(8,128)(2,1)}, bf16[2,224,1280]{2,1,0:T(8,128)(2,1)}, u32[]{:S(2)}, u32[]{:S(2)}) %collective-permute-start.31) | collective-permute-done | bytes 1146912 | tf_op jit(solution)/shard_map/ppermute | solution.py:30
  221.7 10.2 %shard_map.288 = (bf16[256,1280]{1,0:T(8,128)(2,1)S(1)}, f32[256,1280]{1,0:T(8,128)S(1)}) custom-call(s32[1]{0:T(128)} %bitcast.h_ref, bf16[256,1280]{1,0:T(8,128)(2,1)S(1)} %fusion.20.q_ref, bf16[512,2560]{1,0:T(8,128)(2,1)S(1)} %pad_maximum_fusion.1.ka_ref.va_ref, bf16[512,2560]{1,0:T(8,128)(2,1)} %collective-permute-done.20.kb_ref.vb_ref, ...), custom_call_target="tpu_custom_call" | custom-call | flops 1342177280 | bytes 8388608 | tf_op jit(solution)/shard_map/pallas_call | solution.py:212
  240.5 151.7 %shard_map.289 = (f32[256,1408]{1,0:T(8,128)}, bf16[4,2,256,1280]{3,2,1,0:T(8,128)(2,1)}, f32[1280,256]{1,0:T(8,128)}, f32[128,1280]{1,0:T(8,128)}, bf16[2,4,288...) custom-call(bf16[256,1408]{1,0:T(8,128)(2,1)} %concatenate.151.x_ref, ...), custom_call_target="tpu_custom_call" | custom-call | flops 31708938240 | bytes 83886080 | tf_op jit(solution)/shard_map/pallas_call | solution.py:681
  399.5 9.2 %convolution_convert_fusion.1 = bf16[2,1024,1280]{2,1,0:T(8,128)(2,1)S(1)} fusion(bf16[2,1152,1024]{2,1,0:T(8,128)(2,1)S(1)} %bitcast.301, bf16[2,1152,1280]{2,1,0:T(8,128)(2,1)} %bitcast.300), kind=kOutput, calls=%fused_computation.2 | convolution fusion | flops 6042419200 | bytes 15859712 | tf_op jit(solution)/shard_map/xna,xnb->xab/dot_general | solution.py:866
  412.5 19.7 %convolution_convert_fusion = bf16[2,1280,2048]{1,2,0:T(8,128)(2,1)} fusion(bf16[2,1152,1280]{2,1,0:T(8,128)(2,1)} %bitcast.299, bf16[2,1152,2048]{2,1,0:T(8,128)(2,1)} %bitcast.298), kind=kOutput, calls=%fused_computation | convolution fusion | flops 12084838400 | bytes 25821184 | tf_op jit(solution)/shard_map/xna,xnb->xab/dot_general | solution.py:866
  438.3 4.9 slice_bitcast_fusion
  468.3 5.2 collective-permute-done.98
  475.9 5.7 collective-permute-done.99
  483.6 5.9 collective-permute-done.103
  490.2 7.3 collective-permute-done.104
  507.5 14.0 %collective-permute-done.39 = bf16[256,1280]{1,0:T(8,128)(2,1)} collective-permute-done((bf16[256,1280]{1,0:T(8,128)(2,1)}, bf16[256,1280]{1,0:T(8,128)(2,1)}, u32[]{:S(2)}, u32[]{:S(2)}) %collective-permute-start.39) | collective-permute-done | bytes 655392 | tf_op jit(solution)/shard_map/ppermute | solution.py:35
  524.0 11.6 %collective-permute-done.106 = bf16[4,320,256]{2,1,0:T(8,128)(2,1)} collective-permute-done((bf16[4,320,256]{2,1,0:T(8,128)(2,1)}, bf16[4,320,256]{2,1,0:T(8,128)(2,1)}, u32[]{:S(2)}, u32[]{:S(2)}) %collective-permute-start.106) | collective-permute-done | bytes 655392 | tf_op jit(solution)/shard_map/ppermute | solution.py:35
  540.3 7.3 collective-permute-done.38
  582.2 5.0 convert_add_fusion.2
  587.2 9.6 %collective-permute-done.36 = bf16[256,1280]{1,0:T(8,128)(2,1)S(1)} collective-permute-done((bf16[256,1280]{1,0:T(8,128)(2,1)S(1)}, bf16[256,1280]{1,0:T(8,128)(2,1)S(1)}, u32[]{:S(2)}, u32[]{:S(2)}) %collective-permute-start.36) | collective-permute-done | bytes 655392 | tf_op jit(solution)/shard_map/ppermute | solution.py:35
  613.3 14.4 %shard_map.290 = (f32[256,1280]{1,0:T(8,128)S(1)}, f32[512,1280]{1,0:T(8,128)S(1)}, f32[512,1280]{1,0:T(8,128)S(1)}, bf16[512,1280]{1,0:T(8,128)(2,1)S(1)}, bf16[512,1280]{1,0:T(8,128)(2,1)S(1)}) custom-call(s32[1]{0:T(128)} %bitcast.h_ref, bf16[256,1280]{1,0:T(8,128)(2,1)S(1)} %fusion.20.q_ref, bf16[512,2560]{1,0:T(8,128)(2,1)S(1)} %copy-done.1, ...), custom_call_target="tpu_custom_call" | custom-call | flops 3355443200 | bytes 16777216 | tf_op jit(solution)/shard_map/pallas_call | solution.py:241
  671.0 4.9 fusion.108
  684.8 9.5 %collective-permute-done.45 = bf16[256,1280]{1,0:T(8,128)(2,1)S(1)} collective-permute-done((bf16[256,1280]{1,0:T(8,128)(2,1)S(1)}, bf16[256,1280]{1,0:T(8,128)(2,1)S(1)}, u32[]{:S(2)}, u32[]{:S(2)}) %collective-permute-start.45) | collective-permute-done | bytes 655392 | tf_op jit(solution)/shard_map/ppermute | solution.py:30
  719.6 9.7 %collective-permute-done.54 = bf16[160,1280]{1,0:T(8,128)(2,1)S(1)} collective-permute-done((bf16[160,1280]{1,0:T(8,128)(2,1)}, bf16[160,1280]{1,0:T(8,128)(2,1)S(1)}, u32[]{:S(2)}, u32[]{:S(2)}) %collective-permute-start.54) | collective-permute-done | bytes 409632 | tf_op jit(solution)/shard_map/ppermute | solution.py:35
  751.6 5.1 collective-permute-done.91
  756.7 6.4 collective-permute-done.92
  767.8 7.0 collective-permute-done.58
  774.8 6.0 collective-permute-done.59
  786.7 10.9 %collective-permute-done.94 = bf16[160,1280]{1,0:T(8,128)(2,1)S(1)} collective-permute-done((bf16[160,1280]{1,0:T(8,128)(2,1)S(1)}, bf16[160,1280]{1,0:T(8,128)(2,1)S(1)}, u32[]{:S(2)}, u32[]{:S(2)}) %collective-permute-start.94) | collective-permute-done | bytes 409632 | tf_op jit(solution)/shard_map/ppermute | solution.py:35
  800.3 7.4 collective-permute-done.61
  813.5 5.6 collective-permute-done.76
  819.3 4.9 collective-permute-start.78
  (645 shorter events, 409.5 us)
Async XLA Ops:
  35.6 56.1 %collective-permute-start.14 = (bf16[320,1280]{1,0:T(8,128)(2,1)}, bf16[320,1280]{1,0:T(8,128)(2,1)}, u32[]{:S(2)}, u32[]{:S(2)}) collective-permute-start(bf16[320,1280]{1,0:T(8,128)(2,1)} %param.20), channel_id=1, source_target_pairs={{0,1},{1,0},{2,3},{3,2},{4,5},{5,4},{6,7},{7,6},{8,9},{9,8},{10,11... | collective-permute-start | bytes 2457608 | tf_op jit(solution)/shard_map/ppermute | solution.py:26
  50.6 40.5 %collective-permute-start.12 = (bf16[320,1280]{1,0:T(8,128)(2,1)S(1)}, bf16[320,1280]{1,0:T(8,128)(2,1)S(1)}, u32[]{:S(2)}, u32[]{:S(2)}) collective-permute-start(bf16[320,1280]{1,0:T(8,128)(2,1)S(1)} %copy-done.49), channel_id=1, source_target_pairs={{0,2},{1,3},{2,0},{3,1},{4,6},{5,7},{6,4},{7,5},{8,10},{9,11},{10,... | collective-permute-start | bytes 2457608 | tf_op jit(solution)/shard_map/ppermute | solution.py:30
  51.6 44.9 %collective-permute-start.17 = (bf16[320,1280]{1,0:T(8,128)(2,1)}, bf16[320,1280]{1,0:T(8,128)(2,1)S(1)}, u32[]{:S(2)}, u32[]{:S(2)}) collective-permute-start(bf16[320,1280]{1,0:T(8,128)(2,1)} %param.21), channel_id=1, source_target_pairs={{0,1},{1,0},{2,3},{3,2},{4,5},{5,4},{6,7},{7,6},{8,9},{9,8},{10,11... | collective-permute-start | bytes 2457608 | tf_op jit(solution)/shard_map/ppermute | solution.py:26
  56.5 40.0 %collective-permute-start.11 = (bf16[320,1280]{1,0:T(8,128)(2,1)S(1)}, bf16[320,1280]{1,0:T(8,128)(2,1)S(1)}, u32[]{:S(2)}, u32[]{:S(2)}) collective-permute-start(bf16[320,1280]{1,0:T(8,128)(2,1)S(1)} %copy-done.49), channel_id=1, source_target_pairs={{0,1},{1,0},{2,3},{3,2},{4,5},{5,4},{6,7},{7,6},{8,9},{9,8},{10,11... | collective-permute-start | bytes 2457608 | tf_op jit(solution)/shard_map/ppermute | solution.py:26
  118.6 52.2 %collective-permute-start.24 = (bf16[2,1280,224]{1,2,0:T(8,128)(2,1)S(1)}, bf16[2,1280,224]{1,2,0:T(8,128)(2,1)}, u32[]{:S(2)}, u32[]{:S(2)}) collective-permute-start(bf16[2,1280,224]{1,2,0:T(8,128)(2,1)S(1)} %copy-done.47), channel_id=1, source_target_pairs={{0,1},{1,0},{2,3},{3,2},{4,5},{5,4},{6,7},{7,6},{8,9},{9,8},{10,11... | collective-permute-start | bytes 3440648 | tf_op jit(solution)/shard_map/ppermute | solution.py:26
  132.7 35.7 %collective-permute-start.28 = (bf16[2,1280,224]{1,2,0:T(8,128)(2,1)}, bf16[2,1280,224]{1,2,0:T(8,128)(2,1)}, u32[]{:S(2)}, u32[]{:S(2)}) collective-permute-start(bf16[2,1280,224]{1,2,0:T(8,128)(2,1)} %param.29), channel_id=1, source_target_pairs={{0,2},{1,3},{2,0},{3,1},{4,6},{5,7},{6,4},{7,5},{8,10},{9,11},{10,... | collective-permute-start | bytes 3440648 | tf_op jit(solution)/shard_map/ppermute | solution.py:30
  133.2 58.7 %collective-permute-start.27 = (bf16[2,1280,224]{1,2,0:T(8,128)(2,1)}, bf16[2,1280,224]{1,2,0:T(8,128)(2,1)}, u32[]{:S(2)}, u32[]{:S(2)}) collective-permute-start(bf16[2,1280,224]{1,2,0:T(8,128)(2,1)} %param.29), channel_id=1, source_target_pairs={{0,1},{1,0},{2,3},{3,2},{4,5},{5,4},{6,7},{7,6},{8,9},{9,8},{10,11... | collective-permute-start | bytes 3440648 | tf_op jit(solution)/shard_map/ppermute | solution.py:26
  133.3 58.7 %collective-permute-start.31 = (bf16[2,224,1280]{2,1,0:T(8,128)(2,1)}, bf16[2,224,1280]{2,1,0:T(8,128)(2,1)}, u32[]{:S(2)}, u32[]{:S(2)}) collective-permute-start(bf16[2,224,1280]{2,1,0:T(8,128)(2,1)} %refs_8_), channel_id=1, source_target_pairs={{0,2},{1,3},{2,0},{3,1},{4,6},{5,7},{6,4},{7,5},{8,10},{9,11},{10,... | collective-permute-start | bytes 3440648 | tf_op jit(solution)/shard_map/ppermute | solution.py:30
  143.8 51.1 %collective-permute-start.10 = (bf16[256,1408]{1,0:T(8,128)(2,1)}, bf16[256,1408]{1,0:T(8,128)(2,1)}, u32[]{:S(2)}, u32[]{:S(2)}) collective-permute-start(bf16[256,1408]{1,0:T(8,128)(2,1)} %copy-done.57), channel_id=1, source_target_pairs={{0,4},{4,0},{8,12},{12,8},{16,20},{20,16},{24,28},{28,24},{1,5},{5... | collective-permute-start | bytes 2162696 | tf_op jit(solution)/shard_map/ppermute | solution.py:35
  168.4 72.1 %collective-permute-start.30 = (bf16[2,224,1280]{2,1,0:T(8,128)(2,1)}, bf16[2,224,1280]{2,1,0:T(8,128)(2,1)}, u32[]{:S(2)}, u32[]{:S(2)}) collective-permute-start(bf16[2,224,1280]{2,1,0:T(8,128)(2,1)} %refs_8_), channel_id=1, source_target_pairs={{0,1},{1,0},{2,3},{3,2},{4,5},{5,4},{6,7},{7,6},{8,9},{9,8},{10,11... | collective-permute-start | bytes 3440648 | tf_op jit(solution)/shard_map/ppermute | solution.py:26
  170.8 46.1 %collective-permute-start.26 = (bf16[2,1280,224]{1,2,0:T(8,128)(2,1)}, bf16[2,1280,224]{1,2,0:T(8,128)(2,1)}, u32[]{:S(2)}, u32[]{:S(2)}) collective-permute-start(bf16[2,1280,224]{1,2,0:T(8,128)(2,1)} %collective-permute-done.25), channel_id=1, source_target_pairs={{0,1},{1,0},{2,3},{3,2},{4,5},{5,4},{6,7},{7,6},{8,9},{9,8},{10,11... | collective-permute-start | bytes 3440648 | tf_op jit(solution)/shard_map/ppermute | solution.py:26
  192.0 48.5 %collective-permute-start.32 = (bf16[2,224,1280]{2,1,0:T(8,128)(2,1)}, bf16[2,224,1280]{2,1,0:T(8,128)(2,1)}, u32[]{:S(2)}, u32[]{:S(2)}) collective-permute-start(bf16[2,224,1280]{2,1,0:T(8,128)(2,1)} %collective-permute-done.31.refs_10_), channel_id=1, source_target_pairs={{0,1},{1,0},{2,3},{3,2},{4,5},{5,4},{6,7},{7,6},{8,9},{9,8},{10,11... | collective-permute-start | bytes 3440648 | tf_op jit(solution)/shard_map/ppermute | solution.py:26
  412.5 140.2 %collective-permute-start.121 = (bf16[2,224,1280]{2,1,0:T(8,128)(2,1)}, bf16[2,224,1280]{2,1,0:T(8,128)(2,1)}, u32[]{:S(2)}, u32[]{:S(2)}) collective-permute-start(bf16[2,224,1280]{2,1,0:T(8,128)(2,1)} %get-tuple-element.177), channel_id=1, source_target_pairs={{0,1},{1,0},{2,3},{3,2},{4,5},{5,4},{6,7},{7,6},{8,9},{9,8},{10,11... | collective-permute-start | bytes 3440648 | tf_op jit(solution)/shard_map/ppermute | solution.py:26
  436.9 100.4 %collective-permute-start.118 = (bf16[2,1280,224]{1,2,0:T(8,128)(2,1)}, bf16[2,1280,224]{1,2,0:T(8,128)(2,1)}, u32[]{:S(2)}, u32[]{:S(2)}) collective-permute-start(bf16[2,1280,224]{1,2,0:T(8,128)(2,1)} %get-tuple-element.173), channel_id=1, source_target_pairs={{0,1},{1,0},{2,3},{3,2},{4,5},{5,4},{6,7},{7,6},{8,9},{9,8},{10,11... | collective-permute-start | bytes 3440648 | tf_op jit(solution)/shard_map/ppermute | solution.py:26
  466.9 113.2 %collective-permute-start.115 = (bf16[2,1280,224]{1,2,0:T(8,128)(2,1)}, bf16[2,1280,224]{1,2,0:T(8,128)(2,1)}, u32[]{:S(2)}, u32[]{:S(2)}) collective-permute-start(bf16[2,1280,224]{1,2,0:T(8,128)(2,1)} %get-tuple-element.174), channel_id=1, source_target_pairs={{0,1},{1,0},{2,3},{3,2},{4,5},{5,4},{6,7},{7,6},{8,9},{9,8},{10,11... | collective-permute-start | bytes 3440648 | tf_op jit(solution)/shard_map/ppermute | solution.py:26
  467.0 38.3 %collective-permute-start.113 = (bf16[4,28,1280]{2,1,0:T(8,128)(2,1)S(1)}, bf16[4,28,1280]{2,1,0:T(8,128)(2,1)S(1)}, u32[]{:S(2)}, u32[]{:S(2)}) collective-permute-start(bf16[4,28,1280]{2,1,0:T(8,128)(2,1)S(1)} %bitcast_dynamic-update-slice_fusion.20), channel_id=1, source_target_pairs={{0,4},{4,0},{8,12},{12,8},{16,20},{20,16},{24,28},{28,24},{1,5},{5... | collective-permute-start | bytes 860168 | tf_op jit(solution)/shard_map/ppermute | solution.py:35
  537.3 43.1 %collective-permute-start.117 = (bf16[2,1280,224]{1,2,0:T(8,128)(2,1)}, bf16[2,1280,224]{1,2,0:T(8,128)(2,1)}, u32[]{:S(2)}, u32[]{:S(2)}) collective-permute-start(bf16[2,1280,224]{1,2,0:T(8,128)(2,1)} %get-tuple-element.172), channel_id=1, source_target_pairs={{0,1},{1,0},{2,3},{3,2},{4,5},{5,4},{6,7},{7,6},{8,9},{9,8},{10,11... | collective-permute-start | bytes 3440648 | tf_op jit(solution)/shard_map/ppermute | solution.py:26
  578.0 56.7 %collective-permute-start.120 = (bf16[2,224,1280]{2,1,0:T(8,128)(2,1)}, bf16[2,224,1280]{2,1,0:T(8,128)(2,1)}, u32[]{:S(2)}, u32[]{:S(2)}) collective-permute-start(bf16[2,224,1280]{2,1,0:T(8,128)(2,1)} %get-tuple-element.176), channel_id=1, source_target_pairs={{0,1},{1,0},{2,3},{3,2},{4,5},{5,4},{6,7},{7,6},{8,9},{9,8},{10,11... | collective-permute-start | bytes 3440648 | tf_op jit(solution)/shard_map/ppermute | solution.py:26
  578.0 63.6 %collective-permute-start.114 = (bf16[2,1280,224]{1,2,0:T(8,128)(2,1)}, bf16[2,1280,224]{1,2,0:T(8,128)(2,1)}, u32[]{:S(2)}, u32[]{:S(2)}) collective-permute-start(bf16[2,1280,224]{1,2,0:T(8,128)(2,1)} %get-tuple-element.175), channel_id=1, source_target_pairs={{0,1},{1,0},{2,3},{3,2},{4,5},{5,4},{6,7},{7,6},{8,9},{9,8},{10,11... | collective-permute-start | bytes 3440648 | tf_op jit(solution)/shard_map/ppermute | solution.py:26
  580.4 54.4 %collective-permute-start.122 = (bf16[2,224,1280]{2,1,0:T(8,128)(2,1)}, bf16[2,224,1280]{2,1,0:T(8,128)(2,1)}, u32[]{:S(2)}, u32[]{:S(2)}) collective-permute-start(bf16[2,224,1280]{2,1,0:T(8,128)(2,1)} %add_convert_fusion.1), channel_id=1, source_target_pairs={{0,2},{1,3},{2,0},{3,1},{4,6},{5,7},{6,4},{7,5},{8,10},{9,11},{10,... | collective-permute-start | bytes 3440648 | tf_op jit(solution)/shard_map/ppermute | solution.py:30
  596.9 44.8 %collective-permute-start.116 = (bf16[2,1280,224]{1,2,0:T(8,128)(2,1)}, bf16[2,1280,224]{1,2,0:T(8,128)(2,1)}, u32[]{:S(2)}, u32[]{:S(2)}) collective-permute-start(bf16[2,1280,224]{1,2,0:T(8,128)(2,1)} %get-tuple-element.171), channel_id=1, source_target_pairs={{0,2},{1,3},{2,0},{3,1},{4,6},{5,7},{6,4},{7,5},{8,10},{9,11},{10,... | collective-permute-start | bytes 3440648 | tf_op jit(solution)/shard_map/ppermute | solution.py:30
  638.5 38.7 %collective-permute-start.84 = (bf16[320,1280]{1,0:T(8,128)(2,1)}, bf16[320,1280]{1,0:T(8,128)(2,1)}, u32[]{:S(2)}, u32[]{:S(2)}) collective-permute-start(bf16[320,1280]{1,0:T(8,128)(2,1)} %get-tuple-element.186), channel_id=1, source_target_pairs={{0,1},{1,0},{2,3},{3,2},{4,5},{5,4},{6,7},{7,6},{8,9},{9,8},{10,11... | collective-permute-start | bytes 2457608 | tf_op jit(solution)/shard_map/ppermute | solution.py:26
  641.6 38.8 %collective-permute-start.51 = (bf16[320,1280]{1,0:T(8,128)(2,1)}, bf16[320,1280]{1,0:T(8,128)(2,1)}, u32[]{:S(2)}, u32[]{:S(2)}) collective-permute-start(bf16[320,1280]{1,0:T(8,128)(2,1)} %get-tuple-element.192), channel_id=1, source_target_pairs={{0,1},{1,0},{2,3},{3,2},{4,5},{5,4},{6,7},{7,6},{8,9},{9,8},{10,11... | collective-permute-start | bytes 2457608 | tf_op jit(solution)/shard_map/ppermute | solution.py:26
  641.7 35.5 %collective-permute-start.86 = (bf16[320,1280]{1,0:T(8,128)(2,1)}, bf16[320,1280]{1,0:T(8,128)(2,1)}, u32[]{:S(2)}, u32[]{:S(2)}) collective-permute-start(bf16[320,1280]{1,0:T(8,128)(2,1)} %fusion.9), channel_id=1, source_target_pairs={{0,2},{1,3},{2,0},{3,1},{4,6},{5,7},{6,4},{7,5},{8,10},{9,11},{10,... | collective-permute-start | bytes 2457608 | tf_op jit(solution)/shard_map/ppermute | solution.py:30
  646.0 34.5 %collective-permute-start.53 = (bf16[320,1280]{1,0:T(8,128)(2,1)}, bf16[320,1280]{1,0:T(8,128)(2,1)}, u32[]{:S(2)}, u32[]{:S(2)}) collective-permute-start(bf16[320,1280]{1,0:T(8,128)(2,1)} %fusion.15), channel_id=1, source_target_pairs={{0,2},{1,3},{2,0},{3,1},{4,6},{5,7},{6,4},{7,5},{8,10},{9,11},{10,... | collective-permute-start | bytes 2457608 | tf_op jit(solution)/shard_map/ppermute | solution.py:30
  657.9 73.3 %collective-permute-start.74 = (bf16[320,1280]{1,0:T(8,128)(2,1)}, bf16[320,1280]{1,0:T(8,128)(2,1)}, u32[]{:S(2)}, u32[]{:S(2)}) collective-permute-start(bf16[320,1280]{1,0:T(8,128)(2,1)} %get-tuple-element.189), channel_id=1, source_target_pairs={{0,1},{1,0},{2,3},{3,2},{4,5},{5,4},{6,7},{7,6},{8,9},{9,8},{10,11... | collective-permute-start | bytes 2457608 | tf_op jit(solution)/shard_map/ppermute | solution.py:26
  677.1 131.9 %collective-permute-start.73 = (bf16[320,1280]{1,0:T(8,128)(2,1)}, bf16[320,1280]{1,0:T(8,128)(2,1)}, u32[]{:S(2)}, u32[]{:S(2)}) collective-permute-start(bf16[320,1280]{1,0:T(8,128)(2,1)} %get-tuple-element.188), channel_id=1, source_target_pairs={{0,1},{1,0},{2,3},{3,2},{4,5},{5,4},{6,7},{7,6},{8,9},{9,8},{10,11... | collective-permute-start | bytes 2457608 | tf_op jit(solution)/shard_map/ppermute | solution.py:26
  680.5 53.3 %collective-permute-start.63 = (bf16[320,1280]{1,0:T(8,128)(2,1)}, bf16[320,1280]{1,0:T(8,128)(2,1)}, u32[]{:S(2)}, u32[]{:S(2)}) collective-permute-start(bf16[320,1280]{1,0:T(8,128)(2,1)} %get-tuple-element.191), channel_id=1, source_target_pairs={{0,1},{1,0},{2,3},{3,2},{4,5},{5,4},{6,7},{7,6},{8,9},{9,8},{10,11... | collective-permute-start | bytes 2457608 | tf_op jit(solution)/shard_map/ppermute | solution.py:26
  680.5 36.6 %collective-permute-start.87 = (bf16[160,1280]{1,0:T(8,128)(2,1)}, bf16[160,1280]{1,0:T(8,128)(2,1)}, u32[]{:S(2)}, u32[]{:S(2)}) collective-permute-start(bf16[160,1280]{1,0:T(8,128)(2,1)} %fusion.36), channel_id=1, source_target_pairs={{0,4},{4,0},{8,12},{12,8},{16,20},{20,16},{24,28},{28,24},{1,5},{5... | collective-permute-start | bytes 1228808 | tf_op jit(solution)/shard_map/ppermute | solution.py:35
  716.5 95.7 %collective-permute-start.62 = (bf16[320,1280]{1,0:T(8,128)(2,1)}, bf16[320,1280]{1,0:T(8,128)(2,1)S(1)}, u32[]{:S(2)}, u32[]{:S(2)}) collective-permute-start(bf16[320,1280]{1,0:T(8,128)(2,1)} %get-tuple-element.190), channel_id=1, source_target_pairs={{0,1},{1,0},{2,3},{3,2},{4,5},{5,4},{6,7},{7,6},{8,9},{9,8},{10,11... | collective-permute-start | bytes 2457608 | tf_op jit(solution)/shard_map/ppermute | solution.py:26
  745.0 64.1 %collective-permute-start.75 = (bf16[320,1280]{1,0:T(8,128)(2,1)S(1)}, bf16[320,1280]{1,0:T(8,128)(2,1)S(1)}, u32[]{:S(2)}, u32[]{:S(2)}) collective-permute-start(bf16[320,1280]{1,0:T(8,128)(2,1)S(1)} %fusion.11), channel_id=1, source_target_pairs={{0,2},{1,3},{2,0},{3,1},{4,6},{5,7},{6,4},{7,5},{8,10},{9,11},{10,... | collective-permute-start | bytes 2457608 | tf_op jit(solution)/shard_map/ppermute | solution.py:30
  748.9 63.2 %collective-permute-start.64 = (bf16[320,1280]{1,0:T(8,128)(2,1)S(1)}, bf16[320,1280]{1,0:T(8,128)(2,1)S(1)}, u32[]{:S(2)}, u32[]{:S(2)}) collective-permute-start(bf16[320,1280]{1,0:T(8,128)(2,1)S(1)} %fusion.13), channel_id=1, source_target_pairs={{0,2},{1,3},{2,0},{3,1},{4,6},{5,7},{6,4},{7,5},{8,10},{9,11},{10,... | collective-permute-start | bytes 2457608 | tf_op jit(solution)/shard_map/ppermute | solution.py:30
  (177 other events, 1831.5 us)

commit v3 on v2

--- a/solution.py
+++ b/solution.py
@@ -51,21 +51,29 @@
 
 def gather_hp(v):
     far = swap_y(v)
-    return [v, swap_core(v), far, swap_core(far)]
+    return [v, far, swap_core(v), swap_core(far)]
 
 
 def scatter_hp(parts):
-    near = swap_core(parts[1].astype(BF)).astype(F32) + parts[0].astype(F32)
-    over = swap_core(parts[3].astype(BF)).astype(F32) + parts[2].astype(F32)
+    near = swap_core(parts[2].astype(BF)).astype(F32) + parts[0].astype(F32)
+    over = swap_core(parts[3].astype(BF)).astype(F32) + parts[1].astype(F32)
     return near + swap_y(over.astype(BF)).astype(F32)
 
 
+def crossed(b, h):
+    odd, high = (h & 1) == 1, (h & 2) == 2
+    c = [jnp.where(odd, b[i ^ 1], b[i]) for i in range(4)]
+    return [jnp.where(high, c[i ^ 2], c[i]) for i in range(4)]
+
+
 def relative(v, h, axis):
+    c = crossed(jnp.split(v, 4, axis=axis), h)
+    return jnp.concatenate([c[0], c[2], c[1], c[3]], axis=axis)
+
+
+def absolute(v, h, axis):
     b = jnp.split(v, 4, axis=axis)
-    odd = (h & 1) == 1
-    c = [jnp.where(odd, b[i ^ 1], b[i]) for i in range(4)]
-    high = (h & 2) == 2
-    return jnp.concatenate([jnp.where(high, c[i ^ 2], c[i]) for i in range(4)], axis=axis)
+    return jnp.concatenate(crossed([b[0], b[2], b[1], b[3]], h), axis=axis)
 
 
 def gather_ep(v):
@@ -152,6 +160,61 @@
     return other * rows + key % rows <= at
 
 
+def turned(v, cosine, sine):
+    return v * cosine + pltpu.roll(v, HD // 2, 1) * sine
+
+
+def project_kernel(
+    t_ref, f_ref, gain_ref, k_ref, v_ref, q_ref, cos_ref, sin_ref, x_ref, kv_ref, query_ref
+):
+    rows = query_ref.shape[0]
+
+    @pl.when(pl.program_id(0) == 0)
+    def _():
+        for i, ref in enumerate((t_ref, f_ref)):
+            v = ref[...].astype(F32)
+            x_ref[i * rows : (i + 1) * rows, :] = (v * rms(v) * gain_ref[...]).astype(BF)
+
+    x = x_ref[...]
+    cosine, sine = cos_ref[...], sin_ref[...]
+    keys, query = dot(x, k_ref[...]), dot(x[:rows], q_ref[...])
+    kv_ref[1] = dot(x, v_ref[...]).astype(BF)
+    for i in range(k_ref.shape[1] // HD):
+        span = slice(i * HD, (i + 1) * HD)
+        kv_ref[0, :, span] = turned(keys[:, span], cosine, sine).astype(BF)
+        query_ref[:, span] = turned(query[:, span], cosine[:rows], sine[:rows]).astype(BF)
+
+
+def project(tokens, far, gain, k_w, v_w, q_w, cosine, sine):
+    rows, width = tokens.shape
+    two, block = 2 * rows, 2 * HD
+    cols = pl.BlockSpec((width, block), lambda i: (0, i))
+
+    def fixed(v):
+        return pl.BlockSpec(v.shape, lambda i: (0, 0))
+
+    return pl.pallas_call(
+        project_kernel,
+        grid=(width // block,),
+        in_specs=[fixed(tokens), fixed(far), fixed(gain), cols, cols, cols]
+        + [pl.BlockSpec((two, HD), lambda i: (0, 0))] * 2,
+        out_specs=[
+            pl.BlockSpec((two, width), lambda i: (0, 0)),
+            pl.BlockSpec((2, two, block), lambda i: (0, 0, i)),
+            pl.BlockSpec((rows, block), lambda i: (0, i)),
+        ],
+        out_shape=[
+            jax.ShapeDtypeStruct((two, width), BF),
+            jax.ShapeDtypeStruct((2, two, width), BF),
+            jax.ShapeDtypeStruct((rows, width), BF),
+        ],
+        compiler_params=pltpu.CompilerParams(vmem_limit_bytes=40 * MIB),
+        cost_estimate=pl.CostEstimate(
+            flops=10 * rows * width * width, bytes_accessed=14 * MIB, transcendentals=0
+        ),
+    )(tokens, far, gain, k_w, v_w, q_w, cosine, sine)
+
+
 def attend_kernel(h_ref, q_ref, ka_ref, kb_ref, va_ref, vb_ref, o_ref, lse_ref):
     rows = q_ref.shape[0]
     half = ka_ref.shape[0]
@@ -176,15 +239,16 @@
     vb_ref,
     d_ref,
     lse_ref,
+    cos_ref,
+    sin_ref,
     dq_ref,
-    dka_ref,
-    dva_ref,
-    dkb_ref,
-    dvb_ref,
+    da_ref,
+    db_ref,
 ):
     rows = q_ref.shape[0]
     half = ka_ref.shape[0]
     q, d = q_ref[...], d_ref[...]
+    cosine, sine = cos_ref[...], -sin_ref[...]
     s = jnp.concatenate([dot(q, ka_ref[...], (1, 1)), dot(q, kb_ref[...], (1, 1))], axis=1)
     s = jnp.where(score_mask(h_ref, rows, 2 * half), s * HD ** (-0.5), -1e30)
     p = jnp.exp(s - lse_ref[:, 0:1])
@@ -192,22 +256,27 @@
     inner = jnp.sum(p * back, axis=1, keepdims=True)
     sb = (p * (back - inner) * HD ** (-0.5)).astype(BF)
     p = p.astype(BF)
-    dq_ref[...] = dot(sb[:, :half], ka_ref[...]) + dot(sb[:, half:], kb_ref[...])
-    dk = dot(sb, q, (0, 0))
+    dq = dot(sb[:, :half], ka_ref[...]) + dot(sb[:, half:], kb_ref[...])
+    dq_ref[...] = turned(dq, cosine[:rows], sine[:rows]).astype(BF)
+    dk = turned(dot(sb, q, (0, 0)), cosine, sine)
     dv = dot(p, d, (0, 0))
-    dka_ref[...] = dk[:half]
-    dkb_ref[...] = dk[half:].astype(BF)
-    dva_ref[...] = dv[:half]
-    dvb_ref[...] = dv[half:].astype(BF)
-
-
-def head_spec(rows, skip=0):
-    return pl.BlockSpec((rows, HD), lambda i, h: (0, i + skip))
+    da_ref[0] = dk[:half]
+    da_ref[1] = dv[:half]
+    db_ref[0] = dk[half:].astype(BF)
+    db_ref[1] = dv[half:].astype(BF)
+
+
+def head_spec(rows):
+    return pl.BlockSpec((rows, HD), lambda i, h: (0, i))
+
+
+def kv_spec(rows, which):
+    return pl.BlockSpec((None, rows, HD), lambda i, h: (which, 0, i))
 
 
 def attend(h, q, kv_a, kv_b):
     rows, width = q.shape
-    half = kv_a.shape[0]
+    half = kv_a.shape[1]
     flops = 4 * rows * 2 * half * width
     return pl.pallas_call(
         attend_kernel,
@@ -216,10 +285,10 @@
             grid=(H,),
             in_specs=[
                 head_spec(rows),
-                head_spec(half),
-                head_spec(half),
-                head_spec(half, H),
-                head_spec(half, H),
+                kv_spec(half, 0),
+                kv_spec(half, 0),
+                kv_spec(half, 1),
+                kv_spec(half, 1),
             ],
             out_specs=[head_spec(rows), head_spec(rows)],
         ),
@@ -234,10 +303,12 @@
     )(h, q, kv_a, kv_b, kv_a, kv_b)
 
 
-def attend_back(h, q, kv_a, kv_b, d, lse):
+def attend_back(h, q, kv_a, kv_b, d, lse, cosine, sine):
     rows, width = q.shape
-    half = kv_a.shape[0]
+    half = kv_a.shape[1]
     flops = 10 * rows * 2 * half * width
+    table = pl.BlockSpec((2 * half, HD), lambda i, h: (0, 0))
+    both = pl.BlockSpec((2, half, HD), lambda i, h: (0, 0, i))
     return pl.pallas_call(
         attend_back_kernel,
         grid_spec=pltpu.PrefetchScalarGridSpec(
@@ -245,27 +316,27 @@
             grid=(H,),
             in_specs=[
                 head_spec(rows),
-                head_spec(half),
-                head_spec(half),
-                head_spec(half, H),
-                head_spec(half, H),
+                kv_spec(half, 0),
+                kv_spec(half, 0),
+                kv_spec(half, 1),
+                kv_spec(half, 1),
                 head_spec(rows),
                 head_spec(rows),
+                table,
+                table,
             ],
-            out_specs=[head_spec(rows)] + [head_spec(half)] * 4,
+            out_specs=[head_spec(rows), both, both],
         ),
         out_shape=[
-            jax.ShapeDtypeStruct((rows, width), F32),
-            jax.ShapeDtypeStruct((half, width), F32),
-            jax.ShapeDtypeStruct((half, width), F32),
-            jax.ShapeDtypeStruct((half, width), BF),
-            jax.ShapeDtypeStruct((half, width), BF),
+            jax.ShapeDtypeStruct((rows, width), BF),
+            jax.ShapeDtypeStruct((2, half, width), F32),
+            jax.ShapeDtypeStruct((2, half, width), BF),
         ],
         compiler_params=pltpu.CompilerParams(vmem_limit_bytes=40 * MIB),
         cost_estimate=pl.CostEstimate(
             flops=flops, bytes_accessed=16 * MIB, transcendentals=rows * 2 * half * H
         ),
-    )(h, q, kv_a, kv_b, kv_a, kv_b, d, lse)
+    )(h, q, kv_a, kv_b, kv_a, kv_b, d, lse, cosine, sine)
 
 
 def pick_matrix(meta, col, capacity):
@@ -315,7 +386,7 @@
         col = 2 * e_ref[0] + x
         picks, weights = [], []
         for j in range(2):
-            pick = pick_matrix(gs[j][:, width:], col, c)
+            pick = pick_matrix(xs[j][:, width:], total + col, c)
             picks.append(pick)
             rows = dot(pick, xs[j][...], (0, 0))
             xr_ref[x, 0, j * c : (j + 1) * c, :] = rows[:, :width].astype(BF)
@@ -354,12 +425,12 @@
         dxs[j][:, width:] = metas[j].astype(BF)
 
 
-def expert_out_kernel(capacity, e_ref, g0_ref, g1_ref, wa_ref, sa_ref, *refs):
+def expert_out_kernel(capacity, total, e_ref, x0_ref, x1_ref, wa_ref, sa_ref, *refs):
     downs, sd_ref, outs = refs[0:4], refs[4], refs[5:7]
     width = sd_ref.shape[1]
-    tokens = g0_ref.shape[0]
+    tokens = x0_ref.shape[0]
     c = capacity
-    gs = (g0_ref, g1_ref)
+    xs = (x0_ref, x1_ref)
     shared = dot(sa_ref[0], sd_ref[...])
     totals = [shared[:tokens], shared[tokens:]]
     for x in range(2):
@@ -368,7 +439,7 @@
             rows = rows + dot(wa_ref[r, x, 0], downs[r][x])
         rows = rows.astype(BF)
         for j in range(2):
-            pick = pick_matrix(gs[j][...], 2 * e_ref[0] + x, c)
+            pick = pick_matrix(xs[j][...], total + 2 * e_ref[0] + x, c)
             totals[j] = totals[j] + dot(pick, rows[j * c : (j + 1) * c])
     for j in range(2):
         outs[j][...] = totals[j].astype(BF)
@@ -429,14 +500,14 @@
     return outs[0:2], outs[2:4], outs[4:]
 
 
-def expert_out(k, capacity, e, g_pair, wa, sa, downs, sd):
-    tokens = g_pair[0].shape[0]
+def expert_out(k, capacity, total, e, x_pair, wa, sa, downs, sd):
+    tokens = x_pair[0].shape[0]
     width = sd.shape[1]
     c2 = wa.shape[3]
-    last = g_pair[0].shape[1] // LANES - 1
+    last = x_pair[0].shape[1] // LANES - 1
     meta = pl.BlockSpec((tokens, LANES), lambda i, e: (0, last))
     return pl.pallas_call(
-        functools.partial(expert_out_kernel, capacity),
+        functools.partial(expert_out_kernel, capacity, total),
         grid_spec=pltpu.PrefetchScalarGridSpec(
             num_scalar_prefetch=1,
             grid=(1,),
@@ -455,19 +526,19 @@
         cost_estimate=pl.CostEstimate(
             flops=4 * c2 * width * 4 * wa.shape[4], bytes_accessed=10 * MIB, transcendentals=0
         ),
-    )(e, *g_pair, wa, sa, *downs, sd)
-
-
-def dispatch_kernel(capacity, total, x_ref, g_ref, *refs):
-    gates, ups, downs = refs[0:4], refs[4:8], refs[8:12]
-    sg_ref, su_ref, sd_ref = refs[12:15]
-    dx_ref, out_ref, sgg_ref, sdg_ref, xr_ref, gr_ref, gu_ref, wa_ref = refs[15:23]
-    xbuf, sbuf, tbuf, wgu, wd, bounce = refs[23:29]
-    rx_s, rx_r, sx_s, sx_r, sr_s, sr_r, rt_s, rt_r, w_sem, d_sem = refs[29:]
+    )(e, *x_pair, wa, sa, *downs, sd)
+
+
+def dispatch_kernel(capacity, total, x_ref, g0_ref, g1_ref, *refs):
+    experts = refs[0:4]
+    sg_ref, su_ref, sd_ref = refs[4:7]
+    dx_ref, near_ref, far_ref, sgg_ref, sdg_ref, xr_ref, gr_ref, gu_ref, wa_ref = refs[7:16]
+    xbuf, sbuf, tbuf, wgu, wd = refs[16:21]
+    rx_s, rx_r, sx_s, sx_r, sr_s, sr_r, rt_s, rt_r, w_sem = refs[21:]
     k = pl.program_id(0)
     stages = xbuf.shape[0]
     tokens, width = x_ref.shape[0], sg_ref.shape[0]
-    hidden = gates[0].shape[2]
+    hidden = experts[0].shape[1] // 3
     wide = wd.shape[1] // 4
     c = capacity
     e, h = lax.axis_index("ep"), lax.axis_index("hp")
@@ -509,42 +580,20 @@
         ring_x(0).start()
         swap_x(0).start()
         rest = wide - hidden
-        down_copies = []
-        for r in range(4):
-            for x in range(2):
-                copy = pltpu.make_async_copy(
-                    downs[r].at[x],
-                    wd.at[x, pl.ds(r * wide, hidden), :],
-                    d_sem.at[2 * r + x],
-                )
-                copy.start()
-                down_copies.append(copy)
-        todo = [
-            (v[r], x, 2 * r + i)
-            for x in range(2)
-            for r in range(4)
-            for i, v in enumerate((gates, ups))
-        ]
-        slots = bounce.shape[0]
-
-        def load(i):
-            ref, x, _ = todo[i]
-            return pltpu.make_async_copy(ref.at[x], bounce.at[i % slots], w_sem.at[i % slots])
-
-        for i in range(slots):
-            load(i).start()
-        for i, (_, x, at) in enumerate(todo):
-            load(i).wait()
-            wgu[x, :, at * wide : (at + 1) * wide] = jnp.concatenate(
-                [bounce[i % slots], jnp.zeros((width, rest), BF)], axis=1
-            )
-            if i + slots < len(todo):
-                load(i + slots).start()
-        for copy in down_copies:
+        copies = []
+        for x in range(2):
+            for r in range(4):
+                for i, (to, at) in enumerate(((wgu, 2 * r), (wgu, 2 * r + 1), (wd, r))):
+                    copy = pltpu.make_async_copy(
+                        experts[r].at[x, pl.ds(i * hidden, hidden), :],
+                        to.at[x, pl.ds(at * wide, hidden), :],
+                        w_sem.at[len(copies)],
+                    )
+                    copy.start()
+                    copies.append(copy)
+                    to[x, at * wide + hidden : (at + 1) * wide, :] = jnp.zeros((rest, width), BF)
+        for copy in copies:
             copy.wait()
-        for r in range(4):
-            for x in range(2):
-                wd[x, r * wide + hidden : (r + 1) * wide, :] = jnp.zeros((rest, width), BF)
         sgg_ref[...] = jnp.zeros_like(sgg_ref)
         sdg_ref[...] = jnp.zeros_like(sdg_ref)
 
@@ -563,7 +612,8 @@
     swap_x(k).wait_recv()
 
     x2 = jnp.concatenate([xbuf[k, j, :, :width] for j in range(2)], axis=0)
-    g2 = jnp.concatenate([g_ref[0, j, :, :width] for j in range(2)], axis=0)
+    gs = (g0_ref, g1_ref)
+    g2 = jnp.concatenate([g[0] for g in gs], axis=0)
     hg, hu = dot(x2, sg_ref[...]), dot(x2, su_ref[...])
     ab = dot(g2, sd_ref[...], (1, 1))
     s = jax.nn.sigmoid(hg)
@@ -583,20 +633,18 @@
         col = 2 * e + x
         picks, weights = [], []
         for j in range(2):
-            pick = pick_matrix(g_ref[0, j, :, width:], col, c)
+            pick = pick_matrix(xbuf[k, j, :, width:], total + col, c)
             picks.append(pick)
             rows = dot(pick, xbuf[k, j], (0, 0))
             xr_ref[x, 0, j * c : (j + 1) * c, :] = rows[:, :width].astype(BF)
             weights.append(rows[:, width:])
-            gr_ref[x, 0, j * c : (j + 1) * c, :] = dot(
-                pick, g_ref[0, j, :, :width], (0, 0)
-            ).astype(BF)
+            gr_ref[x, 0, j * c : (j + 1) * c, :] = dot(pick, gs[j][0], (0, 0)).astype(BF)
         w = jnp.concatenate(weights, axis=0)
         w = jnp.sum(jnp.where(lane == col, w, 0.0), axis=1, keepdims=True)
         xr, gr = xr_ref[x, 0], gr_ref[x, 0]
         wb = jnp.zeros((2 * c, 1), F32)
         for r in range(4):
-            hgu = dot(xr, wgu[x, :, 2 * r * wide : 2 * (r + 1) * wide])
+            hgu = dot(xr, wgu[x, 2 * r * wide : 2 * (r + 1) * wide, :], (1, 1))
             ab = dot(gr, wd[x, r * wide : (r + 1) * wide, :], (1, 1))
             hg, hu = hgu[:, :wide], hgu[:, wide:]
             s = jax.nn.sigmoid(hg)
@@ -608,7 +656,7 @@
             gu_ref[x, 0, :, at : at + wide] = (ab * hu * (s * (1.0 + hg * (1.0 - s)))).astype(BF)
             gu_ref[x, 0, :, at + wide : at + 2 * wide] = (ab * silu).astype(BF)
             wa_ref[x, 0, :, r * wide : (r + 1) * wide] = (act * w).astype(BF)
-        dxr = dot(gu_ref[x, 0], wgu[x], (1, 1)).astype(BF)
+        dxr = dot(gu_ref[x, 0], wgu[x]).astype(BF)
         rows = dot(wa_ref[x, 0], wd[x]).astype(BF)
         high = wb.astype(BF).astype(F32)
         meta = jnp.where(lane == col, high, 0.0) + jnp.where(lane == total + col, wb - high, 0.0)
@@ -627,7 +675,7 @@
     for j in range(2):
         xbuf[k, j, :, :width] = totals[j].astype(BF)
         xbuf[k, j, :, width:] = metas[j].astype(BF)
-        out_ref[0, j] = outs[j].astype(BF)
+        (near_ref, far_ref)[j][0] = outs[j].astype(BF)
 
     @pl.when(k >= 1)
     def _():
@@ -663,10 +711,11 @@
             ring_t(i).wait_send()
 
 
-def dispatch(capacity, total, x_ext, g_all, gates, ups, downs, sg, su, sd):
-    stages, _, tokens, ext = g_all.shape
+def dispatch(capacity, total, x_ext, g_near, g_far, experts, sg, su, sd):
+    stages = g_near.shape[0]
+    tokens, ext = x_ext.shape
     width, shared = sg.shape
-    hidden = gates[0].shape[2]
+    hidden = experts[0].shape[1] // 3
     wide = -(-hidden // LANES) * LANES
     c2 = 2 * capacity
     once = pl.Buffered(1)
@@ -683,13 +732,15 @@
         grid=(stages,),
         in_specs=[
             fixed((tokens, ext)),
-            pl.BlockSpec((1, 2, tokens, ext), lambda k: (k, 0, 0, 0)),
+            pl.BlockSpec((1, tokens, width), lambda k: (k, 0, 0)),
+            pl.BlockSpec((1, tokens, width), lambda k: (k, 0, 0)),
         ]
-        + [anywhere] * 12
+        + [anywhere] * 4
         + [fixed(sg.shape), fixed(su.shape), fixed(sd.shape)],
         out_specs=[
             fixed((tokens, ext)),
-            pl.BlockSpec((1, 2, tokens, width), lambda k: (k, 0, 0, 0), pipeline_mode=once),
+            pl.BlockSpec((1, tokens, width), lambda k: (k, 0, 0), pipeline_mode=once),
+            pl.BlockSpec((1, tokens, width), lambda k: (k, 0, 0), pipeline_mode=once),
             fixed((width, 2 * shared)),
             fixed((shared, width)),
             per_stage((2, 1, c2, width)),
@@ -699,7 +750,8 @@
         ],
         out_shape=[
             jax.ShapeDtypeStruct((tokens, ext), F32),
-            jax.ShapeDtypeStruct((stages, 2, tokens, width), BF),
+            jax.ShapeDtypeStruct((stages, tokens, width), BF),
+            jax.ShapeDtypeStruct((stages, tokens, width), BF),
             jax.ShapeDtypeStruct((width, 2 * shared), F32),
             jax.ShapeDtypeStruct((shared, width), F32),
             jax.ShapeDtypeStruct((2, stages, c2, width), BF),
@@ -711,12 +763,11 @@
             pltpu.VMEM((stages, 2, tokens, ext), BF),
             pltpu.VMEM((stages, tokens, ext), BF),
             pltpu.VMEM((stages, tokens, ext), BF),
-            pltpu.VMEM((2, width, 8 * wide), BF),
+            pltpu.VMEM((2, 8 * wide, width), BF),
             pltpu.VMEM((2, 4 * wide, width), BF),
-            pltpu.VMEM((2, width, hidden), BF),
         ]
         + [pltpu.SemaphoreType.DMA((stages,))] * 8
-        + [pltpu.SemaphoreType.DMA((2,)), pltpu.SemaphoreType.DMA((8,))],
+        + [pltpu.SemaphoreType.DMA((24,))],
         compiler_params=pltpu.CompilerParams(
             vmem_limit_bytes=63 * MIB, collective_id=0, has_side_effects=True
         ),
@@ -725,7 +776,426 @@
             bytes_accessed=80 * MIB,
             transcendentals=stages * c2 * 8 * hidden,
         ),
-    )(x_ext, g_all, *gates, *ups, *downs, sg, su, sd)
+    )(x_ext, g_near, g_far, *experts, sg, su, sd)
+
+
+def mesh_copy(src, dst, s, r, i, where):
+    return pltpu.make_async_remote_copy(
+        src_ref=src,
+        dst_ref=dst,
+        send_sem=s.at[i],
+        recv_sem=r.at[i],
+        device_id=where,
+        device_id_type=pl.DeviceIdType.MESH,
+    )
+
+
+def greet(peers):
+    barrier = pltpu.get_barrier_semaphore()
+    for where in peers:
+        pl.semaphore_signal(barrier, inc=1, device_id=where, device_id_type=pl.DeviceIdType.MESH)
+    pl.semaphore_wait(barrier, len(peers))
+
+
+def front_kernel(large, count, *refs):
+    tok_ref, exp_ref, cot_ref = refs[0:3]
+    ins = refs[3 : 3 + count]
+    far_ref, expo_ref, g_ref = refs[3 + count : 6 + count]
+    outs = refs[6 + count : 6 + 2 * count]
+    y_s, y_r, c_s, c_r, f_s, f_r, p_s, p_r, q_s, q_r, l_sem, rg_s, rg_r = refs[6 + 2 * count :]
+    stages = g_ref.shape[0]
+    n = 2 * stages
+    e, h = lax.axis_index("ep"), lax.axis_index("hp")
+    x = lax.rem(e, 2)
+    h_core, h_far = h + 1 - 2 * lax.rem(h, 2), lax.rem(h + 2, 4)
+    core, far = (e, h_core), (e, h_far)
+    right, left = (lax.rem(e + 2, n), h), (lax.rem(e + n - 2, n), h)
+    pair = (e + 1 - 2 * x, h)
+    greet((core, far, right, left, pair))
+
+    def ring_g(k):
+        src = cot_ref if k == 0 else g_ref.at[k]
+        return mesh_copy(src, g_ref.at[k + 1], rg_s, rg_r, k, right)
+
+    def part(i, other=False):
+        rows = ins[i].shape[0] // 2
+        return pl.ds((1 - x if other else x) * rows, rows)
+
+    over_y, over_pair, onward, onward_too = [], [], [], []
+    for i, v in enumerate(ins):
+        o = outs[i]
+        if i < large:
+            mine, theirs = part(i), part(i, True)
+            over_y.append(mesh_copy(v.at[mine], o.at[h, mine], y_s, y_r, i, far))
+            got, rest = o.at[h_far, mine], o.at[h_far, theirs]
+            over_pair.append(mesh_copy(got, got, p_s, p_r, i, pair))
+            onward.append(mesh_copy(got, got, f_s, f_r, i, core))
+            onward_too.append(mesh_copy(rest, rest, q_s, q_r, i, core))
+        else:
+            over_y.append(mesh_copy(v, o.at[h], y_s, y_r, i, far))
+            onward.append(mesh_copy(o.at[h_far], o.at[h_far], f_s, f_r, i, core))
+    over_y.append(mesh_copy(tok_ref, far_ref, y_s, y_r, count, far))
+    over_core = [mesh_copy(v, outs[i].at[h], c_s, c_r, i, core) for i, v in enumerate(ins)]
+    over_core.append(mesh_copy(exp_ref, expo_ref, c_s, c_r, count, core))
+    local = [pltpu.make_async_copy(v, outs[i].at[h], l_sem.at[i]) for i, v in enumerate(ins)]
+    local.append(pltpu.make_async_copy(cot_ref, g_ref.at[0], l_sem.at[count]))
+    for copy in over_y:
+        copy.start()
+    ring_g(0).start()
+    for copy in over_core + local:
+        copy.start()
+    for k in range(max(stages - 1, large)):
+        if k < large:
+            over_y[k].wait_recv()
+            over_pair[k].start()
+            onward[k].start()
+        if k < stages - 1:
+            ring_g(k).wait_recv()
+            if k + 1 < stages - 1:
+                ring_g(k + 1).start()
+    for k in range(large, count):
+        over_y[k].wait_recv()
+        onward[k].start()
+    over_y[count].wait_recv()
+    for k in range(large):
+        over_pair[k].wait_recv()
+        onward_too[k].start()
+    for copy in over_y + over_pair + [ring_g(k) for k in range(stages - 1)]:
+        copy.wait_send()
+    for copy in over_core + onward + onward_too + local:
+        copy.wait()
+
+
+def front(stages, tokens, experts, cotangent, blocks, large):
+    count = len(blocks)
+    anywhere, vmem = (pl.BlockSpec(memory_space=m) for m in (pl.ANY, pltpu.VMEM))
+    dma = pltpu.SemaphoreType.DMA
+    return pl.pallas_call(
+        functools.partial(front_kernel, large, count),
+        in_specs=[anywhere] * 2 + [vmem] * (1 + count),
+        out_specs=[anywhere] * (3 + count),
+        out_shape=[
+            jax.ShapeDtypeStruct(tokens.shape, BF),
+            jax.ShapeDtypeStruct(experts.shape, BF),
+            jax.ShapeDtypeStruct((stages,) + cotangent.shape, BF),
+        ]
+        + [jax.ShapeDtypeStruct((4,) + v.shape, BF) for v in blocks],
+        scratch_shapes=[dma((count + 1,))] * 4
+        + [dma((count,))] * 6
+        + [dma((count + 1,))]
+        + [dma((stages,))] * 2,
+        compiler_params=pltpu.CompilerParams(
+            vmem_limit_bytes=32 * MIB, collective_id=1, has_side_effects=True
+        ),
+        cost_estimate=pl.CostEstimate(flops=0, bytes_accessed=120 * MIB, transcendentals=0),
+    )(tokens, experts, cotangent, *blocks)
+
+
+def tail_kernel(
+    m0,
+    m1,
+    m2,
+    m3,
+    sg_ref,
+    sd_ref,
+    sm_ref,
+    fb_ref,
+    tok_ref,
+    gain_ref,
+    first_ref,
+    mid_ref,
+    spread_ref,
+    stack_ref,
+    out_ref,
+    sgout_ref,
+    suout_ref,
+    sdout_ref,
+    smout_ref,
+    tokout_ref,
+    crecv,
+    ysend,
+    yrecv,
+    acc,
+    xrecv,
+    zrecv,
+    fin,
+    sg_c,
+    sg_y,
+    sg_yr,
+    sg_fin,
+    sd_c,
+    sd_y,
+    sd_yr,
+    sd_fin,
+    g_acc,
+    g_recv,
+    f_recv,
+    c_s,
+    c_r,
+    y_s,
+    y_r,
+    x_s,
+    x_r,
+    z_s,
+    z_r,
+    za_s,
+    za_r,
+    xa_s,
+    xa_r,
+    s_s,
+    s_r,
+    d_s,
+    d_r,
+    g_s,
+    g_r,
+    f_s,
+    f_r,
+):
+    mats = (m0, m1, m2, m3)
+    chunks, part = acc.shape[0], acc.shape[3]
+    half = m0.shape[3]
+    e, h = lax.axis_index("ep"), lax.axis_index("hp")
+    x, z = lax.rem(e, 2), e // 2
+    c, y = lax.rem(h, 2), h // 2
+    core, far = (e, h + 1 - 2 * c), (e, lax.rem(h + 2, 4))
+    pair = (e + 1 - 2 * x, h)
+    up = [None] + [(2 * lax.rem(z + s, 4) + x, h) for s in range(1, 4)]
+    next_z = (2 * (z + 1 - 2 * lax.rem(z, 2)) + x, h)
+    greet([core, far, pair] + up[1:])
+
+    def rows(j):
+        return pl.ds(j * part, part)
+
+    def over_core(j, m):
+        return mesh_copy(
+            mats[m].at[:, 1 - c, :, rows(j), :],
+            crecv.at[m, :, :, rows(j), :],
+            c_s,
+            c_r,
+            4 * j + m,
+            core,
+        )
+
+    def over_y(j):
+        return mesh_copy(ysend.at[j], yrecv.at[j], y_s, y_r, j, far)
+
+    def over_x(j):
+        return mesh_copy(acc.at[j, :, 1 - x], xrecv.at[j], x_s, x_r, j, pair)
+
+    def over_z(j, s):
+        return mesh_copy(
+            acc.at[j, lax.rem(z + s, 4), x], zrecv.at[j, s - 1], z_s, z_r, 3 * j + s - 1, up[s]
+        )
+
+    def back_z(j, s):
+        return mesh_copy(fin.at[j, z, x], fin.at[j, z, x], za_s, za_r, 3 * j + s - 1, up[s])
+
+    def back_x(j):
+        return mesh_copy(fin.at[j, :, x], fin.at[j, :, x], xa_s, xa_r, j, pair)
+
+    def add_core(j):
+        for m in range(4):
+            over_core(j, m).wait_recv()
+            for at, to in ((y, acc), (1 - y, ysend)):
+                total = mats[m][at, c, :, rows(j), :].astype(F32)
+                to[j, m] = (total + crecv[m, at, :, rows(j), :].astype(F32)).astype(BF)
+        over_y(j).start()
+
+    def add_y(j):
+        over_y(j).wait_recv()
+        acc[j] = (acc[j].astype(F32) + yrecv[j].astype(F32)).astype(BF)
+        over_x(j).start()
+
+    def add_x(j):
+        over_x(j).wait_recv()
+        acc[j, :, x] = (acc[j, :, x].astype(F32) + xrecv[j].astype(F32)).astype(BF)
+        for s in range(1, 4):
+            over_z(j, s).start()
+
+    def add_z(j):
+        total = acc[j, z, x].astype(F32)
+        for s in range(1, 4):
+            over_z(j, s).wait_recv()
+            total = total + zrecv[j, s - 1].astype(F32)
+        fin[j, z, x] = total.astype(BF)
+        for s in range(1, 4):
+            back_z(j, s).start()
+
+    def end_z(j):
+        for s in range(1, 4):
+            back_z(j, s).wait_recv()
+        back_x(j).start()
+
+    def end_x(j):
+        back_x(j).wait_recv()
+        for m in range(4):
+            for i in range(2):
+                out_ref[m, i * half + j * part : i * half + (j + 1) * part, :] = fin[j, m, i]
+
+    class Flow:
+        def __init__(self, ref, got, to_far, from_far, fin, s, r):
+            self.ref, self.got, self.to_far, self.from_far, self.fin = ref, got, to_far, from_far, fin
+            self.core = mesh_copy(ref.at[:, 1 - c], got, s, r, 0, core)
+            self.far = mesh_copy(to_far, from_far, s, r, 1, far)
+            self.up = [
+                mesh_copy(fin.at[x, z], fin.at[x, z], s, r, 1 + k, up[k]) for k in range(1, 4)
+            ]
+            self.pair = mesh_copy(fin.at[x], fin.at[x], s, r, 5, pair)
+            self.all = [self.core, self.far, self.pair] + self.up
+
+        def step(self, t):
+            if t == 0:
+                self.core.wait_recv()
+                total = self.ref[1 - y, c].astype(F32) + self.got[1 - y].astype(F32)
+                self.to_far[...] = total.astype(BF)
+                self.far.start()
+            if t == 2:
+                self.far.wait_recv()
+                total = self.ref[y, c].astype(F32) + self.got[y].astype(F32)
+                self.fin[x, z] = (total + self.from_far[...].astype(F32)).astype(BF)
+                for copy in self.up:
+                    copy.start()
+            if t == 4:
+                for copy in self.up:
+                    copy.wait_recv()
+                self.pair.start()
+
+    flows = [
+        Flow(sg_ref, sg_c, sg_y, sg_yr, sg_fin, s_s, s_r),
+        Flow(sd_ref, sd_c, sd_y, sd_yr, sd_fin, d_s, d_r),
+    ]
+    route = (core, far, pair, next_z, up[2])
+    small = [
+        mesh_copy(g_acc.at[i], g_recv.at[i], g_s, g_r, i, route[i]) for i in range(len(route))
+    ]
+    back = mesh_copy(fb_ref, f_recv, f_s, f_r, 0, far)
+
+    def side(t):
+        for flow in flows:
+            flow.step(t)
+        if t < len(small):
+            small[t].wait_recv()
+            g_acc[t + 1] = g_acc[t] + g_recv[t]
+            if t + 1 < len(small):
+                small[t + 1].start()
+        if t == 6:
+            back.wait_recv()
+            first_back = first_ref[...] + f_recv[...].astype(F32)
+            values = tok_ref[...].astype(F32)
+            to_tokens = norm_back(values, rms(values), gain_ref[...], first_back)
+            tokout_ref[...] = mid_ref[...] + to_tokens
+        if t == 8:
+            for flow in flows:
+                flow.pair.wait_recv()
+            lanes = sg_fin.shape[3] // 2
+            gate = up_ = down = 0.0
+            for k in range(8):
+                block = sg_fin[k % 2, k // 2]
+                gate = gate + dot(block[:, :lanes], spread_ref[k])
+                up_ = up_ + dot(block[:, lanes:], spread_ref[k])
+                down = down + dot(stack_ref[k], sd_fin[k % 2, k // 2])
+            sgout_ref[...] = gate
+            suout_ref[...] = up_
+            sdout_ref[...] = down
+
+    g_acc[0] = sm_ref[...]
+    for m in range(4):
+        over_core(0, m).start()
+    back.start()
+    for flow in flows:
+        flow.core.start()
+    small[0].start()
+    for j in range(1, chunks):
+        for m in range(4):
+            over_core(j, m).start()
+    steps = (add_core, add_y, add_x, add_z, end_z, end_x)
+    for t in range(chunks + len(steps) - 1):
+        for p in reversed(range(len(steps))):
+            if 0 <= t - p < chunks:
+                steps[p](t - p)
+        side(t)
+    smout_ref[...] = g_acc[len(small)]
+    back.wait_send()
+    for copy in flows[0].all + flows[1].all + small:
+        copy.wait_send()
+    for j in range(chunks):
+        for m in range(4):
+            over_core(j, m).wait_send()
+        for copy in (over_y(j), over_x(j), back_x(j)):
+            copy.wait_send()
+        for s in range(1, 4):
+            over_z(j, s).wait_send()
+            back_z(j, s).wait_send()
+
+
+def tail(mats, sgg, sdg, small, share, tokens, gain, first_back, middle_back, spread, stack):
+    width = mats[0].shape[1]
+    half = width // 8
+    part = 16
+    chunks = half // part
+    dma = pltpu.SemaphoreType.DMA
+    vmem = pl.BlockSpec(memory_space=pltpu.VMEM)
+
+    def buffers(shape):
+        return [
+            pltpu.VMEM((2,) + shape, BF),
+            pltpu.VMEM(shape, BF),
+            pltpu.VMEM(shape, BF),
+            pltpu.VMEM((2, 4) + shape, BF),
+        ]
+
+    return pl.pallas_call(
+        tail_kernel,
+        in_specs=[vmem] * 14,
+        out_specs=[vmem] * 6,
+        out_shape=[
+            jax.ShapeDtypeStruct((4, 2 * half, width), BF),
+            jax.ShapeDtypeStruct((2 * half, spread.shape[2]), F32),
+            jax.ShapeDtypeStruct((2 * half, spread.shape[2]), F32),
+            jax.ShapeDtypeStruct((stack.shape[1], width), F32),
+            jax.ShapeDtypeStruct(small.shape, F32),
+            jax.ShapeDtypeStruct(tokens.shape, F32),
+        ],
+        scratch_shapes=[
+            pltpu.VMEM((4, 2, 2, half, width), BF),
+            pltpu.VMEM((chunks, 4, 2, part, width), BF),
+            pltpu.VMEM((chunks, 4, 2, part, width), BF),
+            pltpu.VMEM((chunks, 4, 2, part, width), BF),
+            pltpu.VMEM((chunks, 4, part, width), BF),
+            pltpu.VMEM((chunks, 3, part, width), BF),
+            pltpu.VMEM((chunks, 4, 2, part, width), BF),
+        ]
+        + buffers(sgg.shape[2:])
+        + buffers(sdg.shape[2:])
+        + [
+            pltpu.VMEM((6,) + small.shape, F32),
+            pltpu.VMEM((5,) + small.shape, F32),
+            pltpu.VMEM(share.shape, BF),
+        ]
+        + [dma((4 * chunks,))] * 2
+        + [dma((chunks,))] * 4
+        + [dma((3 * chunks,))] * 4
+        + [dma((chunks,))] * 2
+        + [dma((6,))] * 4
+        + [dma((5,))] * 2
+        + [dma((1,))] * 2,
+        compiler_params=pltpu.CompilerParams(
+            vmem_limit_bytes=62 * MIB, collective_id=2, has_side_effects=True
+        ),
+        cost_estimate=pl.CostEstimate(flops=0, bytes_accessed=300 * MIB, transcendentals=0),
+    )(
+        *[m.reshape(2, 2, 2, half, width) for m in mats],
+        sgg,
+        sdg,
+        small,
+        share,
+        tokens,
+        gain,
+        first_back,
+        middle_back,
+        spread,
+        stack,
+    )
 
 
 def rms(values):
@@ -735,22 +1205,14 @@
 def norm_back(values, inv, gain, upstream):
     weighted = upstream * gain
     inner = jnp.mean(weighted * values, axis=-1, keepdims=True)
-    to_input = weighted * inv - values * (inv * inv * inv * inner)
-    return to_input, jnp.sum(upstream * values * inv, axis=0)
-
-
-def half_turn(v):
-    lane = lax.broadcasted_iota(jnp.int32, v.shape, 1)
-    return jnp.where(
-        lane % HD < HD // 2, -jnp.roll(v, -HD // 2, axis=1), jnp.roll(v, HD // 2, axis=1)
-    )
+    return weighted * inv - values * (inv * inv * inv * inner)
 
 
 def rotary_tables(positions):
     exponent = jnp.arange(HD // 2, dtype=F32) * (2.0 / HD)
     theta = positions.astype(F32)[:, None] * jnp.power(10000.0, -exponent)[None, :]
-    theta = jnp.concatenate([theta, theta], axis=-1)
-    return jnp.tile(jnp.cos(theta), (1, H)), jnp.tile(jnp.sin(theta), (1, H))
+    cosine, sine = jnp.cos(theta), jnp.sin(theta)
+    return jnp.concatenate([cosine, cosine], axis=1), jnp.concatenate([-sine, sine], axis=1)
 
 
 def per_device(
@@ -781,14 +1243,8 @@
     capacity = -(-(5 * rows * top // (4 * total)) // 16) * 16
     e_arr, h_arr = jnp.full((1,), e, jnp.int32), jnp.full((1,), h, jnp.int32)
 
-    far_tokens = swap_y(tokens)
-    k_w, v_w = gather_hp(key_weight), gather_hp(value_weight)
-    q_w = gather_hp(query_weight)
-    o_w = gather_hp(after(out_weight, q_w[2], k_w[2], v_w[2]))
-    gates, ups, downs = (
-        gather_hp(after(v, o_w[2])) for v in (expert_gate, expert_up, expert_down)
-    )
     units = shared_down.shape[0] // ep
+    pad = -(-units // 16) * 16
     tiny = [attn_gain[:, None], ffn_gain[:, None], router_weight]
     small = jnp.concatenate(tiny + [jnp.zeros((width // 4, LANES - 2 - total), BF)], axis=1)
 
@@ -798,14 +1254,30 @@
         return jnp.pad(v, ((0, 0), (0, LANES - 4 * units)))
 
     small = jnp.concatenate([small, mine(shared_gate), mine(shared_up)], axis=1)
-    small = jnp.concatenate(gather_hp(small), axis=0)
+    sd = lax.dynamic_slice_in_dim(shared_down, e * units, units, axis=0)
+    sd = jnp.pad(sd, ((0, pad - units), (0, 0)))
+    blocks = [key_weight, value_weight, query_weight, out_weight, small, sd]
+    experts = jnp.concatenate(
+        [jnp.swapaxes(expert_gate, 1, 2), jnp.swapaxes(expert_up, 1, 2), expert_down], axis=1
+    )
+    fused = stages == 4
+    if fused:
+        far_tokens, experts_core, g_near, *blocks = front(
+            stages, tokens, experts, cotangent, blocks, 4
+        )
+        experts_far = swap_y(after(experts, blocks[0]))
+        g_far = swap_pair(g_near)
+    else:
+        far_tokens = swap_y(tokens)
+        blocks = [absolute(jnp.stack(gather_hp(v)), h, 0) for v in blocks]
+        g_blocks = gather_ep(cotangent)
+        experts = gather_hp(experts)
+    k_w, v_w, q_w, o_w, small = (v.reshape(width, v.shape[2]) for v in blocks[:5])
     gain_one = small[:, 0].astype(F32)[None, :]
-    small = relative(small, h, 0)
     gain_two = small[:, 1].astype(F32)[None, :]
     router = small[:, 2 : 2 + total]
     sg, su = small[:, LANES : 2 * LANES], small[:, 2 * LANES :]
-    sd = lax.dynamic_slice_in_dim(shared_down, e * units, units, axis=0)
-    sd = relative(jnp.concatenate(gather_hp(sd), axis=0), h, 0)
+    sd = blocks[5][:, :units].reshape(4 * units, width)
     sd = jnp.pad(sd, ((0, LANES - 4 * units), (0, 0)))
 
     expert = jnp.arange(total, dtype=jnp.int32)
@@ -815,40 +1287,16 @@
     below = (jnp.arange(rows)[:, None] > jnp.arange(rows)[None, :]).astype(BF)
     place = jnp.where(hit, dot(below, hit.astype(BF)), -1.0)
     kept = kept.astype(F32)
-    g_ext = jnp.concatenate(
-        [
-            cotangent,
-            place.astype(BF),
-            jnp.zeros((rows, LANES - total), BF),
-        ],
-        axis=1,
-    )
-    g_blocks = gather_ep(g_ext)
 
     pos = jnp.arange(rows, dtype=jnp.int32)
-    pos = jnp.concatenate([h * rows + pos, (h ^ 2) * rows + pos])
+    pos = jnp.concatenate([(h ^ i) * rows + pos for i in (0, 2, 1, 3)])
     cosine, sine = rotary_tables(pos)
     residual = tokens.astype(F32)
-    both = relative(jnp.concatenate([tokens, far_tokens], axis=0), h, 1).astype(F32)
-    inv_one = rms(both)
-    first_in = after((both * inv_one * gain_one).astype(BF), g_blocks)
-
-    def rotate(v, n):
-        return v * cosine[:n] + half_turn(v) * sine[:n]
-
-    def rotate_back(v, n):
-        return v * cosine[:n] - half_turn(v * sine[:n])
-
-    k_w, v_w = jnp.concatenate(k_w, axis=0), jnp.concatenate(v_w, axis=0)
-    q_w, o_w = jnp.concatenate(q_w, axis=0), jnp.concatenate(o_w, axis=0)
-    keys = rotate(dot(first_in, k_w), 2 * rows).astype(BF)
-    values = dot(first_in, v_w).astype(BF)
-    kv_a = jnp.concatenate([keys, values], axis=1)
+    table = cosine[: 2 * rows], sine[: 2 * rows]
+    first_in, kv_a, query = project(tokens, far_tokens, gain_one, k_w, v_w, q_w, *table)
     kv_b = swap_core(kv_a)
-    query = rotate(dot(first_in[:rows], q_w), rows).astype(BF)
     mixed, lse = attend(h_arr, query, kv_a, kv_b)
-    mixed_rel = relative(mixed, h, 1)
-    middle = residual + dot(mixed_rel, o_w)
+    middle = residual + dot(mixed, o_w)
     inv_two = rms(middle)
     second_in = (middle * inv_two * gain_two).astype(BF)
 
@@ -857,32 +1305,56 @@
     gates_of = gates_of / jnp.sum(gates_of, axis=1, keepdims=True)
     pair_weight = gates_of * kept
     x_ext = jnp.concatenate(
-        [second_in, pair_weight.astype(BF), jnp.zeros((rows, LANES - total), BF)], axis=1
+        [
+            second_in,
+            pair_weight.astype(BF),
+            place.astype(BF),
+            jnp.zeros((rows, LANES - 2 * total), BF),
+        ],
+        axis=1,
     )
 
     flat = (2, ep * capacity)
+
+    hidden = expert_down.shape[1]
 
     def expert_grad(left, right):
         return jnp.einsum("xna,xnb->xab", left, right, preferred_element_type=F32)
 
-    if stages <= 4:
-        g_all = jnp.stack([jnp.stack(pair) for pair in g_blocks])
-        dx_sum, out_all, sgg, sdg, xr, gr, gu, wa = dispatch(
-            capacity, total, x_ext, g_all, gates, ups, downs, sg, su, sd
+    if fused:
+        experts = [
+            experts,
+            experts_far,
+            experts_core,
+            swap_core(after(experts_far, mixed)),
+        ]
+        dx_sum, near, far, sgg, sdg, xr, gr, gu, wa = dispatch(
+            capacity, total, x_ext, g_near, g_far, experts, sg, su, sd
         )
-        out_parts = [(out_all[k, 0], out_all[k, 1]) for k in range(stages)]
-        hidden, wide = expert_gate.shape[2], wa.shape[3] // 4
+        far = swap_pair(far)
+        wide = wa.shape[3] // 4
         xr, gr, gu, wa = (v.reshape(flat + (v.shape[-1],)) for v in (xr, gr, gu, wa))
-        gu = expert_grad(xr, gu).astype(BF)
+        gu = expert_grad(gu, xr).astype(BF)
         wa = expert_grad(wa, gr).astype(BF)
-        gate_parts, up_parts = (
-            [gu[:, :, at * wide : at * wide + hidden] for at in range(i, 8, 2)] for i in (0, 1)
-        )
-        down_parts = [wa[:, r * wide : r * wide + hidden] for r in range(4)]
+        dx_sum = after(dx_sum, gu, wa)
+
+        def piece(r):
+            starts = ((gu, 2 * r * wide), (gu, (2 * r + 1) * wide), (wa, r * wide))
+            return jnp.concatenate([v[:, a : a + hidden] for v, a in starts], axis=1)
+
+        piece_near = [piece(r) for r in (0, 1)]
+        piece_core = swap_core(jnp.stack([piece(r) for r in (2, 3)]))
+        piece_sum = (piece_near[1].astype(F32) + piece_core[1].astype(F32)).astype(BF)
+        piece_far = swap_y(piece_sum)
     else:
         x_blocks = gather_ep(after(x_ext, g_blocks))
         carry = (jnp.zeros((width, 2 * LANES), F32), jnp.zeros((LANES, width), F32))
         bufs, dx_parts = None, []
+        gates, ups = (
+            [jnp.swapaxes(v[:, i * hidden : (i + 1) * hidden], 1, 2) for v in experts]
+            for i in (0, 1)
+        )
+        downs = [v[:, 2 * hidden :] for v in experts]
         for k in range(stages):
             dx, carry, bufs = expert_stage(
                 k,
@@ -906,30 +1378,25 @@
         sgg, sdg = carry
         sa, xr, gr, gi, ui, wa = bufs
         out_parts = [
-            expert_out(k, capacity, e_arr, g_blocks[k], wa, sa, downs, sd) for k in range(stages)
+            expert_out(k, capacity, total, e_arr, x_blocks[k], wa, sa, downs, sd)
+            for k in range(stages)
         ]
         xr, gr = xr.reshape(flat + (width,)), gr.reshape(flat + (width,))
         gi, ui, wa = (v.reshape((4,) + flat + (v.shape[-1],)) for v in (gi, ui, wa))
-        gate_parts = [expert_grad(xr, gi[r]) for r in range(4)]
-        up_parts = [expert_grad(xr, ui[r]) for r in range(4)]
-        down_parts = [expert_grad(wa[r], gr) for r in range(4)]
-    layer = (middle + scatter_ep(after(out_parts, dx_sum))).astype(BF)
-    gate_grad, up_grad, down_grad = (
-        scatter_hp(parts) for parts in (gate_parts, up_parts, down_parts)
-    )
-
-    sgg = relative(sgg, h, 0)
-    sgg = scatter_hp(jnp.split(sgg, 4, axis=0)).astype(BF)
-    sdg = scatter_hp(jnp.split(relative(sdg[: 4 * units], h, 0), 4, axis=0)).astype(BF)
-    sgg, sdg = (spread_ep(after(v, dx_sum), e) for v in (sgg, sdg))
-    sdg = sdg.reshape(ep * units, width)
-
-    def spread(v):
-        v = v[:, :, : 4 * units].reshape(ep, width // 4, 4, units)
-        return v.transpose(1, 2, 0, 3).reshape(width // 4, 4 * ep * units).astype(F32)
-
-    sgate_grad, sup_grad = spread(sgg[:, :, :LANES]), spread(sgg[:, :, LANES:])
-    sdown_grad = sdg.astype(F32)
+        routed = scatter_ep(after(out_parts, dx_sum))
+        expert_sum = scatter_hp(
+            [
+                jnp.concatenate(
+                    [
+                        expert_grad(gi[r], xr),
+                        expert_grad(ui[r], xr),
+                        expert_grad(wa[r], gr),
+                    ],
+                    axis=1,
+                )
+                for r in range(4)
+            ]
+        )
 
     grad_out = cotangent.astype(F32)
     weight_back = dx_sum[:, width : width + total] + dx_sum[:, width + total : width + 2 * total]
@@ -938,44 +1405,90 @@
     logits_back = chosen_back.astype(BF)
     router_part = dot(logits_back, second_in, (0, 0))
     second_back = dx_sum[:, :width] + dot(logits_back, router, (1, 1))
-    to_middle, gain_two_part = norm_back(middle, inv_two, gain_two, second_back)
-    middle_back = grad_out + to_middle
+    gain_two_part = jnp.sum(second_back * middle * inv_two, axis=0)
+    middle_back = grad_out + norm_back(middle, inv_two, gain_two, second_back)
     attn_back = middle_back.astype(BF)
-    counts_part = jnp.sum(kept, axis=0)
-    tail = jnp.zeros((1, width - total), F32)
-    sums = jnp.concatenate(
-        [
-            router_part,
-            gain_two_part[None, :],
-            jnp.concatenate([counts_part[None, :], tail], axis=1),
-        ],
-        axis=0,
+    counts_part = jnp.pad(jnp.sum(kept, axis=0), (0, width - total))
+
+    mixed_back = dot(attn_back, o_w, (1, 1)).astype(BF)
+    if fused:
+        mixed_back = after(mixed_back, piece_sum)
+    out_part = dot(mixed, attn_back, (0, 0))
+    query_raw, near_back, far_back = attend_back(
+        h_arr, query, kv_a, kv_b, mixed_back, lse, cosine, sine
     )
-    sums = sum_all_small(sums)
-
-    mixed_back = relative(dot(attn_back, o_w, (1, 1)).astype(BF), h, 1)
-    out_part = dot(mixed_rel, attn_back, (0, 0))
-    out_grad = sum_ep(scatter_hp(jnp.split(out_part, 4, axis=0)), e)
-    dq, dka, dva, dkb, dvb = attend_back(h_arr, query, kv_a, kv_b, mixed_back, lse)
-    dk = dka + swap_core(dkb).astype(F32)
-    dv = dva + swap_core(dvb).astype(F32)
-    query_raw = rotate_back(dq, rows).astype(BF)
-    key_raw = rotate_back(dk, 2 * rows).astype(BF)
-    value_raw = dv.astype(BF)
+    kv_raw = (near_back + swap_core(far_back).astype(F32)).astype(BF)
+    key_raw, value_raw = kv_raw[0], kv_raw[1]
+    if fused:
+        both_out = near.astype(F32) + after(far, query_raw).astype(F32)
+        low_out = both_out.astype(BF)
+        routed = [shift(low_out[k], stages - k) for k in range(1, stages)]
     kv_back = dot(key_raw, k_w, (1, 1)) + dot(value_raw, v_w, (1, 1))
-    from_far = swap_y(kv_back[rows:].astype(BF))
+    q_back = dot(query_raw, q_w, (1, 1))
+    share = kv_back[rows:].astype(BF)
     q_part = dot(first_in[:rows], query_raw, (0, 0))
     k_part = dot(first_in, key_raw, (0, 0))
     v_part = dot(first_in, value_raw, (0, 0))
-    query_grad, key_grad, value_grad = (
-        sum_ep(scatter_hp(jnp.split(v, 4, axis=0)), e) for v in (q_part, k_part, v_part)
+    first_back = kv_back[:rows] + q_back
+    gain_one_part = jnp.zeros((1, width), F32)
+    for values, upstream in ((tokens, first_back), (far_tokens, kv_back[rows:])):
+        values = values.astype(F32)
+        gain_one_part += jnp.sum(upstream * values * rms(values), axis=0, keepdims=True)
+    sums = [router_part, gain_two_part[None, :], counts_part[None, :], gain_one_part]
+    sums = jnp.concatenate(sums + [jnp.zeros((-(total + 3) % 8, width), F32)], axis=0)
+    parts = [q_part, k_part, v_part, out_part]
+
+    sgg = sgg.reshape(4, width // 4, 2 * LANES)
+    sdg = sdg[: 4 * units].reshape(4, units, width)
+    unit = jnp.arange(LANES)
+    to = (unit // units) * (ep * units) + unit % units
+    to = jnp.where(unit < 4 * units, to, -ep * units)[None, :, None]
+    block = jnp.arange(ep)[:, None, None] * units
+    spread = (to + block == jnp.arange(4 * ep * units)[None, None, :]).astype(BF)
+    if fused:
+        sdg = jnp.pad(sdg, ((0, 0), (0, pad - units), (0, 0))).astype(BF)
+        at = jnp.where(jnp.arange(pad) < units, jnp.arange(pad), -ep * units)[None, None, :]
+        stack = (at + block == jnp.arange(ep * units)[None, :, None]).astype(BF)
+        out, sgate_grad, sup_grad, sdown_grad, sums, tokens_grad = tail(
+            [v.astype(BF) for v in parts],
+            sgg.astype(BF).reshape(2, 2, width // 4, 2 * LANES),
+            sdg.reshape(2, 2, pad, width),
+            after(sums, piece_far),
+            share,
+            tokens,
+            gain_one,
+            first_back,
+            middle_back,
+            spread,
+            stack,
+        )
+        grads = [out[i].astype(F32) for i in range(4)]
+        routed = after(routed, sums)
+        routed = both_out[0] + sum(v.astype(F32) for v in routed)
+        piece_far = after(piece_far, sums)
+        expert_sum = sum(v.astype(F32) for v in (piece_near[0], piece_core[0], piece_far))
+    else:
+
+        def over_hp(v):
+            return scatter_hp(jnp.split(relative(v, h, 0), 4, axis=0))
+
+        grads = [sum_ep(over_hp(v), e) for v in parts]
+        sums = sum_all_small(sums)
+        first_back = first_back + swap_y(share).astype(F32)
+        tokens_grad = middle_back + norm_back(residual, rms(residual), gain_one, first_back)
+        sgg, sdg = (
+            spread_ep(over_hp(v)[0].astype(BF), e) for v in (sgg, sdg)
+        )
+        sgate_grad, sup_grad = (
+            jnp.einsum("kra,kan->rn", v, spread, preferred_element_type=F32)
+            for v in (sgg[:, :, :LANES], sgg[:, :, LANES:])
+        )
+        sdown_grad = sdg.reshape(ep * units, width).astype(F32)
+    layer = (middle + routed).astype(BF)
+    gate_grad, up_grad = (
+        jnp.swapaxes(expert_sum[:, i * hidden : (i + 1) * hidden], 1, 2) for i in (0, 1)
     )
-    first_back = dot(query_raw, q_w, (1, 1)) + kv_back[:rows]
-    quarters = jnp.split(from_far.astype(F32), 4, axis=1)
-    first_back = first_back + jnp.concatenate([quarters[i ^ 2] for i in range(4)], axis=1)
-    to_tokens, gain_one_part = norm_back(both[:rows], inv_one[:rows], gain_one, first_back)
-    tokens_grad = middle_back + relative(to_tokens, h, 1)
-    gain_one_grad = sum_all_small(relative(gain_one_part[None, :], h, 1))[0]
+    down_grad = expert_sum[:, 2 * hidden :]
 
     def own(v, n):
         return lax.dynamic_slice_in_dim(v, h * n, n, axis=0)
@@ -983,11 +1496,8 @@
     return (
         layer,
         tokens_grad,
-        own(gain_one_grad, width // 4),
-        query_grad,
-        key_grad,
-        value_grad,
-        out_grad,
+        own(sums[total + 2], width // 4),
+        *grads,
         own(sums[total], width // 4),
         own(sums[:total].T, width // 4),
         sgate_grad,

time: 871 us -> 732 us (0.84)
  Pallas kernels: 176 us -> 412 us
  waiting for transfers between devices: 289 us -> 150 us
  starting transfers between devices: 100 us -> 4.7 us
  local copies, waits for them, and re-layouts: 130 us -> 58.4 us
  other arithmetic: 85.6 us -> 39.1 us
  matrix products: 76.8 us -> 58.1 us
    pallas_call x0 -> x3, Pallas kernels: none -> 248 us  [the longest x1 174 us: tail(): pl.pallas_call(tail_kernel, in_specs=[vmem] * 14, out_specs=[vmem] * 6, o...]
    ppermute x30 -> x3, waiting for transfers between devices: 61.4 us -> 0.01 us  [shift(): return lax.ppermute(v, 'ep', [(i, (i + 2 * steps) % n) for i in range(n)])]
    ppermute x30 -> x3, starting transfers between devices: 45.1 us -> 2.41 us  [shift(): return lax.ppermute(v, 'ep', [(i, (i + 2 * steps) % n) for i in range(n)])]
    ppermute x12 -> x0, waiting for transfers between devices: 39.8 us -> none  [the longest x6 20.1 us: ring(): return lax.ppermute(v, 'ep', [(i, (i + 2) % n) for i in range(n)])]
    ppermute x22 -> x2, waiting for transfers between devices: 96.6 us -> 72.1 us  [swap_y(): return lax.ppermute(v, 'hp', [(i, i ^ 2) for i in range(4)])]
    dot_general x16 -> x13, matrix products: 47.9 us -> 26.9 us  [dot(): lax.dot_general(left, right, (((over[0],), (over[1],)), ((), ())), prefer...]
    ppermute x22 -> x2, starting transfers between devices: 21.1 us -> 0.52 us  [swap_y(): return lax.ppermute(v, 'hp', [(i, i ^ 2) for i in range(4)])]
    add x24 -> x7, other arithmetic: 23.6 us -> 4.65 us  [the longest x1 4.17 us: per_device(): sum((v.astype(F32) for v in (piece_near[0], piece_core[0], piece_far)))]
  transfers between devices with their start and end apart: 123 -> 11, of which waited for: 50 -> 6; matrix products, arithmetic and copies ran while one was open for 30% -> 10% of each run, Pallas kernels for 3% -> 28%
where the time goes in v3:
time: 732 us; the launch traced here: 724 us
  Pallas kernels  412 us (56%)
  waiting for transfers between devices  150 us (20%)
  local copies, waits for them, and re-layouts  58.4 us (8%)
  matrix products  58.1 us (8%)
  other arithmetic  39.1 us (5%)
    pallas_call x1, Pallas kernels, tail(): pl.pallas_call(tail_kernel, in_specs=[vmem] * 14, out_specs=[vmem] * 6, o...  174 us
    pallas_call x1, Pallas kernels, dispatch(): pl.pallas_call(functools.partial(dispatch_kernel, capacity, total), grid=...  140 us
    ppermute x2, waiting for transfers between devices, swap_y(): return lax.ppermute(v, 'hp', [(i, i ^ 2) for i in range(4)])  72.1 us
    ppermute x2, waiting for transfers between devices, swap_pair(): return lax.ppermute(v, 'ep', [(i, i ^ 1) for i in range(n)])  70.9 us
    pallas_call x1, Pallas kernels, front(): pl.pallas_call(functools.partial(front_kernel, large, count), in_specs=[a...  67 us
    dot_general x2, matrix products, expert_grad(): return jnp.einsum('xna,xnb->xab', left, right, preferred_element_type=F32)  31.2 us
    unnamed x153, local copies, waits for them, and re-layouts  28 us
    dot_general x13, matrix products, dot(): lax.dot_general(left, right, (((over[0],), (over[1],)), ((), ())), prefer...  26.9 us
  transfers between devices with their start and end apart: 11, of which 6 were waited for; matrix products, arithmetic and copies ran while one was open for 10% of the time, Pallas kernels for 28%

profile of v3, /device:TPU:0, one launch (start us, length us, event | category | flops | bytes accessed | tf_op | source)
XLA Modules:
  0.0 724.3 jit_solution(10067227063892068106)
XLA Ops:
  4.6 3.3 pad_maximum_fusion.1.refs_1_.refs_0_
  12.7 67.0 %shard_map.288 = (bf16[256,1280]{1,0:T(8,128)(2,1)S(1)}, bf16[2,672,1280]{2,1,0:T(8,128)(2,1)}, bf16[4,256,1280]{2,1,0:T(8,128)(2,1)}, bf16[4,320,1280]{2,1,0:T(...) custom-call(bf16[256,1280]{1,0:T(8,128)(2,1)S(1)} %copy-done.6, ...), custom_call_target="tpu_custom_call" | custom-call | bytes 125829120 | tf_op jit(solution)/shard_map/pallas_call | solution.py:873
  90.9 1.9 copy-done.35
  92.9 7.4 %shard_map.289 = (bf16[512,1280]{1,0:T(8,128)(2,1)S(1)}, bf16[2,512,1280]{2,1,0:T(8,128)(2,1)S(1)}, bf16[256,1280]{1,0:T(8,128)(2,1)S(1)}) custom-call(bf16[256,1280]{1,0:T(8,128)(2,1)S(1)} %copy-done.6, bf16[256,1280]{1,0:T(8,128)(2,1)S(1)} %get-tuple-element.58.f_ref, f32[1,1280]{1,0:T(1,128)S(1)} %reshape.334.gain_ref, bf16[1280,1280]{1,0:T(8,128)(2,1)S(1)} %bitcast.108, ...), custom_call_target="tpu_custom_call" | custom-call | flops 4194304000 | bytes 14680064 | tf_op jit(solution)/shard_map/pallas_call | solution.py:196
  100.5 4.8 collective-permute-done.kb_ref.vb_ref
  105.4 9.5 %shard_map.290 = (bf16[256,1280]{1,0:T(8,128)(2,1)S(1)}, f32[256,1280]{1,0:T(8,128)S(1)}) custom-call(s32[1]{0:T(128)} %bitcast.h_ref, bf16[256,1280]{1,0:T(8,128)(2,1)S(1)} %get-tuple-element.63.q_ref, bf16[2,512,1280]{2,1,0:T(8,128)(2,1)S(1)} %get-tuple-element.64.ka_ref.va_ref, bf16[2,512,1280]{2,1,0:T(8,128)(2,1)S(1)} %collective-permute-done.kb_ref.vb_ref, ...), custom_call_target="tpu_custom_call" | custom-call | flops 1342177280 | bytes 8388608 | tf_op jit(solution)/shard_map/pallas_call | solution.py:281
  115.9 48.4 %collective-permute-done.2.refs_1_ = bf16[2,672,1280]{2,1,0:T(8,128)(2,1)} collective-permute-done((bf16[2,672,1280]{2,1,0:T(8,128)(2,1)}, bf16[2,672,1280]{2,1,0:T(8,128)(2,1)}, u32[]{:S(2)}, u32[]{:S(2)}) %collective-permute-start.2) | collective-permute-done | bytes 3440672 | tf_op jit(solution)/shard_map/ppermute | solution.py:30
  168.0 3.0 multiply_reduce_fusion.2
  173.5 50.5 %collective-permute-done.1.g1_ref = bf16[4,256,1280]{2,1,0:T(8,128)(2,1)} collective-permute-done((bf16[4,256,1280]{2,1,0:T(8,128)(2,1)}, bf16[4,256,1280]{2,1,0:T(8,128)(2,1)}, u32[]{:S(2)}, u32[]{:S(2)}) %collective-permute-start.1) | collective-permute-done | bytes 2621472 | tf_op jit(solution)/shard_map/ppermute | solution.py:35
  223.9 140.4 %shard_map.291 = (f32[256,1408]{1,0:T(8,128)}, bf16[4,256,1280]{2,1,0:T(8,128)(2,1)}, bf16[4,256,1280]{2,1,0:T(8,128)(2,1)}, f32[1280,256]{1,0:T(8,128)}, f32[12...) custom-call(bf16[256,1408]{1,0:T(8,128)(2,1)} %concatenate.42.x_ref,, ...), custom_call_target="tpu_custom_call" | custom-call | flops 31708938240 | bytes 83886080 | tf_op jit(solution)/shard_map/pallas_call | solution.py:730
  364.4 10.7 %convolution_convert_fusion.5 = bf16[2,1024,1280]{2,1,0:T(8,128)(2,1)S(1)} fusion(bf16[2,1152,1024]{2,1,0:T(8,128)(2,1)} %bitcast.129, bf16[2,1152,1280]{2,1,0:T(8,128)(2,1)} %bitcast.128), kind=kOutput, calls=%fused_computation.10 | convolution fusion | flops 6042419200 | bytes 15859712 | tf_op jit(solution)/shard_map/xna,xnb->xab/dot_general | solution.py:1322
  376.7 20.5 %convolution_convert_fusion = bf16[2,2048,1280]{2,1,0:T(8,128)(2,1)} fusion(bf16[2,1152,2048]{2,1,0:T(8,128)(2,1)} %bitcast.126, bf16[2,1152,1280]{2,1,0:T(8,128)(2,1)} %bitcast.127), kind=kOutput, calls=%fused_computation | convolution fusion | flops 12084838400 | bytes 25821184 | tf_op jit(solution)/shard_map/xna,xnb->xab/dot_general | solution.py:1322
  397.3 6.0 fusion.34
  404.0 3.4 pad_maximum_fusion
  416.8 2.0 collective-permute-done.5
  418.8 3.8 fusion.1
  424.2 14.4 %shard_map.292 = (bf16[256,1280]{1,0:T(8,128)(2,1)S(1)}, f32[2,512,1280]{2,1,0:T(8,128)}, bf16[2,512,1280]{2,1,0:T(8,128)(2,1)}) custom-call(s32[1]{0:T(128)} %bitcast.h_ref, bf16[256,1280]{1,0:T(8,128)(2,1)S(1)} %copy-done.9, bf16[2,512,1280]{2,1,0:T(8,128)(2,1)S(1)} %copy-done.3, bf16[2,512,1280]{2,1,0:T(8,128)(2,1)S(1)} %copy-done.5, ...), custom_call_target="tpu_custom_call" | custom-call | flops 3355443200 | bytes 16777216 | tf_op jit(solution)/shard_map/pallas_call | solution.py:312
  445.0 2.2 convert_element_type.219
  447.4 2.7 convolution_convert_fusion.1
  450.2 20.4 %collective-permute-done.4 = bf16[4,256,1280]{2,1,0:T(8,128)(2,1)} collective-permute-done((bf16[4,256,1280]{2,1,0:T(8,128)(2,1)}, bf16[4,256,1280]{2,1,0:T(8,128)(2,1)}, u32[]{:S(2)}, u32[]{:S(2)}) %collective-permute-start.4) | collective-permute-done | bytes 2621472 | tf_op jit(solution)/shard_map/ppermute | solution.py:35
  470.6 4.8 fusion.33
  477.6 2.8 convolution_convert_fusion.4
  482.8 2.6 add_convert_fusion
  491.2 2.3 fusion.7
  494.8 5.1 convolution_convert_fusion.2
  499.8 3.6 convolution_convert_fusion.3
  503.5 23.7 %collective-permute-done.10 = bf16[2,672,1280]{2,1,0:T(8,128)(2,1)} collective-permute-done((bf16[2,672,1280]{2,1,0:T(8,128)(2,1)}, bf16[2,672,1280]{2,1,0:T(8,128)(2,1)}, u32[]{:S(2)}, u32[]{:S(2)}) %collective-permute-start.10) | collective-permute-done | bytes 3440672 | tf_op jit(solution)/shard_map/ppermute | solution.py:30
  527.1 173.7 %shard_map.293 = (bf16[4,320,1280]{2,1,0:T(8,128)(2,1)}, f32[320,896]{1,0:T(8,128)}, f32[320,896]{1,0:T(8,128)}, f32[224,1280]{1,0:T(8,128)}, f32[24,1280]{1,0:T(8,128)}, /*index=5*/f32[256,1280]{1,0:T(8,128)}) custom-call(bf16[2,2,2,160,1280]{4,3,2,1,0:T(8,128)(2,1)} %bitcast.115, bf16[2,2,2,160,1280]{4,3,2,1,0:T(8,128)(2,1)} %bitcast.119, ...), custom_call_target="tpu_custom_call" | custom-call | bytes 314572800 | tf_op jit(solution)/shard_map/pallas_call | solution.py:1147
  702.6 4.2 fusion
  706.8 3.4 fusion.35
  710.7 2.9 bitcast_convert_fusion
  716.2 3.2 fusion.11
  (251 shorter events, 68.0 us)
Async XLA Ops:
  87.3 13.0 %copy-start.22 = (bf16[256,1280]{1,0:T(8,128)(2,1)}, bf16[256,1280]{1,0:T(8,128)(2,1)S(1)}, u32[]{:S(2)}) copy-start(bf16[256,1280]{1,0:T(8,128)(2,1)S(1)} %get-tuple-element.58.f_ref) | copy-start | bytes 1966084
  87.3 83.9 %copy-start.7 = (bf16[4,320,384]{2,1,0:T(8,128)(2,1)}, bf16[4,320,384]{2,1,0:T(8,128)(2,1)S(1)}, u32[]{:S(2)}) copy-start(bf16[4,320,384]{2,1,0:T(8,128)(2,1)S(1)} %get-tuple-element.59) | copy-start | bytes 2949124
  87.3 77.0 %collective-permute-start.2 = (bf16[2,672,1280]{2,1,0:T(8,128)(2,1)}, bf16[2,672,1280]{2,1,0:T(8,128)(2,1)}, u32[]{:S(2)}, u32[]{:S(2)}) collective-permute-start(bf16[2,672,1280]{2,1,0:T(8,128)(2,1)} %pad_maximum_fusion.1.refs_1_.refs_0_), channel_id=1, source_target_pairs={{0,2},{1,3},{2,0},{3,1},{4,6},{5,7},{6,4},{7,5},{8,10},{9,11},{10,... | collective-permute-start | bytes 10321928 | tf_op jit(solution)/shard_map/ppermute | solution.py:30
  90.2 10.1 %copy-start.28 = (f32[1,1280]{1,0:T(1,128)}, f32[1,1280]{1,0:T(1,128)S(1)}, u32[]{:S(2)}) copy-start(f32[1,1280]{1,0:T(1,128)S(1)} %reshape.334.gain_ref) | copy-start | bytes 15364
  100.3 14.5 %copy-start.2 = (bf16[2,512,1280]{2,1,0:T(8,128)(2,1)}, bf16[2,512,1280]{2,1,0:T(8,128)(2,1)S(1)}, u32[]{:S(2)}) copy-start(bf16[2,512,1280]{2,1,0:T(8,128)(2,1)S(1)} %get-tuple-element.64.ka_ref.va_ref) | copy-start | bytes 7864324
  100.3 14.5 %copy-start.8 = (bf16[256,1280]{1,0:T(8,128)(2,1)}, bf16[256,1280]{1,0:T(8,128)(2,1)S(1)}, u32[]{:S(2)}) copy-start(bf16[256,1280]{1,0:T(8,128)(2,1)S(1)} %get-tuple-element.63.q_ref) | copy-start | bytes 1966084
  100.4 14.5 %copy-start.16 = (bf16[512,1280]{1,0:T(8,128)(2,1)}, bf16[512,1280]{1,0:T(8,128)(2,1)S(1)}, u32[]{:S(2)}) copy-start(bf16[512,1280]{1,0:T(8,128)(2,1)S(1)} %get-tuple-element.84) | copy-start | bytes 3932164
  100.4 5.0 collective-permute-start
  105.3 9.5 %copy-start.4 = (bf16[2,512,1280]{2,1,0:T(8,128)(2,1)}, bf16[2,512,1280]{2,1,0:T(8,128)(2,1)S(1)}, u32[]{:S(2)}) copy-start(bf16[2,512,1280]{2,1,0:T(8,128)(2,1)S(1)} %collective-permute-done.kb_ref.vb_ref) | copy-start | bytes 7864324
  105.3 60.5 %copy-start.67 = (s32[256,7]{0,1:T(8,128)S(1)}, s32[256,7]{0,1:T(8,128)}, u32[]{:S(2)}) copy-start(s32[256,7]{0,1:T(8,128)} %param.31) | copy-start | bytes 21508
  105.4 60.6 %copy-start.69 = (s32[256,7]{0,1:T(8,128)S(1)}, s32[256,7]{0,1:T(8,128)}, u32[]{:S(2)}) copy-start(s32[256,7]{0,1:T(8,128)} %param.32) | copy-start | bytes 21508
  105.4 60.8 %copy-start.27 = (bf16[4,32,1280]{2,1,0:T(8,128)(2,1)S(1)}, bf16[4,32,1280]{2,1,0:T(8,128)(2,1)}, u32[]{:S(2)}) copy-start(bf16[4,32,1280]{2,1,0:T(8,128)(2,1)} %copy-done.26) | copy-start | bytes 983044
  115.9 55.1 %copy-start.12 = (bf16[256,1280]{1,0:T(8,128)(2,1)}, bf16[256,1280]{1,0:T(8,128)(2,1)S(1)}, u32[]{:S(2)}) copy-start(bf16[256,1280]{1,0:T(8,128)(2,1)S(1)} %get-tuple-element.65) | copy-start | bytes 1966084
  164.3 59.6 %collective-permute-start.3 = (bf16[2,672,1280]{2,1,0:T(8,128)(2,1)}, bf16[2,672,1280]{2,1,0:T(8,128)(2,1)}, u32[]{:S(2)}, u32[]{:S(2)}) collective-permute-start(bf16[2,672,1280]{2,1,0:T(8,128)(2,1)} %collective-permute-done.2.refs_1_), channel_id=1, source_target_pairs={{0,1},{1,0},{2,3},{3,2},{4,5},{5,4},{6,7},{7,6},{8,9},{9,8},{10,11... | collective-permute-start | bytes 10321928 | tf_op jit(solution)/shard_map/ppermute | solution.py:26
  164.3 59.6 %collective-permute-start.1 = (bf16[4,256,1280]{2,1,0:T(8,128)(2,1)}, bf16[4,256,1280]{2,1,0:T(8,128)(2,1)}, u32[]{:S(2)}, u32[]{:S(2)}) collective-permute-start(bf16[4,256,1280]{2,1,0:T(8,128)(2,1)} %get-tuple-element.67.g0_ref), channel_id=1, source_target_pairs={{0,4},{4,0},{8,12},{12,8},{16,20},{20,16},{24,28},{28,24},{1,5},{5... | collective-permute-start | bytes 7864328 | tf_op jit(solution)/shard_map/ppermute | solution.py:35
  407.4 11.3 %collective-permute-start.5 = (bf16[2,2,672,1280]{3,2,1,0:T(8,128)(2,1)}, bf16[2,2,672,1280]{3,2,1,0:T(8,128)(2,1)}, u32[]{:S(2)}, u32[]{:S(2)}) collective-permute-start(bf16[2,2,672,1280]{3,2,1,0:T(8,128)(2,1)} %pad_maximum_fusion), channel_id=1, source_target_pairs={{0,1},{1,0},{2,3},{3,2},{4,5},{5,4},{6,7},{7,6},{8,9},{9,8},{10,11... | collective-permute-start | bytes 20643848 | tf_op jit(solution)/shard_map/ppermute | solution.py:26
  411.6 59.0 %collective-permute-start.4 = (bf16[4,256,1280]{2,1,0:T(8,128)(2,1)}, bf16[4,256,1280]{2,1,0:T(8,128)(2,1)}, u32[]{:S(2)}, u32[]{:S(2)}) collective-permute-start(bf16[4,256,1280]{2,1,0:T(8,128)(2,1)} %get-tuple-element.73), channel_id=1, source_target_pairs={{0,4},{4,0},{8,12},{12,8},{16,20},{20,16},{24,28},{28,24},{1,5},{5... | collective-permute-start | bytes 7864328 | tf_op jit(solution)/shard_map/ppermute | solution.py:35
  415.7 31.7 %copy-start.42 = (f32[256,1280]{1,0:T(8,128)}, f32[256,1280]{1,0:T(8,128)S(1)}, u32[]{:S(2)}) copy-start(f32[256,1280]{1,0:T(8,128)S(1)} %subtract_add_fusion.mid_ref) | copy-start | bytes 3932164
  418.8 5.3 copy-start.15
  439.4 7.8 %copy-start.66 = (bf16[256,16]{1,0:T(8,128)(2,1)S(1)}, bf16[256,16]{1,0:T(8,128)(2,1)}, u32[]{:S(2)}) copy-start(bf16[256,16]{1,0:T(8,128)(2,1)} %copy-done.65) | copy-start | bytes 24580
  439.4 8.0 %copy-start.13 = (bf16[256,1280]{1,0:T(8,128)(2,1)S(1)}, bf16[256,1280]{1,0:T(8,128)(2,1)}, u32[]{:S(2)}) copy-start(bf16[256,1280]{1,0:T(8,128)(2,1)} %copy-done.12) | copy-start | bytes 1966084
  439.4 43.4 %collective-permute-start.9 = (bf16[2,512,1280]{2,1,0:T(8,128)(2,1)}, bf16[2,512,1280]{2,1,0:T(8,128)(2,1)}, u32[]{:S(2)}, u32[]{:S(2)}) collective-permute-start(bf16[2,512,1280]{2,1,0:T(8,128)(2,1)} %get-tuple-element.86), channel_id=1, source_target_pairs={{0,1},{1,0},{2,3},{3,2},{4,5},{5,4},{6,7},{7,6},{8,9},{9,8},{10,11... | collective-permute-start | bytes 7864328 | tf_op jit(solution)/shard_map/ppermute | solution.py:26
  447.4 23.2 %copy-start.58 = (bf16[4,256,1280]{2,1,0:T(8,128)(2,1)S(1)}, bf16[4,256,1280]{2,1,0:T(8,128)(2,1)}, u32[]{:S(2)}) copy-start(bf16[4,256,1280]{2,1,0:T(8,128)(2,1)} %get-tuple-element.72) | copy-start | bytes 7864324
  450.2 77.0 %collective-permute-start.10 = (bf16[2,672,1280]{2,1,0:T(8,128)(2,1)}, bf16[2,672,1280]{2,1,0:T(8,128)(2,1)}, u32[]{:S(2)}, u32[]{:S(2)}) collective-permute-start(bf16[2,672,1280]{2,1,0:T(8,128)(2,1)} %fusion.1), channel_id=1, source_target_pairs={{0,2},{1,3},{2,0},{3,1},{4,6},{5,7},{6,4},{7,5},{8,10},{9,11},{10,... | collective-permute-start | bytes 10321928 | tf_op jit(solution)/shard_map/ppermute | solution.py:30
  475.4 7.4 %slice-start = ((s8[5242880]{0:T(1024)(128)(4,1)}), s8[4194304]{0:T(1024)(128)(4,1)S(1)}, s32[]{:S(2)}) async-start(s8[5242880]{0:T(1024)(128)(4,1)} %bitcast.116), calls=%async_computation | async-start | bytes 8388608
  477.6 5.2 slice-start.1
  480.4 233.2 %collective-permute-start.6 = (bf16[256,1280]{1,0:T(8,128)(2,1)}, bf16[256,1280]{1,0:T(8,128)(2,1)}, u32[]{:S(2)}, u32[]{:S(2)}) collective-permute-start(bf16[256,1280]{1,0:T(8,128)(2,1)} %get-tuple-element.132), channel_id=1, source_target_pairs={{0,24},{4,28},{8,0},{12,4},{16,8},{20,12},{24,16},{28,20},{1,25},{... | collective-permute-start | bytes 1966088 | tf_op jit(solution)/shard_map/ppermute | solution.py:45
  480.4 233.2 %collective-permute-start.7 = (bf16[256,1280]{1,0:T(8,128)(2,1)}, bf16[256,1280]{1,0:T(8,128)(2,1)}, u32[]{:S(2)}, u32[]{:S(2)}) collective-permute-start(bf16[256,1280]{1,0:T(8,128)(2,1)} %get-tuple-element.131), channel_id=1, source_target_pairs={{0,16},{4,20},{8,24},{12,28},{16,0},{20,4},{24,8},{28,12},{1,17},{... | collective-permute-start | bytes 1966088 | tf_op jit(solution)/shard_map/ppermute | solution.py:45
  482.1 231.5 %collective-permute-start.8 = (bf16[256,1280]{1,0:T(8,128)(2,1)}, bf16[256,1280]{1,0:T(8,128)(2,1)}, u32[]{:S(2)}, u32[]{:S(2)}) collective-permute-start(bf16[256,1280]{1,0:T(8,128)(2,1)} %get-tuple-element.130), channel_id=1, source_target_pairs={{0,8},{4,12},{8,16},{12,20},{16,24},{20,28},{24,0},{28,4},{1,9},{5... | collective-permute-start | bytes 1966088 | tf_op jit(solution)/shard_map/ppermute | solution.py:45
  494.8 5.1 copy-start.57
  527.1 175.5 %copy-start.51 = (bf16[2,224,1280]{2,1,0:T(8,128)(2,1)S(1)}, bf16[2,224,1280]{2,1,0:T(8,128)(2,1)}, u32[]{:S(2)}) copy-start(bf16[2,224,1280]{2,1,0:T(8,128)(2,1)} %get-tuple-element.119) | copy-start | bytes 3440644
  710.7 5.5 copy-start.41
  (53 other events, 132.4 us)

commit v4 on v3

--- a/solution.py
+++ b/solution.py
@@ -149,8 +149,7 @@
     return v
 
 
-def score_mask(h_ref, rows, cols):
-    h = h_ref[0]
+def score_mask(h, rows, cols):
     at = lax.broadcasted_iota(jnp.int32, (rows, cols), 0) + h * rows
     key = lax.broadcasted_iota(jnp.int32, (rows, cols), 1)
     block = key // rows
@@ -209,9 +208,7 @@
             jax.ShapeDtypeStruct((rows, width), BF),
         ],
         compiler_params=pltpu.CompilerParams(vmem_limit_bytes=40 * MIB),
-        cost_estimate=pl.CostEstimate(
-            flops=10 * rows * width * width, bytes_accessed=14 * MIB, transcendentals=0
-        ),
+        cost_estimate=pl.CostEstimate(flops=0, bytes_accessed=0, transcendentals=0),
     )(tokens, far, gain, k_w, v_w, q_w, cosine, sine)
 
 
@@ -220,7 +217,7 @@
     half = ka_ref.shape[0]
     q = q_ref[...]
     s = jnp.concatenate([dot(q, ka_ref[...], (1, 1)), dot(q, kb_ref[...], (1, 1))], axis=1)
-    s = jnp.where(score_mask(h_ref, rows, 2 * half), s * HD ** (-0.5), -1e30)
+    s = jnp.where(score_mask(h_ref[0], rows, 2 * half), s * HD ** (-0.5), -1e30)
     top = jnp.max(s, axis=1, keepdims=True)
     p = jnp.exp(s - top)
     total = jnp.sum(p, axis=1, keepdims=True)
@@ -250,7 +247,7 @@
     q, d = q_ref[...], d_ref[...]
     cosine, sine = cos_ref[...], -sin_ref[...]
     s = jnp.concatenate([dot(q, ka_ref[...], (1, 1)), dot(q, kb_ref[...], (1, 1))], axis=1)
-    s = jnp.where(score_mask(h_ref, rows, 2 * half), s * HD ** (-0.5), -1e30)
+    s = jnp.where(score_mask(h_ref[0], rows, 2 * half), s * HD ** (-0.5), -1e30)
     p = jnp.exp(s - lse_ref[:, 0:1])
     back = jnp.concatenate([dot(d, va_ref[...], (1, 1)), dot(d, vb_ref[...], (1, 1))], axis=1)
     inner = jnp.sum(p * back, axis=1, keepdims=True)
@@ -277,7 +274,6 @@
 def attend(h, q, kv_a, kv_b):
     rows, width = q.shape
     half = kv_a.shape[1]
-    flops = 4 * rows * 2 * half * width
     return pl.pallas_call(
         attend_kernel,
         grid_spec=pltpu.PrefetchScalarGridSpec(
@@ -297,9 +293,7 @@
             jax.ShapeDtypeStruct((rows, width), F32),
         ],
         compiler_params=pltpu.CompilerParams(vmem_limit_bytes=40 * MIB),
-        cost_estimate=pl.CostEstimate(
-            flops=flops, bytes_accessed=8 * MIB, transcendentals=rows * 2 * half * H
-        ),
+        cost_estimate=pl.CostEstimate(flops=0, bytes_accessed=0, transcendentals=0),
     )(h, q, kv_a, kv_b, kv_a, kv_b)
 
 
@@ -529,90 +523,147 @@
     )(e, *x_pair, wa, sa, *downs, sd)
 
 
-def dispatch_kernel(capacity, total, x_ref, g0_ref, g1_ref, *refs):
-    experts = refs[0:4]
-    sg_ref, su_ref, sd_ref = refs[4:7]
-    dx_ref, near_ref, far_ref, sgg_ref, sdg_ref, xr_ref, gr_ref, gu_ref, wa_ref = refs[7:16]
-    xbuf, sbuf, tbuf, wgu, wd = refs[16:21]
-    rx_s, rx_r, sx_s, sx_r, sr_s, sr_r, rt_s, rt_r, w_sem = refs[21:]
+def dispatch_kernel(capacity, total, x_ref, m_ref, g0_ref, g1_ref, *refs):
+    experts = refs[0:3]
+    sg_ref, su_ref, sd_ref = refs[3:6]
+    dx_ref, wb_ref, near_ref, far_ref, sgg_ref, sdg_ref = refs[6:12]
+    xr_ref, gr_ref, gu_ref, wa_ref, last_ref = refs[12:17]
+    xbuf, sbuf, tbuf, mbuf, nbuf, bbuf, sbbuf, tbbuf, wgu, wd = refs[17:27]
+    (
+        rx_s,
+        rx_r,
+        sx_s,
+        sx_r,
+        sr_s,
+        sr_r,
+        rt_s,
+        rt_r,
+        rm_s,
+        rm_r,
+        sm_s,
+        sm_r,
+        sb_s,
+        sb_r,
+        rb_s,
+        rb_r,
+        w_sem,
+        l_s,
+        l_r,
+    ) = refs[27:]
+    experts = experts + (last_ref,)
     k = pl.program_id(0)
     stages = xbuf.shape[0]
     tokens, width = x_ref.shape[0], sg_ref.shape[0]
     hidden = experts[0].shape[1] // 3
     wide = wd.shape[1] // 4
     c = capacity
+    last = stages - 1
     e, h = lax.axis_index("ep"), lax.axis_index("hp")
     n = 2 * stages
-    right, left = lax.rem(e + 2, n), lax.rem(e + n - 2, n)
-    pair = e + 1 - 2 * lax.rem(e, 2)
-
-    def send(src, dst, s, r, i, where):
-        return pltpu.make_async_remote_copy(
-            src_ref=src,
-            dst_ref=dst,
-            send_sem=s.at[i],
-            recv_sem=r.at[i],
-            device_id=(where, h),
-            device_id_type=pl.DeviceIdType.MESH,
-        )
+    right, left = (lax.rem(e + 2, n), h), (lax.rem(e + n - 2, n), h)
+    pair = (e + 1 - 2 * lax.rem(e, 2), h)
+    core = (e, h + 1 - 2 * lax.rem(h, 2))
 
     def ring_x(i):
-        return send(xbuf.at[i, 0], xbuf.at[i + 1, 0], rx_s, rx_r, i, right)
+        return mesh_copy(xbuf.at[i, 0], xbuf.at[i + 1, 0], rx_s, rx_r, i, right)
+
+    def ring_last():
+        return mesh_copy(xbuf.at[last - 1, 1], xbuf.at[last, 1], rx_s, rx_r, last, right)
 
     def swap_x(i):
-        return send(xbuf.at[i, 0], xbuf.at[i, 1], sx_s, sx_r, i, pair)
+        return mesh_copy(xbuf.at[i, 0], xbuf.at[i, 1], sx_s, sx_r, i, pair)
+
+    def ring_m(i):
+        return mesh_copy(mbuf.at[i], mbuf.at[i + 1], rm_s, rm_r, i, right)
+
+    def swap_m(i):
+        return mesh_copy(mbuf.at[i], nbuf.at[i], sm_s, sm_r, i, pair)
 
     def swap_r(i):
-        return send(xbuf.at[i, 1], sbuf.at[i], sr_s, sr_r, i, pair)
+        return mesh_copy(xbuf.at[i, 1], sbuf.at[i], sr_s, sr_r, i, pair)
 
     def ring_t(i):
-        return send(xbuf.at[i, 0], tbuf.at[i], rt_s, rt_r, i, right)
+        return mesh_copy(xbuf.at[i, 0], tbuf.at[i], rt_s, rt_r, i, right)
+
+    def swap_b(i):
+        return mesh_copy(bbuf.at[i, 1], sbbuf.at[i], sb_s, sb_r, i, pair)
+
+    def ring_b(i):
+        return mesh_copy(bbuf.at[i, 0], tbbuf.at[i], rb_s, rb_r, i, right)
+
+    to_core = mesh_copy(experts[1], last_ref, l_s, l_r, 0, core)
+
+    def weight_copies(r):
+        copies = []
+        for x in range(2):
+            for i, (to, at) in enumerate(((wgu, 2 * r), (wgu, 2 * r + 1), (wd, r))):
+                copies.append(
+                    pltpu.make_async_copy(
+                        experts[r].at[x, pl.ds(i * hidden, hidden), :],
+                        to.at[x, pl.ds(at * wide, hidden), :],
+                        w_sem.at[6 * r + 3 * x + i],
+                    )
+                )
+        return copies
 
     @pl.when(k == 0)
     def _():
-        barrier = pltpu.get_barrier_semaphore()
-        for where in (right, left, pair):
-            pl.semaphore_signal(
-                barrier, inc=1, device_id=(where, h), device_id_type=pl.DeviceIdType.MESH
-            )
         xbuf[0, 0] = x_ref[...]
-        pl.semaphore_wait(barrier, 3)
+        mbuf[0] = m_ref[...]
+        greet((right, left, pair, core))
+        ring_m(0).start()
+        swap_m(0).start()
         ring_x(0).start()
         swap_x(0).start()
+        to_core.start()
         rest = wide - hidden
-        copies = []
+        for r in range(3):
+            for copy in weight_copies(r):
+                copy.start()
         for x in range(2):
-            for r in range(4):
-                for i, (to, at) in enumerate(((wgu, 2 * r), (wgu, 2 * r + 1), (wd, r))):
-                    copy = pltpu.make_async_copy(
-                        experts[r].at[x, pl.ds(i * hidden, hidden), :],
-                        to.at[x, pl.ds(at * wide, hidden), :],
-                        w_sem.at[len(copies)],
-                    )
-                    copy.start()
-                    copies.append(copy)
+            for to, count in ((wgu, 8), (wd, 4)):
+                for at in range(count):
                     to[x, at * wide + hidden : (at + 1) * wide, :] = jnp.zeros((rest, width), BF)
-        for copy in copies:
-            copy.wait()
         sgg_ref[...] = jnp.zeros_like(sgg_ref)
         sdg_ref[...] = jnp.zeros_like(sdg_ref)
-
-    @pl.when(k < stages - 1)
-    def _():
+        to_core.wait()
+        for copy in weight_copies(3):
+            copy.start()
+
+    @pl.when(k < last)
+    def _():
+        ring_m(k).wait_recv()
+        swap_m(k + 1).start()
         ring_x(k).wait_recv()
 
-    @pl.when(k < stages - 2)
-    def _():
+    @pl.when(k < last - 1)
+    def _():
+        ring_m(k + 1).start()
         ring_x(k + 1).start()
-
-    @pl.when(k < stages - 1)
-    def _():
         swap_x(k + 1).start()
 
-    swap_x(k).wait_recv()
-
-    x2 = jnp.concatenate([xbuf[k, j, :, :width] for j in range(2)], axis=0)
+    @pl.when(k < last)
+    def _():
+        swap_x(k).wait_recv()
+
+    @pl.when(k == last - 1)
+    def _():
+        ring_last().start()
+
+    @pl.when(k == last)
+    def _():
+        ring_last().wait_recv()
+
+    swap_m(k).wait_recv()
+
+    @pl.when(k == 0)
+    def _():
+        for r in range(4):
+            for copy in weight_copies(r):
+                copy.wait()
+
     gs = (g0_ref, g1_ref)
+    x2 = jnp.concatenate([xbuf[k, j] for j in range(2)], axis=0)
     g2 = jnp.concatenate([g[0] for g in gs], axis=0)
     hg, hu = dot(x2, sg_ref[...]), dot(x2, su_ref[...])
     ab = dot(g2, sd_ref[...], (1, 1))
@@ -627,20 +678,25 @@
     totals = [dx[:tokens], dx[tokens:]]
     out = dot(act, sd_ref[...])
     outs = [out[:tokens], out[tokens:]]
-    metas = [0.0, 0.0]
-    lane = lax.broadcasted_iota(jnp.int32, (2 * c, LANES), 1)
+    backs = [0.0, 0.0]
+    metas = [mbuf[k], nbuf[k]]
+    line = lax.broadcasted_iota(jnp.int32, metas[0].shape, 0)
+    short = lax.broadcasted_iota(jnp.int32, (total, tokens), 0)
+    place = lax.broadcasted_iota(jnp.int32, (c, tokens), 0).astype(F32)
     for x in range(2):
         col = 2 * e + x
-        picks, weights = [], []
+        picks, weights, found = [], [], []
         for j in range(2):
-            pick = pick_matrix(xbuf[k, j, :, width:], total + col, c)
+            code = jnp.sum(jnp.where(line == total + col, metas[j], 0.0), axis=0, keepdims=True)
+            weight = jnp.sum(jnp.where(line == col, metas[j], 0.0), axis=0, keepdims=True)
+            hit = code == place
+            pick = jnp.where(hit, 1.0, 0.0).astype(BF)
+            found.append(hit)
             picks.append(pick)
-            rows = dot(pick, xbuf[k, j], (0, 0))
-            xr_ref[x, 0, j * c : (j + 1) * c, :] = rows[:, :width].astype(BF)
-            weights.append(rows[:, width:])
-            gr_ref[x, 0, j * c : (j + 1) * c, :] = dot(pick, gs[j][0], (0, 0)).astype(BF)
+            weights.append(jnp.sum(jnp.where(hit, weight, 0.0), axis=1, keepdims=True))
+            xr_ref[x, 0, j * c : (j + 1) * c, :] = dot(pick, xbuf[k, j]).astype(BF)
+            gr_ref[x, 0, j * c : (j + 1) * c, :] = dot(pick, gs[j][0]).astype(BF)
         w = jnp.concatenate(weights, axis=0)
-        w = jnp.sum(jnp.where(lane == col, w, 0.0), axis=1, keepdims=True)
         xr, gr = xr_ref[x, 0], gr_ref[x, 0]
         wb = jnp.zeros((2 * c, 1), F32)
         for r in range(4):
@@ -658,67 +714,84 @@
             wa_ref[x, 0, :, r * wide : (r + 1) * wide] = (act * w).astype(BF)
         dxr = dot(gu_ref[x, 0], wgu[x]).astype(BF)
         rows = dot(wa_ref[x, 0], wd[x]).astype(BF)
-        high = wb.astype(BF).astype(F32)
-        meta = jnp.where(lane == col, high, 0.0) + jnp.where(lane == total + col, wb - high, 0.0)
-        meta = meta.astype(BF)
         for j in range(2):
             span = slice(j * c, (j + 1) * c)
-            totals[j] = totals[j] + dot(picks[j], dxr[span])
-            outs[j] = outs[j] + dot(picks[j], rows[span])
-            metas[j] = metas[j] + dot(picks[j], meta[span])
-
-    @pl.when(k < stages - 1)
+            totals[j] = totals[j] + dot(picks[j], dxr[span], (0, 0))
+            outs[j] = outs[j] + dot(picks[j], rows[span], (0, 0))
+            row = jnp.sum(jnp.where(found[j], wb[span], 0.0), axis=0, keepdims=True)
+            backs[j] = backs[j] + jnp.where(short == col, row, 0.0)
+
+    @pl.when(k < last)
     def _():
         ring_x(k).wait_send()
-
-    swap_x(k).wait_send()
+        swap_x(k).wait_send()
+
+    @pl.when(k == last - 1)
+    def _():
+        ring_last().wait_send()
+
     for j in range(2):
-        xbuf[k, j, :, :width] = totals[j].astype(BF)
-        xbuf[k, j, :, width:] = metas[j].astype(BF)
+        xbuf[k, j] = totals[j].astype(BF)
+        bbuf[k, j] = backs[j]
         (near_ref, far_ref)[j][0] = outs[j].astype(BF)
 
     @pl.when(k >= 1)
     def _():
+        swap_b(k).start()
         swap_r(k).start()
 
     def advance(i, first):
+        swap_b(i).wait_recv()
         swap_r(i).wait_recv()
         here = xbuf[i, 0].astype(F32) + sbuf[i].astype(F32)
+        small = bbuf[i, 0] + sbbuf[i]
         if not first:
+            ring_b(i - 1).wait_recv()
             ring_t(i - 1).wait_recv()
             here = here + tbuf[i - 1].astype(F32)
+            small = small + tbbuf[i - 1]
         xbuf[i, 0] = here.astype(BF)
+        bbuf[i, 0] = small
+        ring_b(i).start()
         ring_t(i).start()
 
-    for i in range(1, stages - 1):
+    for i in range(1, last):
 
         @pl.when(k == i + 1)
         def _(i=i):
             advance(i, i == 1)
 
-    @pl.when(k == stages - 1)
-    def _():
+    @pl.when(k == last)
+    def _():
+        swap_b(0).start()
         swap_r(0).start()
-        advance(stages - 1, stages == 2)
+        advance(last, last == 1)
+        swap_b(0).wait_recv()
         swap_r(0).wait_recv()
-        ring_t(stages - 1).wait_recv()
-        dx_ref[...] = (
-            xbuf[0, 0].astype(F32) + sbuf[0].astype(F32) + tbuf[stages - 1].astype(F32)
-        )
+        ring_b(last).wait_recv()
+        ring_t(last).wait_recv()
+        dx_ref[...] = xbuf[0, 0].astype(F32) + sbuf[0].astype(F32) + tbuf[last].astype(F32)
+        wb_ref[...] = bbuf[0, 0] + sbbuf[0] + tbbuf[last]
         for i in range(stages):
             swap_r(i).wait_send()
+            swap_b(i).wait_send()
+            swap_m(i).wait_send()
         for i in range(1, stages):
             ring_t(i).wait_send()
-
-
-def dispatch(capacity, total, x_ext, g_near, g_far, experts, sg, su, sd):
+            ring_b(i).wait_send()
+            ring_m(i - 1).wait_send()
+
+
+def dispatch(capacity, total, x, meta, g_near, g_far, experts, sg, su, sd):
     stages = g_near.shape[0]
-    tokens, ext = x_ext.shape
-    width, shared = sg.shape
+    tokens, width = x.shape
+    lines = meta.shape[0]
+    shared = sg.shape[1]
     hidden = experts[0].shape[1] // 3
     wide = -(-hidden // LANES) * LANES
     c2 = 2 * capacity
     once = pl.Buffered(1)
+    dma = pltpu.SemaphoreType.DMA
 
     def fixed(shape):
         return pl.BlockSpec(shape, lambda k: (0,) * len(shape), pipeline_mode=once)
@@ -731,14 +804,16 @@
         functools.partial(dispatch_kernel, capacity, total),
         grid=(stages,),
         in_specs=[
-            fixed((tokens, ext)),
+            fixed((tokens, width)),
+            fixed(meta.shape),
             pl.BlockSpec((1, tokens, width), lambda k: (k, 0, 0)),
             pl.BlockSpec((1, tokens, width), lambda k: (k, 0, 0)),
         ]
-        + [anywhere] * 4
+        + [anywhere] * 3
         + [fixed(sg.shape), fixed(su.shape), fixed(sd.shape)],
         out_specs=[
-            fixed((tokens, ext)),
+            fixed((tokens, width)),
+            fixed((total, tokens)),
             pl.BlockSpec((1, tokens, width), lambda k: (k, 0, 0), pipeline_mode=once),
             pl.BlockSpec((1, tokens, width), lambda k: (k, 0, 0), pipeline_mode=once),
             fixed((width, 2 * shared)),
@@ -747,9 +822,11 @@
             per_stage((2, 1, c2, width)),
             per_stage((2, 1, c2, 8 * wide)),
             per_stage((2, 1, c2, 4 * wide)),
+            anywhere,
         ],
         out_shape=[
-            jax.ShapeDtypeStruct((tokens, ext), F32),
+            jax.ShapeDtypeStruct((tokens, width), F32),
+            jax.ShapeDtypeStruct((total, tokens), F32),
             jax.ShapeDtypeStruct((stages, tokens, width), BF),
             jax.ShapeDtypeStruct((stages, tokens, width), BF),
             jax.ShapeDtypeStruct((width, 2 * shared), F32),
@@ -758,16 +835,23 @@
             jax.ShapeDtypeStruct((2, stages, c2, width), BF),
             jax.ShapeDtypeStruct((2, stages, c2, 8 * wide), BF),
             jax.ShapeDtypeStruct((2, stages, c2, 4 * wide), BF),
+            jax.ShapeDtypeStruct(experts[0].shape, BF),
         ],
         scratch_shapes=[
-            pltpu.VMEM((stages, 2, tokens, ext), BF),
-            pltpu.VMEM((stages, tokens, ext), BF),
-            pltpu.VMEM((stages, tokens, ext), BF),
+            pltpu.VMEM((stages, 2, tokens, width), BF),
+            pltpu.VMEM((stages, tokens, width), BF),
+            pltpu.VMEM((stages, tokens, width), BF),
+            pltpu.VMEM((stages, lines, tokens), F32),
+            pltpu.VMEM((stages, lines, tokens), F32),
+            pltpu.VMEM((stages, 2, total, tokens), F32),
+            pltpu.VMEM((stages, total, tokens), F32),
+            pltpu.VMEM((stages, total, tokens), F32),
             pltpu.VMEM((2, 8 * wide, width), BF),
             pltpu.VMEM((2, 4 * wide, width), BF),
         ]
-        + [pltpu.SemaphoreType.DMA((stages,))] * 8
-        + [pltpu.SemaphoreType.DMA((24,))],
+        + [dma((stages,))] * 16
+        + [dma((24,))]
+        + [dma((1,))] * 2,
         compiler_params=pltpu.CompilerParams(
             vmem_limit_bytes=63 * MIB, collective_id=0, has_side_effects=True
         ),
@@ -776,7 +860,7 @@
             bytes_accessed=80 * MIB,
             transcendentals=stages * c2 * 8 * hidden,
         ),
-    )(x_ext, g_near, g_far, *experts, sg, su, sd)
+    )(x, meta, g_near, g_far, *experts, sg, su, sd)[:10]
 
 
 def mesh_copy(src, dst, s, r, i, where):
@@ -891,25 +975,349 @@
     )(tokens, experts, cotangent, *blocks)
 
 
+class SharedSum:
+    def __init__(self, at, peers, ref, got, to_far, from_far, fin, s, r):
+        c, y, x, z = at
+        core, far, pair, up = peers
+        self.at, self.fin = at, fin
+        self.ref, self.got, self.to_far, self.from_far = ref, got, to_far, from_far
+        self.core = mesh_copy(ref.at[:, 1 - c], got, s, r, 0, core)
+        self.far = mesh_copy(to_far, from_far, s, r, 1, far)
+        own = fin.at[x, z]
+        self.up = [mesh_copy(own, own, s, r, 1 + k, up[k]) for k in range(1, 4)]
+        self.pair = mesh_copy(fin.at[x], fin.at[x], s, r, 5, pair)
+        self.all = [self.core, self.far, self.pair] + self.up
+
+    def over_y(self):
+        c, y, _, _ = self.at
+        self.core.wait_recv()
+        total = self.ref[1 - y, c].astype(F32) + self.got[1 - y].astype(F32)
+        self.to_far[...] = total.astype(BF)
+        self.far.start()
+
+    def over_z(self):
+        c, y, x, z = self.at
+        self.far.wait_recv()
+        total = self.ref[y, c].astype(F32) + self.got[y].astype(F32)
+        self.fin[x, z] = (total + self.from_far[...].astype(F32)).astype(BF)
+        for copy in self.up:
+            copy.start()
+
+    def over_x(self):
+        for copy in self.up:
+            copy.wait_recv()
+        self.pair.start()
+
+
+def back_kernel(
+    q_ref,
+    ka_ref,
+    kb_ref,
+    va_ref,
+    vb_ref,
+    d_ref,
+    lse_ref,
+    wq_ref,
+    wk_ref,
+    wv_ref,
+    cos_ref,
+    sin_ref,
+    x_ref,
+    tok_ref,
+    ftok_ref,
+    sg_ref,
+    sd_ref,
+    spread_ref,
+    stack_ref,
+    near_ref,
+    mid_ref,
+    away_ref,
+    piece_ref,
+    qp_ref,
+    kp_ref,
+    vp_ref,
+    first_ref,
+    share_ref,
+    gain_ref,
+    sgout_ref,
+    suout_ref,
+    sdout_ref,
+    layer_ref,
+    piece_far,
+    sendb,
+    recvb,
+    nearb,
+    kvacc,
+    qacc,
+    sg_c,
+    sg_y,
+    sg_yr,
+    sg_fin,
+    sd_c,
+    sd_y,
+    sd_yr,
+    sd_fin,
+    xgot,
+    zsend,
+    zgot,
+    k_s,
+    k_r,
+    s_s,
+    s_r,
+    d_s,
+    d_r,
+    x_s,
+    x_r,
+    z_s,
+    z_r,
+    p_s,
+    p_r,
+):
+    i = pl.program_id(0)
+    heads = sendb.shape[0]
+    rows, half = q_ref.shape[0], ka_ref.shape[0]
+    e, h = lax.axis_index("ep"), lax.axis_index("hp")
+    x, z = lax.rem(e, 2), e // 2
+    c, y = lax.rem(h, 2), h // 2
+    core, far = (e, h + 1 - 2 * c), (e, lax.rem(h + 2, 4))
+    pair = (e + 1 - 2 * x, h)
+    up = [None] + [(2 * lax.rem(z + s, 4) + x, h) for s in range(1, 4)]
+
+    def over_core(n):
+        return mesh_copy(sendb.at[n], recvb.at[n], k_s, k_r, n, core)
+
+    def over_x(n):
+        return mesh_copy(away_ref.at[n], xgot.at[n], x_s, x_r, n, pair)
+
+    def home(n):
+        return mesh_copy(zsend.at[n - 1], zgot.at[n - 1], z_s, z_r, n - 1, up[4 - n])
+
+    hidden = piece_ref.shape[1] // 3
+    pieces = []
+    for n in range(6):
+        place = (n // 3, pl.ds(n % 3 * hidden, hidden))
+        pieces.append(mesh_copy(piece_ref.at[place], piece_far.at[place], p_s, p_r, n, far))
+    at, peers = (c, y, x, z), (core, far, pair, up)
+    sums = [
+        SharedSum(at, peers, sg_ref, sg_c, sg_y, sg_yr, sg_fin, s_s, s_r),
+        SharedSum(at, peers, sd_ref, sd_c, sd_y, sd_yr, sd_fin, d_s, d_r),
+    ]
+
+    def send_home(n):
+        over_x(n).wait_recv()
+        zsend[n - 1] = (near_ref[n].astype(F32) + xgot[n].astype(F32)).astype(BF)
+        home(n).start()
+
+    @pl.when(i == 0)
+    def _():
+        greet([core, far, pair] + up[1:])
+        for n in (1, 2, 3, 0):
+            over_x(n).start()
+        for flow in sums:
+            flow.core.start()
+        pieces[0].start()
+        kvacc[...] = jnp.zeros_like(kvacc)
+        qacc[...] = jnp.zeros_like(qacc)
+
+    @pl.when(i < heads)
+    def _():
+        q, d = q_ref[...], d_ref[...]
+        cosine, sine = cos_ref[...], -sin_ref[...]
+        s = jnp.concatenate([dot(q, ka_ref[...], (1, 1)), dot(q, kb_ref[...], (1, 1))], axis=1)
+        s = jnp.where(score_mask(h, rows, 2 * half), s * HD ** (-0.5), -1e30)
+        p = jnp.exp(s - lse_ref[:, 0:1])
+        back = [dot(d, va_ref[...], (1, 1)), dot(d, vb_ref[...], (1, 1))]
+        back = jnp.concatenate(back, axis=1)
+        inner = jnp.sum(p * back, axis=1, keepdims=True)
+        sb = (p * (back - inner) * HD ** (-0.5)).astype(BF)
+        p = p.astype(BF)
+        dq = dot(sb[:, :half], ka_ref[...]) + dot(sb[:, half:], kb_ref[...])
+        dk = turned(dot(sb, q, (0, 0)), cosine, sine)
+        dv = dot(p, d, (0, 0))
+        nearb[lax.rem(i, 2), 0] = dk[:half]
+        nearb[lax.rem(i, 2), 1] = dv[:half]
+        sendb[i, 0] = dk[half:].astype(BF)
+        sendb[i, 1] = dv[half:].astype(BF)
+        over_core(i).start()
+        raw = turned(dq, cosine[:rows], sine[:rows]).astype(BF)
+        qp_ref[...] = dot(x_ref[:rows, :], raw, (0, 0)).astype(BF)
+        qacc[...] += dot(raw, wq_ref[...], (1, 1))
+
+    @pl.when(i > 0)
+    def _():
+        n = i - 1
+        over_core(n).wait_recv()
+        kept = lax.rem(n, 2)
+        key = (nearb[kept, 0] + recvb[n, 0].astype(F32)).astype(BF)
+        value = (nearb[kept, 1] + recvb[n, 1].astype(F32)).astype(BF)
+        kp_ref[...] = dot(x_ref[...], key, (0, 0)).astype(BF)
+        vp_ref[...] = dot(x_ref[...], value, (0, 0)).astype(BF)
+        kvacc[...] += dot(key, wk_ref[...], (1, 1)) + dot(value, wv_ref[...], (1, 1))
+
+    @pl.when(i == 1)
+    def _():
+        for flow in sums:
+            flow.over_y()
+        for copy in pieces[1:]:
+            copy.start()
+
+    @pl.when(i == 4)
+    def _():
+        send_home(1)
+
+    @pl.when(i == 5)
+    def _():
+        for flow in sums:
+            flow.over_z()
+
+    @pl.when(i == 7)
+    def _():
+        send_home(2)
+
+    @pl.when(i == heads - 1)
+    def _():
+        for flow in sums:
+            flow.over_x()
+
+    @pl.when(i == heads)
+    def _():
+        first_ref[...] = qacc[...] + kvacc[:rows, :]
+        share_ref[...] = kvacc[rows:, :].astype(BF)
+        gain = jnp.zeros((1, kvacc.shape[1]), F32)
+        for ref, upstream in ((tok_ref, first_ref[...]), (ftok_ref, kvacc[rows:, :])):
+            v = ref[...].astype(F32)
+            gain = gain + jnp.sum(upstream * v * rms(v), axis=0, keepdims=True)
+        gain_ref[...] = gain
+        send_home(3)
+        over_x(0).wait_recv()
+        total = mid_ref[...] + near_ref[0].astype(F32) + xgot[0].astype(F32)
+        for n in (1, 2, 3):
+            home(n).wait_recv()
+            total = total + zgot[n - 1].astype(F32)
+        layer_ref[...] = total.astype(BF)
+        for flow in sums:
+            flow.pair.wait_recv()
+        lanes = sg_fin.shape[3] // 2
+        gate = more = down = 0.0
+        for k in range(8):
+            block = sg_fin[k % 2, k // 2]
+            gate = gate + dot(block[:, :lanes], spread_ref[k])
+            more = more + dot(block[:, lanes:], spread_ref[k])
+            down = down + dot(stack_ref[k], sd_fin[k % 2, k // 2])
+        sgout_ref[...] = gate
+        suout_ref[...] = more
+        sdout_ref[...] = down
+        for copy in pieces:
+            copy.wait()
+        for flow in sums:
+            for copy in flow.all:
+                copy.wait_send()
+        for n in range(4):
+            over_x(n).wait_send()
+        for n in (1, 2, 3):
+            home(n).wait_send()
+        for n in range(heads):
+            over_core(n).wait_send()
+
+
+def attend_back_and_sums(
+    q, kv_a, kv_b, d, lse, weights, tables, first_in, pairs, sgg, sdg, spread, stack, near, middle, away, piece
+):
+    rows, width = q.shape
+    half = kv_a.shape[1]
+    stages = near.shape[0]
+    dma = pltpu.SemaphoreType.DMA
+    once = pl.Buffered(1)
+    anywhere = pl.BlockSpec(memory_space=pl.ANY)
+
+    def fixed(v):
+        return pl.BlockSpec(v.shape, lambda i: (0,) * v.ndim, pipeline_mode=once)
+
+    def now(i):
+        return i - i // H
+
+    def before(i):
+        return i - 1 + (H - i) // H
+
+    def head(rows_of, at=now):
+        return pl.BlockSpec((rows_of, HD), lambda i: (0, at(i)))
+
+    def kv(which):
+        return pl.BlockSpec((None, half, HD), lambda i: (which, 0, now(i)))
+
+    def shape(dims, dtype):
+        return jax.ShapeDtypeStruct(dims, dtype)
+
+    def buffers(dims):
+        return [
+            pltpu.VMEM((2,) + dims, BF),
+            pltpu.VMEM(dims, BF),
+            pltpu.VMEM(dims, BF),
+            pltpu.VMEM((2, 4) + dims, BF),
+        ]
+
+    kept = [*tables, first_in, *pairs, sgg, sdg, spread, stack, near, middle]
+    ends = [
+        shape((rows, width), F32),
+        shape((rows, width), BF),
+        shape((1, width), F32),
+        shape((width // 4, spread.shape[2]), F32),
+        shape((width // 4, spread.shape[2]), F32),
+        shape((stack.shape[1], width), F32),
+        shape((rows, width), BF),
+    ]
+    return pl.pallas_call(
+        back_kernel,
+        grid=(H + 1,),
+        in_specs=[head(rows), kv(0), kv(0), kv(1), kv(1), head(rows), head(rows)]
+        + [head(width), head(width, before), head(width, before)]
+        + [fixed(v) for v in kept]
+        + [anywhere] * 2,
+        out_specs=[head(width), head(width, before), head(width, before)]
+        + [fixed(v) for v in ends]
+        + [anywhere],
+        out_shape=[shape((width, width), BF)] * 3 + ends + [shape(piece.shape, BF)],
+        scratch_shapes=[
+            pltpu.VMEM((H, 2, half, HD), BF),
+            pltpu.VMEM((H, 2, half, HD), BF),
+            pltpu.VMEM((2, 2, half, HD), F32),
+            pltpu.VMEM((half, width), F32),
+            pltpu.VMEM((rows, width), F32),
+        ]
+        + buffers(sgg.shape[2:])
+        + buffers(sdg.shape[2:])
+        + [
+            pltpu.VMEM((stages, rows, width), BF),
+            pltpu.VMEM((stages - 1, rows, width), BF),
+            pltpu.VMEM((stages - 1, rows, width), BF),
+        ]
+        + [dma((H,))] * 2
+        + [dma((6,))] * 4
+        + [dma((stages,))] * 4
+        + [dma((6,))] * 2,
+        compiler_params=pltpu.CompilerParams(
+            vmem_limit_bytes=60 * MIB, collective_id=3, has_side_effects=True
+        ),
+        cost_estimate=pl.CostEstimate(
+            flops=22 * rows * width * width,
+            bytes_accessed=60 * MIB,
+            transcendentals=rows * 2 * half * H,
+        ),
+    )(q, kv_a, kv_b, kv_a, kv_b, d, lse, *weights, *kept, away, piece)
+
+
 def tail_kernel(
     m0,
     m1,
     m2,
     m3,
-    sg_ref,
-    sd_ref,
     sm_ref,
     fb_ref,
     tok_ref,
     gain_ref,
     first_ref,
     mid_ref,
-    spread_ref,
-    stack_ref,
     out_ref,
-    sgout_ref,
-    suout_ref,
-    sdout_ref,
     smout_ref,
     tokout_ref,
     crecv,
@@ -919,14 +1327,6 @@
     xrecv,
     zrecv,
     fin,
-    sg_c,
-    sg_y,
-    sg_yr,
-    sg_fin,
-    sd_c,
-    sd_y,
-    sd_yr,
-    sd_fin,
     g_acc,
     g_recv,
     f_recv,
@@ -942,10 +1342,6 @@
     za_r,
     xa_s,
     xa_r,
-    s_s,
-    s_r,
-    d_s,
-    d_r,
     g_s,
     g_r,
     f_s,
@@ -1032,91 +1428,49 @@
             for i in range(2):
                 out_ref[m, i * half + j * part : i * half + (j + 1) * part, :] = fin[j, m, i]
 
-    class Flow:
-        def __init__(self, ref, got, to_far, from_far, fin, s, r):
-            self.ref, self.got, self.to_far, self.from_far, self.fin = ref, got, to_far, from_far, fin
-            self.core = mesh_copy(ref.at[:, 1 - c], got, s, r, 0, core)
-            self.far = mesh_copy(to_far, from_far, s, r, 1, far)
-            self.up = [
-                mesh_copy(fin.at[x, z], fin.at[x, z], s, r, 1 + k, up[k]) for k in range(1, 4)
-            ]
-            self.pair = mesh_copy(fin.at[x], fin.at[x], s, r, 5, pair)
-            self.all = [self.core, self.far, self.pair] + self.up
-
-        def step(self, t):
-            if t == 0:
-                self.core.wait_recv()
-                total = self.ref[1 - y, c].astype(F32) + self.got[1 - y].astype(F32)
-                self.to_far[...] = total.astype(BF)
-                self.far.start()
-            if t == 2:
-                self.far.wait_recv()
-                total = self.ref[y, c].astype(F32) + self.got[y].astype(F32)
-                self.fin[x, z] = (total + self.from_far[...].astype(F32)).astype(BF)
-                for copy in self.up:
-                    copy.start()
-            if t == 4:
-                for copy in self.up:
-                    copy.wait_recv()
-                self.pair.start()
-
-    flows = [
-        Flow(sg_ref, sg_c, sg_y, sg_yr, sg_fin, s_s, s_r),
-        Flow(sd_ref, sd_c, sd_y, sd_yr, sd_fin, d_s, d_r),
-    ]
     route = (core, far, pair, next_z, up[2])
     small = [
         mesh_copy(g_acc.at[i], g_recv.at[i], g_s, g_r, i, route[i]) for i in range(len(route))
     ]
+
     back = mesh_copy(fb_ref, f_recv, f_s, f_r, 0, far)
 
     def side(t):
-        for flow in flows:
-            flow.step(t)
-        if t < len(small):
-            small[t].wait_recv()
-            g_acc[t + 1] = g_acc[t] + g_recv[t]
-            if t + 1 < len(small):
-                small[t + 1].start()
-        if t == 6:
-            back.wait_recv()
+        if t == chunks - lead:
+            back.start()
+        if t % 2 == 1 and t // 2 < len(small):
+            i = t // 2
+            small[i].wait_recv()
+            g_acc[i + 1] = g_acc[i] + g_recv[i]
+            if i + 1 < len(small):
+                small[i + 1].start()
+        if t == chunks + 3:
+            back.wait()
             first_back = first_ref[...] + f_recv[...].astype(F32)
             values = tok_ref[...].astype(F32)
             to_tokens = norm_back(values, rms(values), gain_ref[...], first_back)
             tokout_ref[...] = mid_ref[...] + to_tokens
-        if t == 8:
-            for flow in flows:
-                flow.pair.wait_recv()
-            lanes = sg_fin.shape[3] // 2
-            gate = up_ = down = 0.0
-            for k in range(8):
-                block = sg_fin[k % 2, k // 2]
-                gate = gate + dot(block[:, :lanes], spread_ref[k])
-                up_ = up_ + dot(block[:, lanes:], spread_ref[k])
-                down = down + dot(stack_ref[k], sd_fin[k % 2, k // 2])
-            sgout_ref[...] = gate
-            suout_ref[...] = up_
-            sdout_ref[...] = down
-
+
+    lead = 3
     g_acc[0] = sm_ref[...]
     for m in range(4):
         over_core(0, m).start()
-    back.start()
-    for flow in flows:
-        flow.core.start()
     small[0].start()
     for j in range(1, chunks):
         for m in range(4):
             over_core(j, m).start()
-    steps = (add_core, add_y, add_x, add_z, end_z, end_x)
+    for j in range(lead):
+        add_core(j)
+    steps = (add_y, add_x, add_z, end_z, end_x)
     for t in range(chunks + len(steps) - 1):
+        if t + lead < chunks:
+            add_core(t + lead)
         for p in reversed(range(len(steps))):
             if 0 <= t - p < chunks:
                 steps[p](t - p)
         side(t)
     smout_ref[...] = g_acc[len(small)]
-    back.wait_send()
-    for copy in flows[0].all + flows[1].all + small:
+    for copy in small:
         copy.wait_send()
     for j in range(chunks):
         for m in range(4):
@@ -1128,31 +1482,19 @@
             back_z(j, s).wait_send()
 
 
-def tail(mats, sgg, sdg, small, share, tokens, gain, first_back, middle_back, spread, stack):
+def tail(mats, small, share, tokens, gain, first_back, middle_back):
     width = mats[0].shape[1]
     half = width // 8
     part = 16
     chunks = half // part
     dma = pltpu.SemaphoreType.DMA
     vmem = pl.BlockSpec(memory_space=pltpu.VMEM)
-
-    def buffers(shape):
-        return [
-            pltpu.VMEM((2,) + shape, BF),
-            pltpu.VMEM(shape, BF),
-            pltpu.VMEM(shape, BF),
-            pltpu.VMEM((2, 4) + shape, BF),
-        ]
-
     return pl.pallas_call(
         tail_kernel,
-        in_specs=[vmem] * 14,
-        out_specs=[vmem] * 6,
+        in_specs=[vmem] * 10,
+        out_specs=[vmem] * 3,
         out_shape=[
             jax.ShapeDtypeStruct((4, 2 * half, width), BF),
-            jax.ShapeDtypeStruct((2 * half, spread.shape[2]), F32),
-            jax.ShapeDtypeStruct((2 * half, spread.shape[2]), F32),
-            jax.ShapeDtypeStruct((stack.shape[1], width), F32),
             jax.ShapeDtypeStruct(small.shape, F32),
             jax.ShapeDtypeStruct(tokens.shape, F32),
         ],
@@ -1164,10 +1506,6 @@
             pltpu.VMEM((chunks, 4, part, width), BF),
             pltpu.VMEM((chunks, 3, part, width), BF),
             pltpu.VMEM((chunks, 4, 2, part, width), BF),
-        ]
-        + buffers(sgg.shape[2:])
-        + buffers(sdg.shape[2:])
-        + [
             pltpu.VMEM((6,) + small.shape, F32),
             pltpu.VMEM((5,) + small.shape, F32),
             pltpu.VMEM(share.shape, BF),
@@ -1176,25 +1514,20 @@
         + [dma((chunks,))] * 4
         + [dma((3 * chunks,))] * 4
         + [dma((chunks,))] * 2
-        + [dma((6,))] * 4
         + [dma((5,))] * 2
         + [dma((1,))] * 2,
         compiler_params=pltpu.CompilerParams(
-            vmem_limit_bytes=62 * MIB, collective_id=2, has_side_effects=True
+            vmem_limit_bytes=60 * MIB, collective_id=2, has_side_effects=True
         ),
         cost_estimate=pl.CostEstimate(flops=0, bytes_accessed=300 * MIB, transcendentals=0),
     )(
         *[m.reshape(2, 2, 2, half, width) for m in mats],
-        sgg,
-        sdg,
         small,
         share,
         tokens,
         gain,
         first_back,
         middle_back,
-        spread,
-        stack,
     )
 
 
@@ -1248,12 +1581,13 @@
     tiny = [attn_gain[:, None], ffn_gain[:, None], router_weight]
     small = jnp.concatenate(tiny + [jnp.zeros((width // 4, LANES - 2 - total), BF)], axis=1)
 
-    def mine(v):
-        v = v.reshape(width // 4, 4, -1)
-        v = lax.dynamic_slice_in_dim(v, e * units, units, axis=2).reshape(width // 4, 4 * units)
-        return jnp.pad(v, ((0, 0), (0, LANES - 4 * units)))
-
-    small = jnp.concatenate([small, mine(shared_gate), mine(shared_up)], axis=1)
+    unit = jnp.arange(LANES)
+    to = (unit // pad) * (ep * units) + unit % pad
+    to = jnp.where((unit < 4 * pad) & (unit % pad < units), to, -ep * units)
+    column = jnp.arange(4 * ep * units)
+    mine = (column[:, None] == (to + e * units)[None, :]).astype(BF)
+    small = [small, dot(shared_gate, mine).astype(BF), dot(shared_up, mine).astype(BF)]
+    small = jnp.concatenate(small, axis=1)
     sd = lax.dynamic_slice_in_dim(shared_down, e * units, units, axis=0)
     sd = jnp.pad(sd, ((0, pad - units), (0, 0)))
     blocks = [key_weight, value_weight, query_weight, out_weight, small, sd]
@@ -1277,16 +1611,9 @@
     gain_two = small[:, 1].astype(F32)[None, :]
     router = small[:, 2 : 2 + total]
     sg, su = small[:, LANES : 2 * LANES], small[:, 2 * LANES :]
-    sd = blocks[5][:, :units].reshape(4 * units, width)
-    sd = jnp.pad(sd, ((0, LANES - 4 * units), (0, 0)))
-
-    expert = jnp.arange(total, dtype=jnp.int32)
-    hit_each = routes[:, :, None] == expert[None, None, :]
-    hit = jnp.any(hit_each, axis=1)
-    kept = jnp.sum(jnp.where(hit_each, keep_mask[:, :, None], 0), axis=1)
-    below = (jnp.arange(rows)[:, None] > jnp.arange(rows)[None, :]).astype(BF)
-    place = jnp.where(hit, dot(below, hit.astype(BF)), -1.0)
-    kept = kept.astype(F32)
+    sd = blocks[5].reshape(4 * pad, width)
+    if 4 * pad < LANES:
+        sd = jnp.pad(sd, ((0, LANES - 4 * pad), (0, 0)))
 
     pos = jnp.arange(rows, dtype=jnp.int32)
     pos = jnp.concatenate([(h ^ i) * rows + pos for i in (0, 2, 1, 3)])
@@ -1296,24 +1623,25 @@
     first_in, kv_a, query = project(tokens, far_tokens, gain_one, k_w, v_w, q_w, *table)
     kv_b = swap_core(kv_a)
     mixed, lse = attend(h_arr, query, kv_a, kv_b)
+    routes, keep_mask, late = after((routes, keep_mask, jnp.arange(ep)), query)
+    if fused:
+        mixed = after(mixed, g_far)
     middle = residual + dot(mixed, o_w)
     inv_two = rms(middle)
     second_in = (middle * inv_two * gain_two).astype(BF)
+
+    expert = jnp.arange(total, dtype=jnp.int32)
+    hit_each = routes[:, :, None] == expert[None, None, :]
+    hit = jnp.any(hit_each, axis=1)
+    kept = jnp.sum(jnp.where(hit_each, keep_mask[:, :, None], 0), axis=1)
+    below = (jnp.arange(rows)[:, None] > jnp.arange(rows)[None, :]).astype(BF)
+    place = jnp.where(hit, dot(below, hit.astype(BF)), -1.0)
+    kept = kept.astype(F32)
 
     logits = jnp.where(hit, dot(second_in, router), -1e30)
     gates_of = jnp.where(hit, jnp.exp(logits - jnp.max(logits, axis=1, keepdims=True)), 0.0)
     gates_of = gates_of / jnp.sum(gates_of, axis=1, keepdims=True)
     pair_weight = gates_of * kept
-    x_ext = jnp.concatenate(
-        [
-            second_in,
-            pair_weight.astype(BF),
-            place.astype(BF),
-            jnp.zeros((rows, LANES - 2 * total), BF),
-        ],
-        axis=1,
-    )
-
     flat = (2, ep * capacity)
 
     hidden = expert_down.shape[1]
@@ -1322,16 +1650,12 @@
         return jnp.einsum("xna,xnb->xab", left, right, preferred_element_type=F32)
 
     if fused:
-        experts = [
-            experts,
-            experts_far,
-            experts_core,
-            swap_core(after(experts_far, mixed)),
-        ]
-        dx_sum, near, far, sgg, sdg, xr, gr, gu, wa = dispatch(
-            capacity, total, x_ext, g_near, g_far, experts, sg, su, sd
+        meta = jnp.concatenate([pair_weight.T, place.T], axis=0)
+        experts = [experts, experts_far, experts_core]
+        dx_sum, weight_back, near, far, sgg, sdg, xr, gr, gu, wa = dispatch(
+            capacity, total, second_in, meta, g_near, g_far, experts, sg, su, sd
         )
-        far = swap_pair(far)
+        weight_back = weight_back.T
         wide = wa.shape[3] // 4
         xr, gr, gu, wa = (v.reshape(flat + (v.shape[-1],)) for v in (xr, gr, gu, wa))
         gu = expert_grad(gu, xr).astype(BF)
@@ -1345,8 +1669,16 @@
         piece_near = [piece(r) for r in (0, 1)]
         piece_core = swap_core(jnp.stack([piece(r) for r in (2, 3)]))
         piece_sum = (piece_near[1].astype(F32) + piece_core[1].astype(F32)).astype(BF)
-        piece_far = swap_y(piece_sum)
     else:
+        x_ext = jnp.concatenate(
+            [
+                second_in,
+                pair_weight.astype(BF),
+                place.astype(BF),
+                jnp.zeros((rows, LANES - 2 * total), BF),
+            ],
+            axis=1,
+        )
         x_blocks = gather_ep(after(x_ext, g_blocks))
         carry = (jnp.zeros((width, 2 * LANES), F32), jnp.zeros((LANES, width), F32))
         bufs, dx_parts = None, []
@@ -1375,6 +1707,10 @@
             )
             dx_parts.append(dx)
         dx_sum = scatter_ep(dx_parts)
+        weight_back = (
+            dx_sum[:, width : width + total] + dx_sum[:, width + total : width + 2 * total]
+        )
+        dx_sum = dx_sum[:, :width]
         sgg, sdg = carry
         sa, xr, gr, gi, ui, wa = bufs
         out_parts = [
@@ -1399,12 +1735,11 @@
         )
 
     grad_out = cotangent.astype(F32)
-    weight_back = dx_sum[:, width : width + total] + dx_sum[:, width + total : width + 2 * total]
     gate_back = weight_back * kept
     chosen_back = gates_of * (gate_back - jnp.sum(gates_of * gate_back, axis=1, keepdims=True))
     logits_back = chosen_back.astype(BF)
     router_part = dot(logits_back, second_in, (0, 0))
-    second_back = dx_sum[:, :width] + dot(logits_back, router, (1, 1))
+    second_back = dx_sum + dot(logits_back, router, (1, 1))
     gain_two_part = jnp.sum(second_back * middle * inv_two, axis=0)
     middle_back = grad_out + norm_back(middle, inv_two, gain_two, second_back)
     attn_back = middle_back.astype(BF)
@@ -1414,77 +1749,91 @@
     if fused:
         mixed_back = after(mixed_back, piece_sum)
     out_part = dot(mixed, attn_back, (0, 0))
-    query_raw, near_back, far_back = attend_back(
-        h_arr, query, kv_a, kv_b, mixed_back, lse, cosine, sine
-    )
-    kv_raw = (near_back + swap_core(far_back).astype(F32)).astype(BF)
-    key_raw, value_raw = kv_raw[0], kv_raw[1]
+    sgg = sgg.reshape(4, width // 4, 2 * LANES)
+    sdg = sdg[: 4 * pad].reshape(4, pad, width)
+    block = late[:, None, None] * units
+    spread = (to[None, :, None] + block == column[None, None, :]).astype(BF)
+
+    def small_sums(gain_one_part):
+        lines = [router_part, gain_two_part[None, :], counts_part[None, :], gain_one_part]
+        return jnp.concatenate(lines + [jnp.zeros((-(total + 3) % 8, width), F32)], axis=0)
+
     if fused:
-        both_out = near.astype(F32) + after(far, query_raw).astype(F32)
-        low_out = both_out.astype(BF)
-        routed = [shift(low_out[k], stages - k) for k in range(1, stages)]
-    kv_back = dot(key_raw, k_w, (1, 1)) + dot(value_raw, v_w, (1, 1))
-    q_back = dot(query_raw, q_w, (1, 1))
-    share = kv_back[rows:].astype(BF)
-    q_part = dot(first_in[:rows], query_raw, (0, 0))
-    k_part = dot(first_in, key_raw, (0, 0))
-    v_part = dot(first_in, value_raw, (0, 0))
-    first_back = kv_back[:rows] + q_back
-    gain_one_part = jnp.zeros((1, width), F32)
-    for values, upstream in ((tokens, first_back), (far_tokens, kv_back[rows:])):
-        values = values.astype(F32)
-        gain_one_part += jnp.sum(upstream * values * rms(values), axis=0, keepdims=True)
-    sums = [router_part, gain_two_part[None, :], counts_part[None, :], gain_one_part]
-    sums = jnp.concatenate(sums + [jnp.zeros((-(total + 3) % 8, width), F32)], axis=0)
-    parts = [q_part, k_part, v_part, out_part]
-
-    sgg = sgg.reshape(4, width // 4, 2 * LANES)
-    sdg = sdg[: 4 * units].reshape(4, units, width)
-    unit = jnp.arange(LANES)
-    to = (unit // units) * (ep * units) + unit % units
-    to = jnp.where(unit < 4 * units, to, -ep * units)[None, :, None]
-    block = jnp.arange(ep)[:, None, None] * units
-    spread = (to + block == jnp.arange(4 * ep * units)[None, None, :]).astype(BF)
-    if fused:
-        sdg = jnp.pad(sdg, ((0, 0), (0, pad - units), (0, 0))).astype(BF)
+        sdg = sdg.astype(BF)
         at = jnp.where(jnp.arange(pad) < units, jnp.arange(pad), -ep * units)[None, None, :]
         stack = (at + block == jnp.arange(ep * units)[None, :, None]).astype(BF)
-        out, sgate_grad, sup_grad, sdown_grad, sums, tokens_grad = tail(
-            [v.astype(BF) for v in parts],
+        (
+            q_part,
+            k_part,
+            v_part,
+            first_back,
+            share,
+            gain_one_part,
+            sgate_grad,
+            sup_grad,
+            sdown_grad,
+            layer,
+            piece_far,
+        ) = attend_back_and_sums(
+            query,
+            kv_a,
+            kv_b,
+            mixed_back,
+            lse,
+            (q_w, k_w, v_w),
+            (cosine, sine),
+            first_in,
+            (tokens, far_tokens),
             sgg.astype(BF).reshape(2, 2, width // 4, 2 * LANES),
             sdg.reshape(2, 2, pad, width),
-            after(sums, piece_far),
+            spread,
+            stack,
+            near,
+            middle,
+            far,
+            piece_sum,
+        )
+        out, sums, tokens_grad = tail(
+            [q_part, k_part, v_part, out_part.astype(BF)],
+            small_sums(gain_one_part),
             share,
             tokens,
             gain_one,
             first_back,
             middle_back,
-            spread,
-            stack,
         )
         grads = [out[i].astype(F32) for i in range(4)]
-        routed = after(routed, sums)
-        routed = both_out[0] + sum(v.astype(F32) for v in routed)
-        piece_far = after(piece_far, sums)
         expert_sum = sum(v.astype(F32) for v in (piece_near[0], piece_core[0], piece_far))
     else:
+        query_raw, near_back, far_back = attend_back(
+            h_arr, query, kv_a, kv_b, mixed_back, lse, cosine, sine
+        )
+        kv_raw = (near_back + swap_core(far_back).astype(F32)).astype(BF)
+        key_raw, value_raw = kv_raw[0], kv_raw[1]
+        kv_back = dot(key_raw, k_w, (1, 1)) + dot(value_raw, v_w, (1, 1))
+        q_part = dot(first_in[:rows], query_raw, (0, 0))
+        k_part = dot(first_in, key_raw, (0, 0))
+        v_part = dot(first_in, value_raw, (0, 0))
+        first_back = kv_back[:rows] + dot(query_raw, q_w, (1, 1))
+        gain_one_part = jnp.zeros((1, width), F32)
+        for values, upstream in ((tokens, first_back), (far_tokens, kv_back[rows:])):
+            values = values.astype(F32)
+            gain_one_part += jnp.sum(upstream * values * rms(values), axis=0, keepdims=True)
 
         def over_hp(v):
             return scatter_hp(jnp.split(relative(v, h, 0), 4, axis=0))
 
-        grads = [sum_ep(over_hp(v), e) for v in parts]
-        sums = sum_all_small(sums)
-        first_back = first_back + swap_y(share).astype(F32)
+        grads = [sum_ep(over_hp(v), e) for v in (q_part, k_part, v_part, out_part)]
+        sums = sum_all_small(small_sums(gain_one_part))
+        first_back = first_back + swap_y(kv_back[rows:].astype(BF)).astype(F32)
         tokens_grad = middle_back + norm_back(residual, rms(residual), gain_one, first_back)
-        sgg, sdg = (
-            spread_ep(over_hp(v)[0].astype(BF), e) for v in (sgg, sdg)
-        )
+        sgg, sdg = (spread_ep(over_hp(v)[0].astype(BF), e) for v in (sgg, sdg))
         sgate_grad, sup_grad = (
             jnp.einsum("kra,kan->rn", v, spread, preferred_element_type=F32)
             for v in (sgg[:, :, :LANES], sgg[:, :, LANES:])
         )
-        sdown_grad = sdg.reshape(ep * units, width).astype(F32)
-    layer = (middle + routed).astype(BF)
+        sdown_grad = sdg[:, :units].reshape(ep * units, width).astype(F32)
+        layer = (middle + routed).astype(BF)
     gate_grad, up_grad = (
         jnp.swapaxes(expert_sum[:, i * hidden : (i + 1) * hidden], 1, 2) for i in (0, 1)
     )

time: 732 us -> 629 us (0.86)
  waiting for transfers between devices: 150 us -> 62.2 us
  Pallas kernels: 412 us -> 449 us
  local copies, waits for them, and re-layouts: 58.4 us -> 36.5 us
  matrix products: 58.1 us -> 41.3 us
  other arithmetic: 39.1 us -> 30.3 us
    ppermute x2 -> x1, waiting for transfers between devices: 72.1 us -> 15.6 us  [swap_y(): return lax.ppermute(v, 'hp', [(i, i ^ 2) for i in range(4)])]
    pallas_call x2, Pallas kernels: 188 us -> 238 us  [the longest x1 127 us: tail(): pl.pallas_call(tail_kernel, in_specs=[vmem] * 10, out_specs=[vmem] * 3, o...]
    ppermute x2 -> x1, waiting for transfers between devices: 70.9 us -> 45.2 us  [swap_pair(): return lax.ppermute(v, 'ep', [(i, i ^ 1) for i in range(n)])]
    dot_general x13 -> x9, matrix products: 26.9 us -> 10 us  [dot(): lax.dot_general(left, right, (((over[0],), (over[1],)), ((), ())), prefer...]
    pallas_call x1, Pallas kernels: 140 us -> 126 us  [dispatch(): pl.pallas_call(functools.partial(dispatch_kernel, capacity, total), grid=...]
    unnamed x153 -> x122, local copies, waits for them, and re-layouts: 28 us -> 17.8 us
    convert_element_type x5 -> x2, other arithmetic: 12.4 us -> 2.37 us  [the longest x1 1.6 us: per_device(): spread = (to[None, :, None] + block == column[None, None, :]).astype(BF)]
  transfers between devices with their start and end apart: 11 -> 4, of which waited for: 6 -> 3; matrix products, arithmetic and copies ran while one was open for 10% -> 3% of each run, Pallas kernels for 28% -> 2%
where the time goes in v4:
time: 629 us; the launch traced here: 623 us
  Pallas kernels  449 us (71%)
  waiting for transfers between devices  62.2 us (10%)
  matrix products  41.3 us (7%)
  local copies, waits for them, and re-layouts  36.5 us (6%)
  other arithmetic  30.3 us (5%)
    pallas_call x1, Pallas kernels, tail(): pl.pallas_call(tail_kernel, in_specs=[vmem] * 10, out_specs=[vmem] * 3, o...  127 us
    pallas_call x1, Pallas kernels, dispatch(): pl.pallas_call(functools.partial(dispatch_kernel, capacity, total), grid=...  126 us
    pallas_call x1, Pallas kernels, attend_back_and_sums(): pl.pallas_call(back_kernel, grid=(H + 1,), in_specs=[head(rows), kv(0), k...  111 us
    pallas_call x1, Pallas kernels, front(): pl.pallas_call(functools.partial(front_kernel, large, count), in_specs=[a...  67 us
    ppermute x1, waiting for transfers between devices, swap_pair(): return lax.ppermute(v, 'ep', [(i, i ^ 1) for i in range(n)])  45.2 us
    dot_general x2, matrix products, expert_grad(): return jnp.einsum('xna,xnb->xab', left, right, preferred_element_type=F32)  31.3 us
    unnamed x122, local copies, waits for them, and re-layouts  17.8 us
    ppermute x1, waiting for transfers between devices, swap_y(): return lax.ppermute(v, 'hp', [(i, i ^ 2) for i in range(4)])  15.6 us
  transfers between devices with their start and end apart: 4, of which 3 were waited for; matrix products, arithmetic and copies ran while one was open for 3% of the time, Pallas kernels for 2%

profile of v4, /device:TPU:0, one launch (start us, length us, event | category | flops | bytes accessed | tf_op | source)
XLA Modules:
  0.0 622.9 jit_solution(5081786312006395694)
XLA Ops:
  0.8 3.1 multiply_sine_fusion
  5.2 1.4 fusion.4
  8.0 3.5 pad_maximum_fusion.1.refs_1_.refs_0_
  12.8 1.1 copy-done.19
  14.0 1.1 copy-done.20
  15.1 67.0 %shard_map.288 = (bf16[256,1280]{1,0:T(8,128)(2,1)S(1)}, bf16[2,672,1280]{2,1,0:T(8,128)(2,1)}, bf16[4,256,1280]{2,1,0:T(8,128)(2,1)}, bf16[4,320,1280]{2,1,0:T(...) custom-call(bf16[256,1280]{1,0:T(8,128)(2,1)S(1)} %copy-done.7, ...), custom_call_target="tpu_custom_call" | custom-call | bytes 125829120 | tf_op jit(solution)/shard_map/pallas_call | solution.py:957
  82.1 1.7 copy-done.6
  83.9 1.8 copy-done.22
  86.2 8.5 %shard_map.289 = (bf16[512,1280]{1,0:T(8,128)(2,1)S(1)}, bf16[2,512,1280]{2,1,0:T(8,128)(2,1)S(1)}, bf16[256,1280]{1,0:T(8,128)(2,1)S(1)}) custom-call(bf16[256,1280]{1,0:T(8,128)(2,1)S(1)} %copy-done.7, bf16[256,1280]{1,0:T(8,128)(2,1)S(1)} %get-tuple-element.61.f_ref.ftok_ref, f32[1,1280]{1,0:T(1,128)S(1)} %reshape.312.gain_ref, ...), custom_call_target="tpu_custom_call" | custom-call | tf_op jit(solution)/shard_map/pallas_call | solution.py:195
  96.2 1.5 collective-permute-start.1
  99.3 1.4 collective-permute-done.kb_ref.vb_ref
  100.7 9.5 %shard_map.290 = (bf16[256,1280]{1,0:T(8,128)(2,1)S(1)}, f32[256,1280]{1,0:T(8,128)S(1)}) custom-call(s32[1]{0:T(128)} %bitcast.8.h_ref, bf16[256,1280]{1,0:T(8,128)(2,1)S(1)} %get-tuple-element.66.q_ref, bf16[2,512,1280]{2,1,0:T(8,128)(2,1)S(1)} %get-tuple-element.67.ka_ref.va_ref, bf16[2,512,1280]{2,1,0:T(8,128)(2,1)S(1)} %collective-permute-done.kb_ref.vb_ref, ...), custom_call_target="tpu_custom_call" | custom-call | tf_op jit(solution)/shard_map/pallas_call | solution.py:277
  110.3 45.2 %collective-permute-done.1.g1_ref = bf16[4,256,1280]{2,1,0:T(8,128)(2,1)} collective-permute-done((bf16[4,256,1280]{2,1,0:T(8,128)(2,1)}, bf16[4,256,1280]{2,1,0:T(8,128)(2,1)}, u32[]{:S(2)}, u32[]{:S(2)}) %collective-permute-start.1) | collective-permute-done | bytes 2621472 | tf_op jit(solution)/shard_map/ppermute | solution.py:35
  158.3 15.6 %collective-permute-done.2.refs_1_ = bf16[2,672,1280]{2,1,0:T(8,128)(2,1)S(1)} collective-permute-done((bf16[2,672,1280]{2,1,0:T(8,128)(2,1)S(1)}, bf16[2,672,1280]{2,1,0:T(8,128)(2,1)S(1)}, u32[]{:S(2)}, u32[]{:S(2)}) %collective-permute-start.2) | collective-permute-done | bytes 3440672 | tf_op jit(solution)/shard_map/ppermute | solution.py:30
  173.9 1.8 copy-done.57
  175.7 125.6 %shard_map.291 = (f32[256,1280]{1,0:T(8,128)}, f32[16,256]{1,0:T(8,128)}, bf16[4,256,1280]{2,1,0:T(8,128)(2,1)}, bf16[4,256,1280]{2,1,0:T(8,128)(2,1)}, f32[1280...) custom-call(bf16[256,1280]{1,0:T(8,128)(2,1)} %copy-done.30, ...), custom_call_target="tpu_custom_call" | custom-call | flops 31708938240 | bytes 83886080 | tf_op jit(solution)/shard_map/pallas_call | solution.py:803
  301.3 10.7 %convolution_convert_fusion.2 = bf16[2,1024,1280]{2,1,0:T(8,128)(2,1)S(1)} fusion(bf16[2,1152,1024]{2,1,0:T(8,128)(2,1)} %bitcast.123, bf16[2,1152,1280]{2,1,0:T(8,128)(2,1)} %bitcast.122), kind=kOutput, calls=%fused_computation.7 | convolution fusion | flops 6042419200 | bytes 15859712 | tf_op jit(solution)/shard_map/xna,xnb->xab/dot_general | solution.py:1650
  312.0 1.3 fusion.32
  313.3 20.6 %convolution_convert_fusion = bf16[2,2048,1280]{2,1,0:T(8,128)(2,1)} fusion(bf16[2,1152,2048]{2,1,0:T(8,128)(2,1)} %bitcast.120, bf16[2,1152,1280]{2,1,0:T(8,128)(2,1)} %bitcast.121), kind=kOutput, calls=%fused_computation | convolution fusion | flops 12084838400 | bytes 25821184 | tf_op jit(solution)/shard_map/xna,xnb->xab/dot_general | solution.py:1650
  333.9 5.9 fusion.30
  340.7 3.5 pad_maximum_fusion
  347.3 1.6 fusion.2.spread_ref
  350.7 1.7 multiply_reduce_fusion
  353.5 2.7 convolution_convert_fusion.1
  356.9 1.9 convolution_convert_fusion.3.d_ref
  358.8 3.8 fusion.1.piece_ref
  362.6 111.1 %shard_map.292 = (bf16[1280,1280]{1,0:T(8,128)(2,1)}, bf16[1280,1280]{1,0:T(8,128)(2,1)}, bf16[1280,1280]{1,0:T(8,128)(2,1)}, f32[256,1280]{1,0:T(8,128)}, bf16[...) custom-call(bf16[256,1280]{1,0:T(8,128)(2,1)} %copy-done.12, ...), custom_call_target="tpu_custom_call" | custom-call | flops 9227468800 | bytes 62914560 | tf_op jit(solution)/shard_map/pallas_call | solution.py:1269
  473.7 2.0 concatenate.46.sm_ref
  475.7 127.0 %shard_map.293 = (bf16[4,320,1280]{2,1,0:T(8,128)(2,1)}, f32[24,1280]{1,0:T(8,128)}, f32[256,1280]{1,0:T(8,128)}) custom-call(bf16[2,2,2,160,1280]{4,3,2,1,0:T(8,128)(2,1)} %bitcast.113, bf16[2,2,2,160,1280]{4,3,2,1,0:T(8,128)(2,1)} %bitcast.114, bf16[2,2,2,160,1280]{4,3,2,1,0:T(8,128)(2,1)} %bitcast.115, bf16[2,2,2,160,1280]{4,3,2,1,0:T(8,128)(2,1)} %bitcast.112, ...), custom_call_target="tpu_custom_call" | custom-call | bytes 314572800 | tf_op jit(solution)/shard_map/pallas_call | solution.py:1492
  604.5 3.8 fusion
  608.4 3.4 fusion.31
  612.3 2.9 bitcast_convert_fusion
  (175 shorter events, 27.7 us)
Async XLA Ops:
  0.7 5.9 copy-start.55
  0.7 6.0 copy-start.56
  0.7 6.2 copy-start.53
  15.1 70.9 %copy-start.33 = (f32[1024,64]{1,0:T(8,128)S(1)}, f32[1024,64]{1,0:T(8,128)}, u32[]{:S(2)}) copy-start(f32[1024,64]{1,0:T(8,128)} %get-tuple-element.136) | copy-start | bytes 786436
  15.1 70.9 %copy-start.35 = (f32[1024,64]{1,0:T(8,128)S(1)}, f32[1024,64]{1,0:T(8,128)}, u32[]{:S(2)}) copy-start(f32[1024,64]{1,0:T(8,128)} %get-tuple-element.137) | copy-start | bytes 786436
  85.6 9.1 %copy-start.4 = (bf16[4,320,1280]{2,1,0:T(8,128)(2,1)}, bf16[4,320,1280]{2,1,0:T(8,128)(2,1)S(1)}, u32[]{:S(2)}) copy-start(bf16[4,320,1280]{2,1,0:T(8,128)(2,1)S(1)} %get-tuple-element.63) | copy-start | bytes 9830404
  85.6 9.1 %copy-start.5 = (bf16[4,320,1280]{2,1,0:T(8,128)(2,1)}, bf16[4,320,1280]{2,1,0:T(8,128)(2,1)S(1)}, u32[]{:S(2)}) copy-start(bf16[4,320,1280]{2,1,0:T(8,128)(2,1)S(1)} %get-tuple-element.64) | copy-start | bytes 9830404
  85.6 9.1 %copy-start.11 = (bf16[256,1280]{1,0:T(8,128)(2,1)}, bf16[256,1280]{1,0:T(8,128)(2,1)S(1)}, u32[]{:S(2)}) copy-start(bf16[256,1280]{1,0:T(8,128)(2,1)S(1)} %get-tuple-element.61.f_ref.ftok_ref) | copy-start | bytes 1966084
  85.6 9.1 %copy-start.25 = (bf16[4,32,1280]{2,1,0:T(8,128)(2,1)}, bf16[4,32,1280]{2,1,0:T(8,128)(2,1)S(1)}, u32[]{:S(2)}) copy-start(bf16[4,32,1280]{2,1,0:T(8,128)(2,1)S(1)} %get-tuple-element.76) | copy-start | bytes 983044
  85.6 71.1 %copy-start.8 = (bf16[4,320,384]{2,1,0:T(8,128)(2,1)}, bf16[4,320,384]{2,1,0:T(8,128)(2,1)S(1)}, u32[]{:S(2)}) copy-start(bf16[4,320,384]{2,1,0:T(8,128)(2,1)S(1)} %get-tuple-element.62) | copy-start | bytes 2949124
  86.0 8.7 %copy-start.21 = (f32[1,1280]{1,0:T(1,128)}, f32[1,1280]{1,0:T(1,128)S(1)}, u32[]{:S(2)}) copy-start(f32[1,1280]{1,0:T(1,128)S(1)} %reshape.312.gain_ref) | copy-start | bytes 15364
  86.2 11.5 %copy-start.28 = (bf16[2,672,1280]{2,1,0:T(8,128)(2,1)S(1)}, bf16[2,672,1280]{2,1,0:T(8,128)(2,1)}, u32[]{:S(2)}) copy-start(bf16[2,672,1280]{2,1,0:T(8,128)(2,1)} %pad_maximum_fusion.1.refs_1_.refs_0_) | copy-start | bytes 10321924
  86.2 12.0 %copy-start.52 = (s32[256,7]{0,1:T(8,128)S(1)}, s32[256,7]{0,1:T(8,128)}, u32[]{:S(2)}) copy-start(s32[256,7]{0,1:T(8,128)} %param.31) | copy-start | bytes 21508
  86.2 12.0 %copy-start.54 = (s32[256,7]{0,1:T(8,128)S(1)}, s32[256,7]{0,1:T(8,128)}, u32[]{:S(2)}) copy-start(s32[256,7]{0,1:T(8,128)} %param.32) | copy-start | bytes 21508
  95.8 14.4 %copy-start.2 = (bf16[2,512,1280]{2,1,0:T(8,128)(2,1)}, bf16[2,512,1280]{2,1,0:T(8,128)(2,1)S(1)}, u32[]{:S(2)}) copy-start(bf16[2,512,1280]{2,1,0:T(8,128)(2,1)S(1)} %get-tuple-element.67.ka_ref.va_ref) | copy-start | bytes 7864324
  95.8 14.4 %copy-start.12 = (bf16[256,1280]{1,0:T(8,128)(2,1)}, bf16[256,1280]{1,0:T(8,128)(2,1)S(1)}, u32[]{:S(2)}) copy-start(bf16[256,1280]{1,0:T(8,128)(2,1)S(1)} %get-tuple-element.66.q_ref) | copy-start | bytes 1966084
  95.8 4.9 collective-permute-start
  96.2 59.2 %collective-permute-start.1 = (bf16[4,256,1280]{2,1,0:T(8,128)(2,1)}, bf16[4,256,1280]{2,1,0:T(8,128)(2,1)}, u32[]{:S(2)}, u32[]{:S(2)}) collective-permute-start(bf16[4,256,1280]{2,1,0:T(8,128)(2,1)} %get-tuple-element.69.g0_ref), channel_id=1, source_target_pairs={{0,4},{4,0},{8,12},{12,8},{16,20},{20,16},{24,28},{28,24},{1,5},{5... | collective-permute-start | bytes 7864328 | tf_op jit(solution)/shard_map/ppermute | solution.py:35
  97.7 76.2 %collective-permute-start.2 = (bf16[2,672,1280]{2,1,0:T(8,128)(2,1)S(1)}, bf16[2,672,1280]{2,1,0:T(8,128)(2,1)S(1)}, u32[]{:S(2)}, u32[]{:S(2)}) collective-permute-start(bf16[2,672,1280]{2,1,0:T(8,128)(2,1)S(1)} %copy-done.28), channel_id=1, source_target_pairs={{0,2},{1,3},{2,0},{3,1},{4,6},{5,7},{6,4},{7,5},{8,10},{9,11},{10,... | collective-permute-start | bytes 10321928 | tf_op jit(solution)/shard_map/ppermute | solution.py:30
  100.7 9.5 %copy-start.3 = (bf16[2,512,1280]{2,1,0:T(8,128)(2,1)}, bf16[2,512,1280]{2,1,0:T(8,128)(2,1)S(1)}, u32[]{:S(2)}) copy-start(bf16[2,512,1280]{2,1,0:T(8,128)(2,1)S(1)} %collective-permute-done.kb_ref.vb_ref) | copy-start | bytes 7864324
  100.7 54.7 %copy-start.23 = (bf16[4,320,1280]{2,1,0:T(8,128)(2,1)S(1)}, bf16[4,320,1280]{2,1,0:T(8,128)(2,1)}, u32[]{:S(2)}) copy-start(bf16[4,320,1280]{2,1,0:T(8,128)(2,1)} %copy-done.22) | copy-start | bytes 9830404
  110.2 46.5 %copy-start.13 = (bf16[256,1280]{1,0:T(8,128)(2,1)}, bf16[256,1280]{1,0:T(8,128)(2,1)S(1)}, u32[]{:S(2)}) copy-start(bf16[256,1280]{1,0:T(8,128)(2,1)S(1)} %get-tuple-element.70) | copy-start | bytes 1966084
  110.2 46.5 %copy-start.16 = (f32[256,1280]{1,0:T(8,128)}, f32[256,1280]{1,0:T(8,128)S(1)}, u32[]{:S(2)}) copy-start(f32[256,1280]{1,0:T(8,128)S(1)} %get-tuple-element.85.lse_ref) | copy-start | bytes 3932164
  156.8 17.1 %copy-start.30 = (bf16[256,1280]{1,0:T(8,128)(2,1)}, bf16[256,1280]{1,0:T(8,128)(2,1)S(1)}, u32[]{:S(2)}) copy-start(bf16[256,1280]{1,0:T(8,128)(2,1)S(1)} %multiply_convert_fusion.x_ref) | copy-start | bytes 1966084
  344.1 14.6 %collective-permute-start.3 = (bf16[2,2,672,1280]{3,2,1,0:T(8,128)(2,1)}, bf16[2,2,672,1280]{3,2,1,0:T(8,128)(2,1)}, u32[]{:S(2)}, u32[]{:S(2)}) collective-permute-start(bf16[2,2,672,1280]{3,2,1,0:T(8,128)(2,1)} %pad_maximum_fusion), channel_id=1, source_target_pairs={{0,1},{1,0},{2,3},{3,2},{4,5},{5,4},{6,7},{7,6},{8,9},{9,8},{10,11... | collective-permute-start | bytes 20643848 | tf_op jit(solution)/shard_map/ppermute | solution.py:26
  344.2 5.6 copy-start.50
  345.2 5.5 copy-start.27
  345.2 5.5 copy-start.32
  475.7 128.8 %copy-start.39 = (bf16[2,224,1280]{2,1,0:T(8,128)(2,1)S(1)}, bf16[2,224,1280]{2,1,0:T(8,128)(2,1)}, u32[]{:S(2)}) copy-start(bf16[2,224,1280]{2,1,0:T(8,128)(2,1)} %get-tuple-element.112) | copy-start | bytes 3440644
  612.3 5.5 copy-start.49
  612.3 6.3 %copy-start.44 = (f32[256,1280]{1,0:T(8,128)S(1)}, f32[256,1280]{1,0:T(8,128)}, u32[]{:S(2)}) copy-start(f32[256,1280]{1,0:T(8,128)} %get-tuple-element.167) | copy-start | bytes 3932164
  615.2 5.5 copy-start.47
  (30 other events, 83.7 us)

commit v5 on v4

--- a/solution.py
+++ b/solution.py
@@ -523,12 +523,12 @@
     )(e, *x_pair, wa, sa, *downs, sd)
 
 
-def dispatch_kernel(capacity, total, x_ref, m_ref, g0_ref, g1_ref, *refs):
+def dispatch_kernel(capacity, total, x_ref, m_ref, g0_ref, g1_ref, g_all, *refs):
     experts = refs[0:3]
     sg_ref, su_ref, sd_ref = refs[3:6]
     dx_ref, wb_ref, near_ref, far_ref, sgg_ref, sdg_ref = refs[6:12]
-    xr_ref, gr_ref, gu_ref, wa_ref, last_ref = refs[12:17]
-    xbuf, sbuf, tbuf, mbuf, nbuf, bbuf, sbbuf, tbbuf, wgu, wd = refs[17:27]
+    xr_ref, gr_ref, gu_ref, wa_ref, last_ref, down_far, down_last = refs[12:19]
+    xbuf, sbuf, tbuf, mbuf, nbuf, bbuf, sbbuf, tbbuf, wgu, wd, gbuf, gown, acts, wacts = refs[19:33]
     (
         rx_s,
         rx_r,
@@ -549,13 +549,13 @@
         w_sem,
         l_s,
         l_r,
-    ) = refs[27:]
+    ) = refs[33:]
     experts = experts + (last_ref,)
     k = pl.program_id(0)
     stages = xbuf.shape[0]
     tokens, width = x_ref.shape[0], sg_ref.shape[0]
     hidden = experts[0].shape[1] // 3
-    wide = wd.shape[1] // 4
+    inner = 4 * hidden
     c = capacity
     last = stages - 1
     e, h = lax.axis_index("ep"), lax.axis_index("hp")
@@ -563,6 +563,7 @@
     right, left = (lax.rem(e + 2, n), h), (lax.rem(e + n - 2, n), h)
     pair = (e + 1 - 2 * lax.rem(e, 2), h)
     core = (e, h + 1 - 2 * lax.rem(h, 2))
+    y_far = (e, lax.rem(h + 2, 4))
 
     def ring_x(i):
         return mesh_copy(xbuf.at[i, 0], xbuf.at[i + 1, 0], rx_s, rx_r, i, right)
@@ -592,15 +593,24 @@
         return mesh_copy(bbuf.at[i, 0], tbbuf.at[i], rb_s, rb_r, i, right)
 
     to_core = mesh_copy(experts[1], last_ref, l_s, l_r, 0, core)
+    down_over = mesh_copy(
+        experts[0].at[:, pl.ds(2 * hidden, hidden), :], down_far, l_s, l_r, 1, y_far
+    )
+    down_on = mesh_copy(down_far, down_last, l_s, l_r, 2, core)
+    last_g = mesh_copy(g_all.at[last], gbuf, l_s, l_r, 3, pair)
 
     def weight_copies(r):
         copies = []
         for x in range(2):
-            for i, (to, at) in enumerate(((wgu, 2 * r), (wgu, 2 * r + 1), (wd, r))):
+            for i, (to, at) in enumerate(((wgu, 0), (wgu, inner), (wd, 0))):
+                if i == 2 and r % 2 == 1:
+                    src = (down_far if r == 1 else down_last).at[x]
+                else:
+                    src = experts[r].at[x, pl.ds(i * hidden, hidden), :]
                 copies.append(
                     pltpu.make_async_copy(
-                        experts[r].at[x, pl.ds(i * hidden, hidden), :],
-                        to.at[x, pl.ds(at * wide, hidden), :],
+                        src,
+                        to.at[x, pl.ds(at + r * hidden, hidden), :],
                         w_sem.at[6 * r + 3 * x + i],
                     )
                 )
@@ -610,25 +620,18 @@
     def _():
         xbuf[0, 0] = x_ref[...]
         mbuf[0] = m_ref[...]
-        greet((right, left, pair, core))
+        greet((right, left, pair, core, y_far))
+        down_over.start()
         ring_m(0).start()
         swap_m(0).start()
         ring_x(0).start()
         swap_x(0).start()
         to_core.start()
-        rest = wide - hidden
-        for r in range(3):
+        for r in (0, 2):
             for copy in weight_copies(r):
                 copy.start()
-        for x in range(2):
-            for to, count in ((wgu, 8), (wd, 4)):
-                for at in range(count):
-                    to[x, at * wide + hidden : (at + 1) * wide, :] = jnp.zeros((rest, width), BF)
         sgg_ref[...] = jnp.zeros_like(sgg_ref)
         sdg_ref[...] = jnp.zeros_like(sdg_ref)
-        to_core.wait()
-        for copy in weight_copies(3):
-            copy.start()
 
     @pl.when(k < last)
     def _():
@@ -646,25 +649,44 @@
     def _():
         swap_x(k).wait_recv()
 
+    @pl.when(k == last - 2)
+    def _():
+        last_g.start()
+
     @pl.when(k == last - 1)
     def _():
         ring_last().start()
 
+    @pl.when(k < last)
+    def _():
+        gown[...] = g1_ref[0]
+
     @pl.when(k == last)
     def _():
         ring_last().wait_recv()
+        last_g.wait()
+        gown[...] = gbuf[...]
 
     swap_m(k).wait_recv()
 
     @pl.when(k == 0)
     def _():
+        down_over.wait_recv()
+        down_on.start()
+        for copy in weight_copies(1):
+            copy.start()
+        to_core.wait()
+        down_on.wait()
+        for copy in weight_copies(3):
+            copy.start()
+        down_over.wait_send()
         for r in range(4):
             for copy in weight_copies(r):
                 copy.wait()
 
-    gs = (g0_ref, g1_ref)
+    gs = (g0_ref.at[0], gown)
     x2 = jnp.concatenate([xbuf[k, j] for j in range(2)], axis=0)
-    g2 = jnp.concatenate([g[0] for g in gs], axis=0)
+    g2 = jnp.concatenate([g[...] for g in gs], axis=0)
     hg, hu = dot(x2, sg_ref[...]), dot(x2, su_ref[...])
     ab = dot(g2, sd_ref[...], (1, 1))
     s = jax.nn.sigmoid(hg)
@@ -674,50 +696,49 @@
     ui = (ab * silu).astype(BF)
     sgg_ref[...] += dot(x2, jnp.concatenate([gi, ui], axis=1), (0, 0))
     sdg_ref[...] += dot(act, g2, (0, 0))
+    acts[k] = act
     dx = dot(gi, sg_ref[...], (1, 1)) + dot(ui, su_ref[...], (1, 1))
     totals = [dx[:tokens], dx[tokens:]]
-    out = dot(act, sd_ref[...])
-    outs = [out[:tokens], out[tokens:]]
     backs = [0.0, 0.0]
-    metas = [mbuf[k], nbuf[k]]
-    line = lax.broadcasted_iota(jnp.int32, metas[0].shape, 0)
+    line = lax.broadcasted_iota(jnp.int32, m_ref.shape, 0)
     short = lax.broadcasted_iota(jnp.int32, (total, tokens), 0)
     place = lax.broadcasted_iota(jnp.int32, (c, tokens), 0).astype(F32)
+
+    def hits(i, j, x):
+        code = jnp.where(line == total + 2 * e + x, (mbuf, nbuf)[j][i], 0.0)
+        return jnp.sum(code, axis=0, keepdims=True) == place
+
     for x in range(2):
         col = 2 * e + x
         picks, weights, found = [], [], []
         for j in range(2):
-            code = jnp.sum(jnp.where(line == total + col, metas[j], 0.0), axis=0, keepdims=True)
-            weight = jnp.sum(jnp.where(line == col, metas[j], 0.0), axis=0, keepdims=True)
-            hit = code == place
+            weight = jnp.where(line == col, (mbuf, nbuf)[j][k], 0.0)
+            weight = jnp.sum(weight, axis=0, keepdims=True)
+            hit = hits(k, j, x)
             pick = jnp.where(hit, 1.0, 0.0).astype(BF)
             found.append(hit)
             picks.append(pick)
             weights.append(jnp.sum(jnp.where(hit, weight, 0.0), axis=1, keepdims=True))
             xr_ref[x, 0, j * c : (j + 1) * c, :] = dot(pick, xbuf[k, j]).astype(BF)
-            gr_ref[x, 0, j * c : (j + 1) * c, :] = dot(pick, gs[j][0]).astype(BF)
+            gr_ref[x, 0, j * c : (j + 1) * c, :] = dot(pick, gs[j][...]).astype(BF)
         w = jnp.concatenate(weights, axis=0)
         xr, gr = xr_ref[x, 0], gr_ref[x, 0]
-        wb = jnp.zeros((2 * c, 1), F32)
-        for r in range(4):
-            hgu = dot(xr, wgu[x, 2 * r * wide : 2 * (r + 1) * wide, :], (1, 1))
-            ab = dot(gr, wd[x, r * wide : (r + 1) * wide, :], (1, 1))
-            hg, hu = hgu[:, :wide], hgu[:, wide:]
-            s = jax.nn.sigmoid(hg)
-            silu = hg * s
-            act = silu * hu
-            wb = wb + jnp.sum(act * ab, axis=1, keepdims=True)
-            ab = ab * w
-            at = 2 * r * wide
-            gu_ref[x, 0, :, at : at + wide] = (ab * hu * (s * (1.0 + hg * (1.0 - s)))).astype(BF)
-            gu_ref[x, 0, :, at + wide : at + 2 * wide] = (ab * silu).astype(BF)
-            wa_ref[x, 0, :, r * wide : (r + 1) * wide] = (act * w).astype(BF)
+        hgu = dot(xr, wgu[x], (1, 1))
+        ab = dot(gr, wd[x], (1, 1))
+        hg, hu = hgu[:, :inner], hgu[:, inner:]
+        s = jax.nn.sigmoid(hg)
+        silu = hg * s
+        act = silu * hu
+        wb = jnp.sum(act * ab, axis=1, keepdims=True)
+        ab = ab * w
+        gu_ref[x, 0, :, :inner] = (ab * hu * (s * (1.0 + hg * (1.0 - s)))).astype(BF)
+        gu_ref[x, 0, :, inner:] = (ab * silu).astype(BF)
+        wa_ref[x, 0] = (act * w).astype(BF)
+        wacts[k, x] = wa_ref[x, 0]
         dxr = dot(gu_ref[x, 0], wgu[x]).astype(BF)
-        rows = dot(wa_ref[x, 0], wd[x]).astype(BF)
         for j in range(2):
             span = slice(j * c, (j + 1) * c)
             totals[j] = totals[j] + dot(picks[j], dxr[span], (0, 0))
-            outs[j] = outs[j] + dot(picks[j], rows[span], (0, 0))
             row = jnp.sum(jnp.where(found[j], wb[span], 0.0), axis=0, keepdims=True)
             backs[j] = backs[j] + jnp.where(short == col, row, 0.0)
 
@@ -733,7 +754,6 @@
     for j in range(2):
         xbuf[k, j] = totals[j].astype(BF)
         bbuf[k, j] = backs[j]
-        (near_ref, far_ref)[j][0] = outs[j].astype(BF)
 
     @pl.when(k >= 1)
     def _():
@@ -761,11 +781,26 @@
         def _(i=i):
             advance(i, i == 1)
 
+    def forward(i):
+        out = dot(acts[i], sd_ref[...])
+        outs = [out[:tokens], out[tokens:]]
+        for x in range(2):
+            rows = dot(wacts[i, x], wd[x]).astype(BF)
+            for j in range(2):
+                pick = jnp.where(hits(i, j, x), 1.0, 0.0).astype(BF)
+                outs[j] = outs[j] + dot(pick, rows[j * c : (j + 1) * c], (0, 0))
+        near_ref[i] = outs[0].astype(BF)
+        far_ref[i] = outs[1].astype(BF)
+
     @pl.when(k == last)
     def _():
         swap_b(0).start()
         swap_r(0).start()
+        for i in range(stages // 2 + 1):
+            forward(i)
         advance(last, last == 1)
+        for i in range(stages // 2 + 1, stages):
+            forward(i)
         swap_b(0).wait_recv()
         swap_r(0).wait_recv()
         ring_b(last).wait_recv()
@@ -784,11 +819,12 @@
 
 def dispatch(capacity, total, x, meta, g_near, g_far, experts, sg, su, sd):
     stages = g_near.shape[0]
+    most = stages - 1
     tokens, width = x.shape
     lines = meta.shape[0]
     shared = sg.shape[1]
     hidden = experts[0].shape[1] // 3
-    wide = -(-hidden // LANES) * LANES
+    inner = 4 * hidden
     c2 = 2 * capacity
     once = pl.Buffered(1)
     dma = pltpu.SemaphoreType.DMA
@@ -807,21 +843,24 @@
             fixed((tokens, width)),
             fixed(meta.shape),
             pl.BlockSpec((1, tokens, width), lambda k: (k, 0, 0)),
-            pl.BlockSpec((1, tokens, width), lambda k: (k, 0, 0)),
+            pl.BlockSpec((1, tokens, width), lambda k: (k - k // most, 0, 0)),
+            anywhere,
         ]
         + [anywhere] * 3
         + [fixed(sg.shape), fixed(su.shape), fixed(sd.shape)],
         out_specs=[
             fixed((tokens, width)),
             fixed((total, tokens)),
-            pl.BlockSpec((1, tokens, width), lambda k: (k, 0, 0), pipeline_mode=once),
-            pl.BlockSpec((1, tokens, width), lambda k: (k, 0, 0), pipeline_mode=once),
+            fixed((stages, tokens, width)),
+            fixed((stages, tokens, width)),
             fixed((width, 2 * shared)),
             fixed((shared, width)),
             per_stage((2, 1, c2, width)),
             per_stage((2, 1, c2, width)),
-            per_stage((2, 1, c2, 8 * wide)),
-            per_stage((2, 1, c2, 4 * wide)),
+            per_stage((2, 1, c2, 2 * inner)),
+            per_stage((2, 1, c2, inner)),
+            anywhere,
+            anywhere,
             anywhere,
         ],
         out_shape=[
@@ -833,9 +872,11 @@
             jax.ShapeDtypeStruct((shared, width), F32),
             jax.ShapeDtypeStruct((2, stages, c2, width), BF),
             jax.ShapeDtypeStruct((2, stages, c2, width), BF),
-            jax.ShapeDtypeStruct((2, stages, c2, 8 * wide), BF),
-            jax.ShapeDtypeStruct((2, stages, c2, 4 * wide), BF),
-            jax.ShapeDtypeStruct(experts[0].shape, BF),
+            jax.ShapeDtypeStruct((2, stages, c2, 2 * inner), BF),
+            jax.ShapeDtypeStruct((2, stages, c2, inner), BF),
+            jax.ShapeDtypeStruct(experts[1].shape, BF),
+            jax.ShapeDtypeStruct((2, hidden, width), BF),
+            jax.ShapeDtypeStruct((2, hidden, width), BF),
         ],
         scratch_shapes=[
             pltpu.VMEM((stages, 2, tokens, width), BF),
@@ -846,12 +887,16 @@
             pltpu.VMEM((stages, 2, total, tokens), F32),
             pltpu.VMEM((stages, total, tokens), F32),
             pltpu.VMEM((stages, total, tokens), F32),
-            pltpu.VMEM((2, 8 * wide, width), BF),
-            pltpu.VMEM((2, 4 * wide, width), BF),
+            pltpu.VMEM((2, 2 * inner, width), BF),
+            pltpu.VMEM((2, inner, width), BF),
+            pltpu.VMEM((tokens, width), BF),
+            pltpu.VMEM((tokens, width), BF),
+            pltpu.VMEM((stages, 2 * tokens, shared), BF),
+            pltpu.VMEM((stages, 2, c2, inner), BF),
         ]
         + [dma((stages,))] * 16
         + [dma((24,))]
-        + [dma((1,))] * 2,
+        + [dma((4,))] * 2,
         compiler_params=pltpu.CompilerParams(
             vmem_limit_bytes=63 * MIB, collective_id=0, has_side_effects=True
         ),
@@ -860,7 +905,89 @@
             bytes_accessed=80 * MIB,
             transcendentals=stages * c2 * 8 * hidden,
         ),
-    )(x, meta, g_near, g_far, *experts, sg, su, sd)[:10]
+    )(x, meta, g_near, g_far, g_near, *experts, sg, su, sd)[:10]
+
+
+def expert_grad_kernel(
+    xr_ref, gr_ref, gu_ref, wa_ref, near_ref, far_ref, keep, sendb, recvb, s_s, s_r
+):
+    s = pl.program_id(0)
+    steps = sendb.shape[0]
+    half = sendb.shape[1]
+    h = lax.axis_index("hp")
+    core = (lax.axis_index("ep"), h + 1 - 2 * lax.rem(h, 2))
+
+    def over_core(n):
+        return mesh_copy(sendb.at[n], recvb.at[n], s_s, s_r, n, core)
+
+    @pl.when(s == 0)
+    def _():
+        greet([core])
+
+    def give(v):
+        sendb[s] = v[half:].astype(BF)
+        over_core(s).start()
+        keep[lax.rem(s, 2)] = v[:half].astype(BF)
+
+    @pl.when((s < steps) & (lax.rem(s, 3) < 2))
+    def _():
+        give(dot(gu_ref[0], xr_ref[0], (0, 0)))
+
+    @pl.when((s < steps) & (lax.rem(s, 3) == 2))
+    def _():
+        give(dot(wa_ref[0], gr_ref[0], (0, 0)))
+
+    @pl.when(s > 0)
+    def _():
+        n = s - 1
+        over_core(n).wait_recv()
+        total = (keep[lax.rem(n, 2)].astype(F32) + recvb[n].astype(F32)).astype(BF)
+        near_ref[0, 0] = total[: half // 2]
+        far_ref[0, 0] = total[half // 2 :]
+
+    @pl.when(s == steps)
+    def _():
+        for n in range(steps):
+            over_core(n).wait_send()
+
+
+def expert_grads(xr, gr, gu, wa, hidden):
+    rows, width = xr.shape[1:]
+    inner, steps = 4 * hidden, 6
+    dma = pltpu.SemaphoreType.DMA
+
+    def now(s):
+        return s - s // steps
+
+    def before(s):
+        return s - 1 + (steps - s) // steps
+
+    rows_in = pl.BlockSpec((1, rows, width), lambda s: (now(s) // 3, 0, 0))
+    out = pl.BlockSpec((1, 1, hidden, width), lambda s: (before(s) // 3, before(s) % 3, 0, 0))
+    near, far = pl.pallas_call(
+        expert_grad_kernel,
+        grid=(steps + 1,),
+        in_specs=[
+            rows_in,
+            rows_in,
+            pl.BlockSpec(
+                (1, rows, inner), lambda s: (now(s) // 3, 0, now(s) % 3 - now(s) % 3 // 2)
+            ),
+            pl.BlockSpec((1, rows, inner), lambda s: (now(s) // 3, 0, 0)),
+        ],
+        out_specs=[out, out],
+        out_shape=[jax.ShapeDtypeStruct((2, 3, hidden, width), BF)] * 2,
+        scratch_shapes=[pltpu.VMEM((2, inner // 2, width), BF)]
+        + [pltpu.VMEM((steps, inner // 2, width), BF)] * 2
+        + [dma((steps,))] * 2,
+        compiler_params=pltpu.CompilerParams(
+            vmem_limit_bytes=60 * MIB, collective_id=4, has_side_effects=True
+        ),
+        cost_estimate=pl.CostEstimate(
+            flops=12 * rows * inner * width, bytes_accessed=40 * MIB, transcendentals=0
+        ),
+    )(xr, gr, gu, wa)
+    return (v.reshape(2, 3 * hidden, width) for v in (near, far))
 
 
 def mesh_copy(src, dst, s, r, i, where):
@@ -1599,8 +1726,9 @@
         far_tokens, experts_core, g_near, *blocks = front(
             stages, tokens, experts, cotangent, blocks, 4
         )
-        experts_far = swap_y(after(experts, blocks[0]))
-        g_far = swap_pair(g_near)
+        own = experts[:, : 2 * expert_down.shape[1]]
+        experts_far = swap_y(after(own, blocks[0]))
+        g_far = swap_pair(g_near[: stages - 1])
     else:
         far_tokens = swap_y(tokens)
         blocks = [absolute(jnp.stack(gather_hp(v)), h, 0) for v in blocks]
@@ -1656,19 +1784,8 @@
             capacity, total, second_in, meta, g_near, g_far, experts, sg, su, sd
         )
         weight_back = weight_back.T
-        wide = wa.shape[3] // 4
         xr, gr, gu, wa = (v.reshape(flat + (v.shape[-1],)) for v in (xr, gr, gu, wa))
-        gu = expert_grad(gu, xr).astype(BF)
-        wa = expert_grad(wa, gr).astype(BF)
-        dx_sum = after(dx_sum, gu, wa)
-
-        def piece(r):
-            starts = ((gu, 2 * r * wide), (gu, (2 * r + 1) * wide), (wa, r * wide))
-            return jnp.concatenate([v[:, a : a + hidden] for v, a in starts], axis=1)
-
-        piece_near = [piece(r) for r in (0, 1)]
-        piece_core = swap_core(jnp.stack([piece(r) for r in (2, 3)]))
-        piece_sum = (piece_near[1].astype(F32) + piece_core[1].astype(F32)).astype(BF)
+        piece_near, piece_sum = expert_grads(xr, gr, gu, wa, hidden)
     else:
         x_ext = jnp.concatenate(
             [
@@ -1746,8 +1863,6 @@
     counts_part = jnp.pad(jnp.sum(kept, axis=0), (0, width - total))
 
     mixed_back = dot(attn_back, o_w, (1, 1)).astype(BF)
-    if fused:
-        mixed_back = after(mixed_back, piece_sum)
     out_part = dot(mixed, attn_back, (0, 0))
     sgg = sgg.reshape(4, width // 4, 2 * LANES)
     sdg = sdg[: 4 * pad].reshape(4, pad, width)
@@ -1803,7 +1918,10 @@
             middle_back,
         )
         grads = [out[i].astype(F32) for i in range(4)]
-        expert_sum = sum(v.astype(F32) for v in (piece_near[0], piece_core[0], piece_far))
+        spans = [slice(i * hidden, (i + 1) * hidden) for i in range(3)]
+        gate_grad, up_grad, down_grad = (
+            piece_near[:, a].astype(F32) + piece_far[:, a].astype(F32) for a in spans
+        )
     else:
         query_raw, near_back, far_back = attend_back(
             h_arr, query, kv_a, kv_b, mixed_back, lse, cosine, sine
@@ -1834,10 +1952,8 @@
         )
         sdown_grad = sdg[:, :units].reshape(ep * units, width).astype(F32)
         layer = (middle + routed).astype(BF)
-    gate_grad, up_grad = (
-        jnp.swapaxes(expert_sum[:, i * hidden : (i + 1) * hidden], 1, 2) for i in (0, 1)
-    )
-    down_grad = expert_sum[:, 2 * hidden :]
+        gate_grad, up_grad, down_grad = jnp.split(expert_sum, 3, axis=1)
+    gate_grad, up_grad = jnp.swapaxes(gate_grad, 1, 2), jnp.swapaxes(up_grad, 1, 2)
 
     def own(v, n):
         return lax.dynamic_slice_in_dim(v, h * n, n, axis=0)

time: 629 us -> 626 us (level); the launches traced: 623 us -> 626 us
  Pallas kernels: 449 us -> 519 us
  waiting for transfers between devices: 62.2 us -> 31.7 us
  matrix products: 41.3 us -> 12.4 us
    pallas_call x1, Pallas kernels: 126 us -> 164 us  [dispatch(): pl.pallas_call(functools.partial(dispatch_kernel, capacity, total), grid=...]
    dot_general x2 -> x0, matrix products: 31.3 us -> none  [expert_grad(): return jnp.einsum('xna,xnb->xab', left, right, preferred_element_type=F32)]
    pallas_call x0 -> x1, Pallas kernels: none -> 30.3 us  [expert_grads(): pl.pallas_call(expert_grad_kernel, grid=(steps + 1,), in_specs=[rows_in,...]
    ppermute x1, waiting for transfers between devices: 45.2 us -> 24.1 us  [swap_pair(): return lax.ppermute(v, 'ep', [(i, i ^ 1) for i in range(n)])]
    slice x3 -> x1, local copies, waits for them, and re-layouts: 10.6 us -> 1.4 us  [per_device(): g_far = swap_pair(g_near[:stages - 1])]
    ppermute x1, waiting for transfers between devices: 15.6 us -> 7.6 us  [swap_y(): return lax.ppermute(v, 'hp', [(i, i ^ 2) for i in range(4)])]
    unnamed x122 -> x116, local copies, waits for them, and re-layouts: 17.8 us -> 18.3 us
  transfers between devices with their start and end apart: 4 -> 3, of which waited for: 3 -> 2; matrix products, arithmetic and copies ran while one was open for 3% -> 2% of each run, Pallas kernels for 2% -> 2%
where the time goes in v5:
time: 626 us
  Pallas kernels  519 us (83%)
  waiting for transfers between devices  31.7 us (5%)
  local copies, waits for them, and re-layouts  30.7 us (5%)
  other arithmetic  28.7 us (5%)
  matrix products  12.4 us (2%)
    pallas_call x1, Pallas kernels, dispatch(): pl.pallas_call(functools.partial(dispatch_kernel, capacity, total), grid=...  164 us
    pallas_call x1, Pallas kernels, tail(): pl.pallas_call(tail_kernel, in_specs=[vmem] * 10, out_specs=[vmem] * 3, o...  128 us
    pallas_call x1, Pallas kernels, attend_back_and_sums(): pl.pallas_call(back_kernel, grid=(H + 1,), in_specs=[head(rows), kv(0), k...  111 us
    pallas_call x1, Pallas kernels, front(): pl.pallas_call(functools.partial(front_kernel, large, count), in_specs=[a...  67 us
    pallas_call x1, Pallas kernels, expert_grads(): pl.pallas_call(expert_grad_kernel, grid=(steps + 1,), in_specs=[rows_in,...  30.3 us
    ppermute x1, waiting for transfers between devices, swap_pair(): return lax.ppermute(v, 'ep', [(i, i ^ 1) for i in range(n)])  24.1 us
    unnamed x116, local copies, waits for them, and re-layouts  18.3 us
  transfers between devices with their start and end apart: 3, of which 2 were waited for; matrix products, arithmetic and copies ran while one was open for 2% of the time, Pallas kernels for 2%

profile of v5, /device:TPU:0, one launch (start us, length us, event | category | flops | bytes accessed | tf_op | source)
XLA Modules:
  0.0 626.4 jit_solution(5187790179662395890)
XLA Ops:
  0.8 3.1 multiply_sine_fusion
  10.5 3.5 pad_maximum_fusion.refs_1_.refs_0_
  14.7 1.3 concatenate.29.refs_7_
  16.0 1.1 copy-done.21
  17.1 1.1 copy-done.22
  18.3 67.0 %shard_map.288 = (bf16[256,1280]{1,0:T(8,128)(2,1)S(1)}, bf16[2,672,1280]{2,1,0:T(8,128)(2,1)}, bf16[4,256,1280]{2,1,0:T(8,128)(2,1)S(1)}, bf16[4,320,1280]{2,1,...) custom-call(bf16[256,1280]{1,0:T(8,128)(2,1)S(1)} %copy-done.6, ...), custom_call_target="tpu_custom_call" | custom-call | bytes 125829120 | tf_op jit(solution)/shard_map/pallas_call | solution.py:1084
  85.3 1.7 copy-done.5
  86.9 1.7 copy-done.24
  90.3 8.0 %shard_map.289 = (bf16[512,1280]{1,0:T(8,128)(2,1)S(1)}, bf16[2,512,1280]{2,1,0:T(8,128)(2,1)S(1)}, bf16[256,1280]{1,0:T(8,128)(2,1)S(1)}) custom-call(bf16[256,1280]{1,0:T(8,128)(2,1)S(1)} %copy-done.6, bf16[256,1280]{1,0:T(8,128)(2,1)S(1)} %get-tuple-element.61.f_ref.ftok_ref, f32[1,1280]{1,0:T(1,128)S(1)} %reshape.316.gain_ref, ...), custom_call_target="tpu_custom_call" | custom-call | tf_op jit(solution)/shard_map/pallas_call | solution.py:195
  98.4 1.0 copy-done.17
  99.8 1.4 slice.71
  101.2 1.5 collective-permute-start.1
  102.9 1.5 pad_maximum_fusion.1
  105.0 2.3 pad_maximum_fusion.3.sin_ref
  109.5 1.6 fusion.spread_ref
  112.0 10.3 %shard_map.290 = (bf16[256,1280]{1,0:T(8,128)(2,1)S(1)}, f32[256,1280]{1,0:T(8,128)S(1)}) custom-call(s32[1]{0:T(128)} %bitcast.8.h_ref, bf16[256,1280]{1,0:T(8,128)(2,1)S(1)} %copy-done.13, bf16[2,512,1280]{2,1,0:T(8,128)(2,1)S(1)} %get-tuple-element.67.ka_ref.va_ref, bf16[2,512,1280]{2,1,0:T(8,128)(2,1)} %collective-permute-done.kb_ref.vb_ref, ...), custom_call_target="tpu_custom_call" | custom-call | tf_op jit(solution)/shard_map/pallas_call | solution.py:277
  122.3 24.1 %collective-permute-done.1.g1_ref = bf16[3,256,1280]{2,1,0:T(8,128)(2,1)} collective-permute-done((bf16[3,256,1280]{2,1,0:T(8,128)(2,1)}, bf16[3,256,1280]{2,1,0:T(8,128)(2,1)}, u32[]{:S(2)}, u32[]{:S(2)}) %collective-permute-start.1) | collective-permute-done | bytes 1966112 | tf_op jit(solution)/shard_map/ppermute | solution.py:35
  146.4 1.1 multiply_reduce_fusion.2
  149.2 7.6 %collective-permute-done.2.refs_1_ = bf16[2,448,1280]{2,1,0:T(8,128)(2,1)} collective-permute-done((bf16[2,448,1280]{2,1,0:T(8,128)(2,1)}, bf16[2,448,1280]{2,1,0:T(8,128)(2,1)}, u32[]{:S(2)}, u32[]{:S(2)}) %collective-permute-start.2) | collective-permute-done | bytes 2293792 | tf_op jit(solution)/shard_map/ppermute | solution.py:30
  156.8 164.1 %shard_map.291 = (f32[256,1280]{1,0:T(8,128)}, f32[16,256]{1,0:T(8,128)}, bf16[4,256,1280]{2,1,0:T(8,128)(2,1)}, bf16[4,256,1280]{2,1,0:T(8,128)(2,1)}, f32[1280...) custom-call(bf16[256,1280]{1,0:T(8,128)(2,1)} %copy-done.31, ...), custom_call_target="tpu_custom_call" | custom-call | flops 31708938240 | bytes 83886080 | tf_op jit(solution)/shard_map/pallas_call | solution.py:839
  322.5 1.3 fusion.30
  323.8 2.7 multiply_reduce_fusion
  327.0 1.5 copy-done.26
  328.6 1.9 convolution_convert_fusion.1.d_ref
  330.5 2.8 convolution_convert_fusion
  335.4 30.3 %shard_map.292 = (bf16[2,3,224,1280]{3,2,1,0:T(8,128)(2,1)}, bf16[2,3,224,1280]{3,2,1,0:T(8,128)(2,1)}) custom-call(bf16[2,1152,1280]{2,1,0:T(8,128)(2,1)} %bitcast.109, bf16[2,1152,1280]{2,1,0:T(8,128)(2,1)} %bitcast.110, bf16[2,1152,1792]{2,1,0:T(8,128)(2,1)} %bitcast.108, bf16[2,1152,896]{2,1,0:T(8,128)(2,1)} %bitcast.111), custom_call_target="tpu_custom_call" | custom-call | flops 15854469120 | bytes 41943040 | tf_op jit(solution)/shard_map/pallas_call | solution.py:967
  365.6 111.1 %shard_map.293 = (bf16[1280,1280]{1,0:T(8,128)(2,1)}, bf16[1280,1280]{1,0:T(8,128)(2,1)}, bf16[1280,1280]{1,0:T(8,128)(2,1)}, f32[256,1280]{1,0:T(8,128)}, bf16[...) custom-call(bf16[256,1280]{1,0:T(8,128)(2,1)} %copy-done.12, ...), custom_call_target="tpu_custom_call" | custom-call | flops 9227468800 | bytes 62914560 | tf_op jit(solution)/shard_map/pallas_call | solution.py:1396
  476.7 2.0 concatenate.35.sm_ref
  478.7 128.3 %shard_map.294 = (bf16[4,320,1280]{2,1,0:T(8,128)(2,1)}, f32[24,1280]{1,0:T(8,128)}, f32[256,1280]{1,0:T(8,128)}) custom-call(bf16[2,2,2,160,1280]{4,3,2,1,0:T(8,128)(2,1)} %bitcast.103, bf16[2,2,2,160,1280]{4,3,2,1,0:T(8,128)(2,1)} %bitcast.104, bf16[2,2,2,160,1280]{4,3,2,1,0:T(8,128)(2,1)} %bitcast.105, bf16[2,2,2,160,1280]{4,3,2,1,0:T(8,128)(2,1)} %bitcast.96, ...), custom_call_target="tpu_custom_call" | custom-call | bytes 314572800 | tf_op jit(solution)/shard_map/pallas_call | solution.py:1619
  608.9 5.3 bitcast_convert_fusion
  616.2 3.1 convert_add_fusion
  620.7 1.1 copy.50
  (161 shorter events, 28.7 us)
Async XLA Ops:
  0.6 4.7 copy-start
  0.7 5.6 copy-start.48
  0.7 6.5 %copy-start.52 = (bf16[320]{0:T(512)(128)(2,1)S(1)}, bf16[320]{0:T(512)(128)(2,1)}, u32[]{:S(2)}) copy-start(bf16[320]{0:T(512)(128)(2,1)} %param.18) | copy-start | bytes 1924
  0.8 7.3 %copy-start.53 = (bf16[320]{0:T(512)(128)(2,1)S(1)}, bf16[320]{0:T(512)(128)(2,1)}, u32[]{:S(2)}) copy-start(bf16[320]{0:T(512)(128)(2,1)} %param.23) | copy-start | bytes 1924
  0.8 8.0 %copy-start.50 = (bf16[320,16]{0,1:T(8,128)(2,1)S(1)}, bf16[320,16]{0,1:T(8,128)(2,1)}, u32[]{:S(2)}) copy-start(bf16[320,16]{0,1:T(8,128)(2,1)} %param.24) | copy-start | bytes 30724
  10.4 5.5 copy-start.6
  10.5 5.5 copy-start.9
  10.5 5.5 copy-start.19
  10.5 5.5 copy-start.20
  18.3 71.5 %copy-start.33 = (f32[1024,64]{1,0:T(8,128)S(1)}, f32[1024,64]{1,0:T(8,128)}, u32[]{:S(2)}) copy-start(f32[1024,64]{1,0:T(8,128)} %get-tuple-element.124) | copy-start | bytes 786436
  18.3 71.5 %copy-start.34 = (f32[1024,64]{1,0:T(8,128)S(1)}, f32[1024,64]{1,0:T(8,128)}, u32[]{:S(2)}) copy-start(f32[1024,64]{1,0:T(8,128)} %get-tuple-element.125) | copy-start | bytes 786436
  89.4 8.9 %copy-start.3 = (bf16[4,320,1280]{2,1,0:T(8,128)(2,1)}, bf16[4,320,1280]{2,1,0:T(8,128)(2,1)S(1)}, u32[]{:S(2)}) copy-start(bf16[4,320,1280]{2,1,0:T(8,128)(2,1)S(1)} %get-tuple-element.63) | copy-start | bytes 9830404
  89.4 8.9 %copy-start.4 = (bf16[4,320,1280]{2,1,0:T(8,128)(2,1)}, bf16[4,320,1280]{2,1,0:T(8,128)(2,1)S(1)}, u32[]{:S(2)}) copy-start(bf16[4,320,1280]{2,1,0:T(8,128)(2,1)S(1)} %get-tuple-element.64) | copy-start | bytes 9830404
  89.4 8.9 %copy-start.11 = (bf16[256,1280]{1,0:T(8,128)(2,1)}, bf16[256,1280]{1,0:T(8,128)(2,1)S(1)}, u32[]{:S(2)}) copy-start(bf16[256,1280]{1,0:T(8,128)(2,1)S(1)} %get-tuple-element.61.f_ref.ftok_ref) | copy-start | bytes 1966084
  89.4 10.4 %copy-start.16 = (bf16[4,256,1280]{2,1,0:T(8,128)(2,1)}, bf16[4,256,1280]{2,1,0:T(8,128)(2,1)S(1)}, u32[]{:S(2)}) copy-start(bf16[4,256,1280]{2,1,0:T(8,128)(2,1)S(1)} %get-tuple-element.69.g0_ref.g_all) | copy-start | bytes 7864324
  89.8 8.6 %copy-start.23 = (f32[1,1280]{1,0:T(1,128)}, f32[1,1280]{1,0:T(1,128)S(1)}, u32[]{:S(2)}) copy-start(f32[1,1280]{1,0:T(1,128)S(1)} %reshape.316.gain_ref) | copy-start | bytes 15364
  99.4 12.5 %copy-start.2 = (bf16[2,512,1280]{2,1,0:T(8,128)(2,1)}, bf16[2,512,1280]{2,1,0:T(8,128)(2,1)S(1)}, u32[]{:S(2)}) copy-start(bf16[2,512,1280]{2,1,0:T(8,128)(2,1)S(1)} %get-tuple-element.67.ka_ref.va_ref) | copy-start | bytes 7864324
  99.4 12.5 %collective-permute-start = (bf16[2,512,1280]{2,1,0:T(8,128)(2,1)S(1)}, bf16[2,512,1280]{2,1,0:T(8,128)(2,1)}, u32[]{:S(2)}, u32[]{:S(2)}) collective-permute-start(bf16[2,512,1280]{2,1,0:T(8,128)(2,1)S(1)} %get-tuple-element.67.ka_ref.va_ref), channel_id=1, source_target_pairs={{0,1},{1,0},{2,3},{3,2},{4,5},{5,4},{6,7},{7,6},{8,9},{9,8},{10,11... | collective-permute-start | bytes 7864328 | tf_op jit(solution)/shard_map/ppermute | solution.py:26
  99.8 3.1 copy-start.38
  101.2 3.8 copy-start.49
  101.2 3.8 copy-start.51
  101.2 45.2 %collective-permute-start.1 = (bf16[3,256,1280]{2,1,0:T(8,128)(2,1)}, bf16[3,256,1280]{2,1,0:T(8,128)(2,1)}, u32[]{:S(2)}, u32[]{:S(2)}) collective-permute-start(bf16[3,256,1280]{2,1,0:T(8,128)(2,1)} %slice.71), channel_id=1, source_target_pairs={{0,4},{4,0},{8,12},{12,8},{16,20},{20,16},{24,28},{28,24},{1,5},{5... | collective-permute-start | bytes 5898248 | tf_op jit(solution)/shard_map/ppermute | solution.py:35
  104.4 3.8 copy-start.54
  104.4 52.4 %collective-permute-start.2 = (bf16[2,448,1280]{2,1,0:T(8,128)(2,1)}, bf16[2,448,1280]{2,1,0:T(8,128)(2,1)}, u32[]{:S(2)}, u32[]{:S(2)}) collective-permute-start(bf16[2,448,1280]{2,1,0:T(8,128)(2,1)} %pad_maximum_fusion.1), channel_id=1, source_target_pairs={{0,2},{1,3},{2,0},{3,1},{4,6},{5,7},{6,4},{7,5},{8,10},{9,11},{10,... | collective-permute-start | bytes 6881288 | tf_op jit(solution)/shard_map/ppermute | solution.py:30
  107.2 3.8 copy-start.8
  112.0 34.4 %copy-start.25 = (bf16[4,320,1280]{2,1,0:T(8,128)(2,1)S(1)}, bf16[4,320,1280]{2,1,0:T(8,128)(2,1)}, u32[]{:S(2)}) copy-start(bf16[4,320,1280]{2,1,0:T(8,128)(2,1)} %copy-done.24) | copy-start | bytes 9830404
  122.3 25.2 %copy-start.14 = (bf16[256,1280]{1,0:T(8,128)(2,1)}, bf16[256,1280]{1,0:T(8,128)(2,1)S(1)}, u32[]{:S(2)}) copy-start(bf16[256,1280]{1,0:T(8,128)(2,1)S(1)} %get-tuple-element.70) | copy-start | bytes 1966084
  122.3 25.2 %copy-start.18 = (f32[256,1280]{1,0:T(8,128)}, f32[256,1280]{1,0:T(8,128)S(1)}, u32[]{:S(2)}) copy-start(f32[256,1280]{1,0:T(8,128)S(1)} %get-tuple-element.79.lse_ref) | copy-start | bytes 3932164
  147.7 9.1 %copy-start.31 = (bf16[256,1280]{1,0:T(8,128)(2,1)}, bf16[256,1280]{1,0:T(8,128)(2,1)S(1)}, u32[]{:S(2)}) copy-start(bf16[256,1280]{1,0:T(8,128)(2,1)S(1)} %multiply_convert_fusion.x_ref) | copy-start | bytes 1966084
  608.9 7.3 %copy-start.39 = (bf16[2,3,224,1280]{3,2,1,0:T(8,128)(2,1)S(1)}, bf16[2,3,224,1280]{3,2,1,0:T(8,128)(2,1)}, u32[]{:S(2)}) copy-start(bf16[2,3,224,1280]{3,2,1,0:T(8,128)(2,1)} %get-tuple-element.104) | copy-start | bytes 10321924
  608.9 7.3 %copy-start.40 = (bf16[2,672,1280]{2,1,0:T(8,128)(2,1)S(1)}, bf16[2,672,1280]{2,1,0:T(8,128)(2,1)}, u32[]{:S(2)}) copy-start(bf16[2,672,1280]{2,1,0:T(8,128)(2,1)} %get-tuple-element.105) | copy-start | bytes 10321924
  616.2 3.7 copy-start.46
  (26 other events, 47.2 us)

commit v6 on v5

--- a/solution.py
+++ b/solution.py
@@ -649,7 +649,7 @@
     def _():
         swap_x(k).wait_recv()
 
-    @pl.when(k == last - 2)
+    @pl.when(k == 0)
     def _():
         last_g.start()
 

time: 626 us -> 612 us (0.978)
  Pallas kernels: 519 us -> 505 us
    pallas_call x1, Pallas kernels: 164 us -> 150 us  [dispatch(): pl.pallas_call(functools.partial(dispatch_kernel, capacity, total), grid=...]
where the time goes in v6:
time: 612 us
  Pallas kernels  505 us (83%)
  waiting for transfers between devices  31.7 us (5%)
  local copies, waits for them, and re-layouts  30.7 us (5%)
  other arithmetic  28.7 us (5%)
  matrix products  12.4 us (2%)
    pallas_call x1, Pallas kernels, dispatch(): pl.pallas_call(functools.partial(dispatch_kernel, capacity, total), grid=...  150 us
    pallas_call x1, Pallas kernels, tail(): pl.pallas_call(tail_kernel, in_specs=[vmem] * 10, out_specs=[vmem] * 3, o...  128 us
    pallas_call x1, Pallas kernels, attend_back_and_sums(): pl.pallas_call(back_kernel, grid=(H + 1,), in_specs=[head(rows), kv(0), k...  111 us
    pallas_call x1, Pallas kernels, front(): pl.pallas_call(functools.partial(front_kernel, large, count), in_specs=[a...  67 us
    pallas_call x1, Pallas kernels, expert_grads(): pl.pallas_call(expert_grad_kernel, grid=(steps + 1,), in_specs=[rows_in,...  30.3 us
    ppermute x1, waiting for transfers between devices, swap_pair(): return lax.ppermute(v, 'ep', [(i, i ^ 1) for i in range(n)])  24.1 us
    unnamed x116, local copies, waits for them, and re-layouts  18.3 us
    dot_general x9, matrix products, dot(): lax.dot_general(left, right, (((over[0],), (over[1],)), ((), ())), prefer...  12.4 us
  transfers between devices with their start and end apart: 3, of which 2 were waited for; matrix products, arithmetic and copies ran while one was open for 2% of the time, Pallas kernels for 2%

profile of v6, /device:TPU:0, one launch (start us, length us, event | category | flops | bytes accessed | tf_op | source)
XLA Modules:
  0.0 612.3 jit_solution(14501571900491201634)
XLA Ops:
  0.8 3.1 multiply_sine_fusion
  10.5 3.5 pad_maximum_fusion.refs_1_.refs_0_
  14.7 1.3 concatenate.29.refs_7_
  16.0 1.1 copy-done.21
  17.1 1.1 copy-done.22
  18.3 67.0 %shard_map.288 = (bf16[256,1280]{1,0:T(8,128)(2,1)S(1)}, bf16[2,672,1280]{2,1,0:T(8,128)(2,1)}, bf16[4,256,1280]{2,1,0:T(8,128)(2,1)S(1)}, bf16[4,320,1280]{2,1,...) custom-call(bf16[256,1280]{1,0:T(8,128)(2,1)S(1)} %copy-done.6, ...), custom_call_target="tpu_custom_call" | custom-call | bytes 125829120 | tf_op jit(solution)/shard_map/pallas_call | solution.py:1084
  85.3 1.7 copy-done.5
  86.9 1.7 copy-done.24
  90.3 8.0 %shard_map.289 = (bf16[512,1280]{1,0:T(8,128)(2,1)S(1)}, bf16[2,512,1280]{2,1,0:T(8,128)(2,1)S(1)}, bf16[256,1280]{1,0:T(8,128)(2,1)S(1)}) custom-call(bf16[256,1280]{1,0:T(8,128)(2,1)S(1)} %copy-done.6, bf16[256,1280]{1,0:T(8,128)(2,1)S(1)} %get-tuple-element.61.f_ref.ftok_ref, f32[1,1280]{1,0:T(1,128)S(1)} %reshape.316.gain_ref, ...), custom_call_target="tpu_custom_call" | custom-call | tf_op jit(solution)/shard_map/pallas_call | solution.py:195
  98.4 1.0 copy-done.17
  99.8 1.4 slice.71
  101.2 1.5 collective-permute-start.1
  102.9 1.5 pad_maximum_fusion.1
  105.0 2.3 pad_maximum_fusion.3.sin_ref
  109.5 1.6 fusion.spread_ref
  112.0 10.3 %shard_map.290 = (bf16[256,1280]{1,0:T(8,128)(2,1)S(1)}, f32[256,1280]{1,0:T(8,128)S(1)}) custom-call(s32[1]{0:T(128)} %bitcast.8.h_ref, bf16[256,1280]{1,0:T(8,128)(2,1)S(1)} %copy-done.13, bf16[2,512,1280]{2,1,0:T(8,128)(2,1)S(1)} %get-tuple-element.67.ka_ref.va_ref, bf16[2,512,1280]{2,1,0:T(8,128)(2,1)} %collective-permute-done.kb_ref.vb_ref, ...), custom_call_target="tpu_custom_call" | custom-call | tf_op jit(solution)/shard_map/pallas_call | solution.py:277
  122.3 24.1 %collective-permute-done.1.g1_ref = bf16[3,256,1280]{2,1,0:T(8,128)(2,1)} collective-permute-done((bf16[3,256,1280]{2,1,0:T(8,128)(2,1)}, bf16[3,256,1280]{2,1,0:T(8,128)(2,1)}, u32[]{:S(2)}, u32[]{:S(2)}) %collective-permute-start.1) | collective-permute-done | bytes 1966112 | tf_op jit(solution)/shard_map/ppermute | solution.py:35
  146.4 1.1 multiply_reduce_fusion.2
  149.2 7.6 %collective-permute-done.2.refs_1_ = bf16[2,448,1280]{2,1,0:T(8,128)(2,1)} collective-permute-done((bf16[2,448,1280]{2,1,0:T(8,128)(2,1)}, bf16[2,448,1280]{2,1,0:T(8,128)(2,1)}, u32[]{:S(2)}, u32[]{:S(2)}) %collective-permute-start.2) | collective-permute-done | bytes 2293792 | tf_op jit(solution)/shard_map/ppermute | solution.py:30
  156.8 150.0 %shard_map.291 = (f32[256,1280]{1,0:T(8,128)}, f32[16,256]{1,0:T(8,128)}, bf16[4,256,1280]{2,1,0:T(8,128)(2,1)}, bf16[4,256,1280]{2,1,0:T(8,128)(2,1)}, f32[1280...) custom-call(bf16[256,1280]{1,0:T(8,128)(2,1)} %copy-done.31, ...), custom_call_target="tpu_custom_call" | custom-call | flops 31708938240 | bytes 83886080 | tf_op jit(solution)/shard_map/pallas_call | solution.py:839
  308.5 1.3 fusion.30
  309.8 2.7 multiply_reduce_fusion
  313.0 1.5 copy-done.26
  314.5 1.9 convolution_convert_fusion.1.d_ref
  316.4 2.8 convolution_convert_fusion
  321.3 30.3 %shard_map.292 = (bf16[2,3,224,1280]{3,2,1,0:T(8,128)(2,1)}, bf16[2,3,224,1280]{3,2,1,0:T(8,128)(2,1)}) custom-call(bf16[2,1152,1280]{2,1,0:T(8,128)(2,1)} %bitcast.109, bf16[2,1152,1280]{2,1,0:T(8,128)(2,1)} %bitcast.110, bf16[2,1152,1792]{2,1,0:T(8,128)(2,1)} %bitcast.108, bf16[2,1152,896]{2,1,0:T(8,128)(2,1)} %bitcast.111), custom_call_target="tpu_custom_call" | custom-call | flops 15854469120 | bytes 41943040 | tf_op jit(solution)/shard_map/pallas_call | solution.py:967
  351.6 111.1 %shard_map.293 = (bf16[1280,1280]{1,0:T(8,128)(2,1)}, bf16[1280,1280]{1,0:T(8,128)(2,1)}, bf16[1280,1280]{1,0:T(8,128)(2,1)}, f32[256,1280]{1,0:T(8,128)}, bf16[...) custom-call(bf16[256,1280]{1,0:T(8,128)(2,1)} %copy-done.12, ...), custom_call_target="tpu_custom_call" | custom-call | flops 9227468800 | bytes 62914560 | tf_op jit(solution)/shard_map/pallas_call | solution.py:1396
  462.7 2.0 concatenate.35.sm_ref
  464.7 128.3 %shard_map.294 = (bf16[4,320,1280]{2,1,0:T(8,128)(2,1)}, f32[24,1280]{1,0:T(8,128)}, f32[256,1280]{1,0:T(8,128)}) custom-call(bf16[2,2,2,160,1280]{4,3,2,1,0:T(8,128)(2,1)} %bitcast.103, bf16[2,2,2,160,1280]{4,3,2,1,0:T(8,128)(2,1)} %bitcast.104, bf16[2,2,2,160,1280]{4,3,2,1,0:T(8,128)(2,1)} %bitcast.105, bf16[2,2,2,160,1280]{4,3,2,1,0:T(8,128)(2,1)} %bitcast.96, ...), custom_call_target="tpu_custom_call" | custom-call | bytes 314572800 | tf_op jit(solution)/shard_map/pallas_call | solution.py:1619
  594.8 5.3 bitcast_convert_fusion
  602.1 3.1 convert_add_fusion
  606.7 1.1 copy.50
  (161 shorter events, 28.7 us)
Async XLA Ops:
  0.6 4.7 copy-start
  0.7 5.6 copy-start.48
  0.7 6.5 %copy-start.52 = (bf16[320]{0:T(512)(128)(2,1)S(1)}, bf16[320]{0:T(512)(128)(2,1)}, u32[]{:S(2)}) copy-start(bf16[320]{0:T(512)(128)(2,1)} %param.18) | copy-start | bytes 1924
  0.8 7.3 %copy-start.53 = (bf16[320]{0:T(512)(128)(2,1)S(1)}, bf16[320]{0:T(512)(128)(2,1)}, u32[]{:S(2)}) copy-start(bf16[320]{0:T(512)(128)(2,1)} %param.23) | copy-start | bytes 1924
  0.8 8.0 %copy-start.50 = (bf16[320,16]{0,1:T(8,128)(2,1)S(1)}, bf16[320,16]{0,1:T(8,128)(2,1)}, u32[]{:S(2)}) copy-start(bf16[320,16]{0,1:T(8,128)(2,1)} %param.24) | copy-start | bytes 30724
  10.4 5.5 copy-start.6
  10.5 5.5 copy-start.9
  10.5 5.5 copy-start.19
  10.5 5.5 copy-start.20
  18.3 71.5 %copy-start.33 = (f32[1024,64]{1,0:T(8,128)S(1)}, f32[1024,64]{1,0:T(8,128)}, u32[]{:S(2)}) copy-start(f32[1024,64]{1,0:T(8,128)} %get-tuple-element.124) | copy-start | bytes 786436
  18.3 71.5 %copy-start.34 = (f32[1024,64]{1,0:T(8,128)S(1)}, f32[1024,64]{1,0:T(8,128)}, u32[]{:S(2)}) copy-start(f32[1024,64]{1,0:T(8,128)} %get-tuple-element.125) | copy-start | bytes 786436
  89.4 8.9 %copy-start.3 = (bf16[4,320,1280]{2,1,0:T(8,128)(2,1)}, bf16[4,320,1280]{2,1,0:T(8,128)(2,1)S(1)}, u32[]{:S(2)}) copy-start(bf16[4,320,1280]{2,1,0:T(8,128)(2,1)S(1)} %get-tuple-element.63) | copy-start | bytes 9830404
  89.4 8.9 %copy-start.4 = (bf16[4,320,1280]{2,1,0:T(8,128)(2,1)}, bf16[4,320,1280]{2,1,0:T(8,128)(2,1)S(1)}, u32[]{:S(2)}) copy-start(bf16[4,320,1280]{2,1,0:T(8,128)(2,1)S(1)} %get-tuple-element.64) | copy-start | bytes 9830404
  89.4 8.9 %copy-start.11 = (bf16[256,1280]{1,0:T(8,128)(2,1)}, bf16[256,1280]{1,0:T(8,128)(2,1)S(1)}, u32[]{:S(2)}) copy-start(bf16[256,1280]{1,0:T(8,128)(2,1)S(1)} %get-tuple-element.61.f_ref.ftok_ref) | copy-start | bytes 1966084
  89.4 10.4 %copy-start.16 = (bf16[4,256,1280]{2,1,0:T(8,128)(2,1)}, bf16[4,256,1280]{2,1,0:T(8,128)(2,1)S(1)}, u32[]{:S(2)}) copy-start(bf16[4,256,1280]{2,1,0:T(8,128)(2,1)S(1)} %get-tuple-element.69.g0_ref.g_all) | copy-start | bytes 7864324
  89.8 8.6 %copy-start.23 = (f32[1,1280]{1,0:T(1,128)}, f32[1,1280]{1,0:T(1,128)S(1)}, u32[]{:S(2)}) copy-start(f32[1,1280]{1,0:T(1,128)S(1)} %reshape.316.gain_ref) | copy-start | bytes 15364
  99.4 12.5 %copy-start.2 = (bf16[2,512,1280]{2,1,0:T(8,128)(2,1)}, bf16[2,512,1280]{2,1,0:T(8,128)(2,1)S(1)}, u32[]{:S(2)}) copy-start(bf16[2,512,1280]{2,1,0:T(8,128)(2,1)S(1)} %get-tuple-element.67.ka_ref.va_ref) | copy-start | bytes 7864324
  99.4 12.5 %collective-permute-start = (bf16[2,512,1280]{2,1,0:T(8,128)(2,1)S(1)}, bf16[2,512,1280]{2,1,0:T(8,128)(2,1)}, u32[]{:S(2)}, u32[]{:S(2)}) collective-permute-start(bf16[2,512,1280]{2,1,0:T(8,128)(2,1)S(1)} %get-tuple-element.67.ka_ref.va_ref), channel_id=1, source_target_pairs={{0,1},{1,0},{2,3},{3,2},{4,5},{5,4},{6,7},{7,6},{8,9},{9,8},{10,11... | collective-permute-start | bytes 7864328 | tf_op jit(solution)/shard_map/ppermute | solution.py:26
  99.8 3.1 copy-start.38
  101.2 3.8 copy-start.49
  101.2 3.8 copy-start.51
  101.2 45.2 %collective-permute-start.1 = (bf16[3,256,1280]{2,1,0:T(8,128)(2,1)}, bf16[3,256,1280]{2,1,0:T(8,128)(2,1)}, u32[]{:S(2)}, u32[]{:S(2)}) collective-permute-start(bf16[3,256,1280]{2,1,0:T(8,128)(2,1)} %slice.71), channel_id=1, source_target_pairs={{0,4},{4,0},{8,12},{12,8},{16,20},{20,16},{24,28},{28,24},{1,5},{5... | collective-permute-start | bytes 5898248 | tf_op jit(solution)/shard_map/ppermute | solution.py:35
  104.4 3.8 copy-start.54
  104.4 52.4 %collective-permute-start.2 = (bf16[2,448,1280]{2,1,0:T(8,128)(2,1)}, bf16[2,448,1280]{2,1,0:T(8,128)(2,1)}, u32[]{:S(2)}, u32[]{:S(2)}) collective-permute-start(bf16[2,448,1280]{2,1,0:T(8,128)(2,1)} %pad_maximum_fusion.1), channel_id=1, source_target_pairs={{0,2},{1,3},{2,0},{3,1},{4,6},{5,7},{6,4},{7,5},{8,10},{9,11},{10,... | collective-permute-start | bytes 6881288 | tf_op jit(solution)/shard_map/ppermute | solution.py:30
  107.2 3.8 copy-start.8
  112.0 34.4 %copy-start.25 = (bf16[4,320,1280]{2,1,0:T(8,128)(2,1)S(1)}, bf16[4,320,1280]{2,1,0:T(8,128)(2,1)}, u32[]{:S(2)}) copy-start(bf16[4,320,1280]{2,1,0:T(8,128)(2,1)} %copy-done.24) | copy-start | bytes 9830404
  122.3 25.2 %copy-start.14 = (bf16[256,1280]{1,0:T(8,128)(2,1)}, bf16[256,1280]{1,0:T(8,128)(2,1)S(1)}, u32[]{:S(2)}) copy-start(bf16[256,1280]{1,0:T(8,128)(2,1)S(1)} %get-tuple-element.70) | copy-start | bytes 1966084
  122.3 25.2 %copy-start.18 = (f32[256,1280]{1,0:T(8,128)}, f32[256,1280]{1,0:T(8,128)S(1)}, u32[]{:S(2)}) copy-start(f32[256,1280]{1,0:T(8,128)S(1)} %get-tuple-element.79.lse_ref) | copy-start | bytes 3932164
  147.7 9.1 %copy-start.31 = (bf16[256,1280]{1,0:T(8,128)(2,1)}, bf16[256,1280]{1,0:T(8,128)(2,1)S(1)}, u32[]{:S(2)}) copy-start(bf16[256,1280]{1,0:T(8,128)(2,1)S(1)} %multiply_convert_fusion.x_ref) | copy-start | bytes 1966084
  594.8 7.3 %copy-start.39 = (bf16[2,3,224,1280]{3,2,1,0:T(8,128)(2,1)S(1)}, bf16[2,3,224,1280]{3,2,1,0:T(8,128)(2,1)}, u32[]{:S(2)}) copy-start(bf16[2,3,224,1280]{3,2,1,0:T(8,128)(2,1)} %get-tuple-element.104) | copy-start | bytes 10321924
  594.8 7.3 %copy-start.40 = (bf16[2,672,1280]{2,1,0:T(8,128)(2,1)S(1)}, bf16[2,672,1280]{2,1,0:T(8,128)(2,1)}, u32[]{:S(2)}) copy-start(bf16[2,672,1280]{2,1,0:T(8,128)(2,1)} %get-tuple-element.105) | copy-start | bytes 10321924
  602.1 3.7 copy-start.46
  (26 other events, 47.2 us)
